TPU v7x, 128 devices: a whole 4x4x4 slice. The times are simulated.
128 devices in a mesh: dp: 32 (over z_hi, x, y), fsdp: 4 (over z_lo, core).
Axes of the slice: x: 4, y: 4, z: 4 (z_hi: 2, z_lo: 2; z = z_hi * 2 + z_lo), core: 2. Of those that a mesh axis runs over, the one named last changes fastest.
Arguments:
- tokens: bfloat16 [32768, 1024], P(('dp', 'fsdp')), may hold values from -6 to 6
- attn_norm_gain: bfloat16 [1024], P('fsdp'), may hold values from 0.5 to 1.5
- attn_norm_shift: bfloat16 [1024], P('fsdp'), may hold values from -4 to 4
- qkv_weight: bfloat16 [1024, 3072], P('fsdp'), may hold values from -0.1875 to 0.1875
- qkv_bias: bfloat16 [3072], P('fsdp'), may hold values from -6 to 6
- out_weight: bfloat16 [1024, 1024], P('fsdp'), may hold values from -0.5 to 0.5
- mlp_norm_gain: bfloat16 [1024], P('fsdp'), may hold values from 0.5 to 1.5
- mlp_norm_shift: bfloat16 [1024], P('fsdp'), may hold values from -4 to 4
- gate_up_weight: bfloat16 [1024, 5632], P('fsdp'), may hold values from -0.1875 to 0.1875
- down_weight: bfloat16 [2816, 1024], P('fsdp'), may hold values from -0.109375 to 0.109375
- cotangent: bfloat16 [32768, 1024], P(('dp', 'fsdp')), may hold values from -6 to 6
Outputs:
- layer_out: bfloat16 [32768, 1024], P(('dp', 'fsdp'))
- tokens_grad: float32 [32768, 1024], P(('dp', 'fsdp'))
- grad_attn_norm_gain: float32 [1024], P('fsdp')
- grad_attn_norm_shift: float32 [1024], P('fsdp')
- grad_qkv_weight: float32 [1024, 3072], P('fsdp')
- grad_qkv_bias: float32 [3072], P('fsdp')
- grad_out_weight: float32 [1024, 1024], P('fsdp')
- grad_mlp_norm_gain: float32 [1024], P('fsdp')
- grad_mlp_norm_shift: float32 [1024], P('fsdp')
- grad_gate_up_weight: float32 [1024, 5632], P('fsdp')
- grad_down_weight: float32 [2816, 1024], P('fsdp')
All inputs are finite; a program needn't handle non-finite values.
Results may differ from a plain program's by a relative error of at most 0.028.
Values may be sent and summed in bfloat16 or wider, within the bound.
No kernel may reach another device: no remote copies, remote signals or barrier semaphores. Data moves between devices by JAX's collectives and lax.ppermute only.
A program may use at most 192 MiB of HBM per device.

v0:
```python
import math

import jax
import jax.numpy as jnp
from jax import lax
from jax.sharding import PartitionSpec as P

D = 1024
HEADS = 16
HEAD = 64
ROTARY = 16
FF = 2816


epsilon = 1e-05
masked = -1e30


def apply_layer_normalization(operand, norm_gain, norm_shift):
    centred = operand - jnp.mean(operand, axis=1, keepdims=True)
    inverse = lax.rsqrt(jnp.mean(centred * centred, axis=1, keepdims=True) + epsilon)
    normed = centred * inverse
    return (normed * norm_gain + norm_shift, normed, inverse)


def norm_back(incoming, normed, inverse, norm_gain):
    scaled = incoming * norm_gain
    centred_grad = (
        scaled
        - jnp.mean(scaled, axis=1, keepdims=True)
        - normed * jnp.mean(scaled * normed, axis=1, keepdims=True)
    )
    return (inverse * centred_grad, jnp.sum(incoming * normed, axis=0), jnp.sum(incoming, axis=0))


def rotary_tables(places):
    indices = jnp.arange(ROTARY // 2, dtype=jnp.float32)
    frequency = jnp.exp(indices * (-math.log(10000.0) / (ROTARY // 2)))
    angles = places[:, None] * frequency[None, :]
    return (jnp.cos(angles)[:, None, :], jnp.sin(angles)[:, None, :])


def rotate(operand, cosine, sine_table):
    half_dims = ROTARY // 2
    leading = operand[:, :, :half_dims]
    trailing = operand[:, :, half_dims:ROTARY]
    return jnp.concatenate(
        [
            leading * cosine - trailing * sine_table,
            trailing * cosine + leading * sine_table,
            operand[:, :, ROTARY:],
        ],
        axis=2,
    )


def contract_rows(former, latter):
    return lax.dot_general(
        former, latter, (((0,), (0,)), ((), ())), preferred_element_type=jnp.float32
    )


def contract_cols(former, latter):
    return lax.dot_general(
        former, latter, (((1,), (1,)), ((), ())), preferred_element_type=jnp.float32
    )


def attention_scores(queries, keyset, places):
    length = keyset.shape[0]
    scores = jnp.einsum(
        "qhd,khd->hqk", queries, keyset, preferred_element_type=jnp.float32
    ) * HEAD ** (-0.5)
    allowed = jnp.arange(length)[None, :] <= places[:, None]
    return jnp.where(allowed[None], scores, masked)


def body(
    tokens,
    attn_norm_gain,
    attn_norm_shift,
    qkv_weight,
    qkv_bias,
    out_weight,
    mlp_norm_gain,
    mlp_norm_shift,
    gate_up_weight,
    down_weight,
    cotangent,
):
    gathered = (
        lax.all_gather(qkv_weight, "fsdp", axis=0, tiled=True),
        lax.all_gather(out_weight, "fsdp", axis=0, tiled=True),
        lax.all_gather(gate_up_weight, "fsdp", axis=0, tiled=True),
        lax.all_gather(down_weight, "fsdp", axis=0, tiled=True),
        lax.all_gather(attn_norm_gain, "fsdp", axis=0, tiled=True),
        lax.all_gather(attn_norm_shift, "fsdp", axis=0, tiled=True),
        lax.all_gather(qkv_bias, "fsdp", axis=0, tiled=True),
        lax.all_gather(mlp_norm_gain, "fsdp", axis=0, tiled=True),
        lax.all_gather(mlp_norm_shift, "fsdp", axis=0, tiled=True),
    )
    (
        qkv_full,
        out_full,
        gate_up_full,
        down_full,
        attention_norm_scale,
        shift_attn,
        bias_full,
        feedforward_norm_scale,
        feedforward_norm_bias,
    ) = gathered
    attention_norm_scale = attention_norm_scale.astype(jnp.float32)
    feedforward_norm_scale = feedforward_norm_scale.astype(jnp.float32)
    tok_rows = tokens.shape[0]
    places = lax.axis_index("fsdp") * tok_rows + jnp.arange(tok_rows)
    cosine, sine_table = rotary_tables(places.astype(jnp.float32))
    inputs = tokens.astype(jnp.float32)
    attention_normalized_input, attention_standardized, attention_inverse_deviation = (
        apply_layer_normalization(inputs, attention_norm_scale, shift_attn.astype(jnp.float32))
    )
    hidden_attn = attention_normalized_input.astype(jnp.bfloat16)
    projected = jnp.dot(
        hidden_attn, qkv_full, preferred_element_type=jnp.float32
    ) + bias_full.astype(jnp.float32)
    queries = rotate(projected[:, :D].reshape(tok_rows, HEADS, HEAD), cosine, sine_table).astype(
        jnp.bfloat16
    )
    keys_local = (
        rotate(projected[:, D : 2 * D].reshape(tok_rows, HEADS, HEAD), cosine, sine_table)
        .astype(jnp.bfloat16)
        .reshape(tok_rows, D)
    )
    values_local = projected[:, 2 * D :].astype(jnp.bfloat16)
    keys_all, values_all = (
        lax.all_gather(keys_local, "fsdp", axis=0, tiled=True),
        lax.all_gather(values_local, "fsdp", axis=0, tiled=True),
    )
    length = keys_all.shape[0]
    keyset = keys_all.reshape(length, HEADS, HEAD)
    valueset = values_all.reshape(length, HEADS, HEAD)
    scores = attention_scores(queries, keyset, places)
    largest = jnp.max(scores, axis=2, keepdims=True)
    exp_scores = jnp.exp(scores - largest)
    totals = jnp.sum(exp_scores, axis=2, keepdims=True)
    probs_low = (exp_scores / totals).astype(jnp.bfloat16)
    logsum = largest + jnp.log(totals)
    attn_mixed = (
        jnp.einsum("hqk,khd->qhd", probs_low, valueset, preferred_element_type=jnp.float32)
        .reshape(tok_rows, D)
        .astype(jnp.bfloat16)
    )
    residual_between = inputs + jnp.dot(attn_mixed, out_full, preferred_element_type=jnp.float32)
    feedforward_normalized_input, feedforward_standardized, feedforward_inverse_deviation = (
        apply_layer_normalization(
            residual_between, feedforward_norm_scale, feedforward_norm_bias.astype(jnp.float32)
        )
    )
    hidden_mlp = feedforward_normalized_input.astype(jnp.bfloat16)
    gate_up = jnp.dot(hidden_mlp, gate_up_full, preferred_element_type=jnp.float32)
    gate_part = gate_up[:, :FF]
    upward = gate_up[:, FF:]
    sigmoid = jax.nn.sigmoid(gate_part)
    activation = (gate_part * sigmoid * upward).astype(jnp.bfloat16)
    layer_out = (
        residual_between + jnp.dot(activation, down_full, preferred_element_type=jnp.float32)
    ).astype(jnp.bfloat16)
    qkv_back, out_back, gate_up_back, down_back = (
        lax.all_gather(qkv_weight, "fsdp", axis=0, tiled=True),
        lax.all_gather(out_weight, "fsdp", axis=0, tiled=True),
        lax.all_gather(gate_up_weight, "fsdp", axis=0, tiled=True),
        lax.all_gather(down_weight, "fsdp", axis=0, tiled=True),
    )
    keys_again, values_again = (
        lax.all_gather(keys_local, "fsdp", axis=0, tiled=True),
        lax.all_gather(values_local, "fsdp", axis=0, tiled=True),
    )
    keyset = keys_again.reshape(length, HEADS, HEAD)
    valueset = values_again.reshape(length, HEADS, HEAD)
    grad_out = cotangent.astype(jnp.float32)
    grad_activation = contract_cols(cotangent, down_back)
    grad_down = contract_rows(activation, cotangent)
    grad_gate = grad_activation * upward * (sigmoid * (1.0 + gate_part * (1.0 - sigmoid)))
    grad_upward = grad_activation * (gate_part * sigmoid)
    grad_gate_up = jnp.concatenate([grad_gate, grad_upward], axis=1).astype(jnp.bfloat16)
    grad_gate_up_w = contract_rows(hidden_mlp, grad_gate_up)
    feedforward_hidden_gradient = contract_cols(grad_gate_up, gate_up_back)
    grad_norm_mlp, grad_gain_mlp, grad_shift_mlp = norm_back(
        feedforward_hidden_gradient,
        feedforward_standardized,
        feedforward_inverse_deviation,
        feedforward_norm_scale,
    )
    grad_middle = grad_out + grad_norm_mlp
    grad_branch = grad_middle.astype(jnp.bfloat16)
    grad_out_w = contract_rows(attn_mixed, grad_branch)
    grad_mixed = (
        contract_cols(grad_branch, out_back).astype(jnp.bfloat16).reshape(tok_rows, HEADS, HEAD)
    )
    scores = attention_scores(queries, keyset, places)
    attn_probs = jnp.exp(scores - logsum)
    grad_probs = jnp.einsum(
        "qhd,khd->hqk", grad_mixed, valueset, preferred_element_type=jnp.float32
    )
    row_delta = jnp.sum(attn_probs * grad_probs, axis=2, keepdims=True)
    grad_scores = (attn_probs * (grad_probs - row_delta)).astype(jnp.bfloat16)
    score_scale = HEAD ** (-0.5)
    grad_queries = (
        jnp.einsum("hqk,khd->qhd", grad_scores, keyset, preferred_element_type=jnp.float32)
        * score_scale
    )
    grad_keys = (
        jnp.einsum("hqk,qhd->khd", grad_scores, queries, preferred_element_type=jnp.float32)
        * score_scale
    ).reshape(length, D)
    grad_values = jnp.einsum(
        "hqk,qhd->khd",
        attn_probs.astype(jnp.bfloat16),
        grad_mixed,
        preferred_element_type=jnp.float32,
    ).reshape(length, D)
    grad_keys, grad_values = (
        lax.psum_scatter(
            grad_keys.astype(jnp.bfloat16), "fsdp", scatter_dimension=0, tiled=True
        ).astype(jnp.float32),
        lax.psum_scatter(
            grad_values.astype(jnp.bfloat16), "fsdp", scatter_dimension=0, tiled=True
        ).astype(jnp.float32),
    )
    grad_projected = jnp.concatenate(
        [
            rotate(grad_queries, cosine, -sine_table).reshape(tok_rows, D),
            rotate(grad_keys.reshape(tok_rows, HEADS, HEAD), cosine, -sine_table).reshape(
                tok_rows, D
            ),
            grad_values,
        ],
        axis=1,
    ).astype(jnp.bfloat16)
    grad_qkv_w = contract_rows(hidden_attn, grad_projected)
    grad_bias = jnp.sum(grad_projected, axis=0, dtype=jnp.float32)
    attention_hidden_gradient = contract_cols(grad_projected, qkv_back)
    grad_norm_attn, grad_gain_attn, grad_shift_attn = norm_back(
        attention_hidden_gradient,
        attention_standardized,
        attention_inverse_deviation,
        attention_norm_scale,
    )
    tokens_grad = grad_middle + grad_norm_attn
    grad_terms = (
        grad_qkv_w,
        grad_out_w,
        grad_gate_up_w,
        grad_down,
        grad_gain_attn,
        grad_shift_attn,
        grad_bias,
        grad_gain_mlp,
        grad_shift_mlp,
    )
    owned_grads = (
        lax.psum_scatter(
            grad_terms[0].astype(jnp.bfloat16), "fsdp", scatter_dimension=0, tiled=True
        ).astype(jnp.float32),
        lax.psum_scatter(
            grad_terms[1].astype(jnp.bfloat16), "fsdp", scatter_dimension=0, tiled=True
        ).astype(jnp.float32),
        lax.psum_scatter(
            grad_terms[2].astype(jnp.bfloat16), "fsdp", scatter_dimension=0, tiled=True
        ).astype(jnp.float32),
        lax.psum_scatter(
            grad_terms[3].astype(jnp.bfloat16), "fsdp", scatter_dimension=0, tiled=True
        ).astype(jnp.float32),
        lax.psum_scatter(
            grad_terms[4].astype(jnp.bfloat16), "fsdp", scatter_dimension=0, tiled=True
        ).astype(jnp.float32),
        lax.psum_scatter(
            grad_terms[5].astype(jnp.bfloat16), "fsdp", scatter_dimension=0, tiled=True
        ).astype(jnp.float32),
        lax.psum_scatter(
            grad_terms[6].astype(jnp.bfloat16), "fsdp", scatter_dimension=0, tiled=True
        ).astype(jnp.float32),
        lax.psum_scatter(
            grad_terms[7].astype(jnp.bfloat16), "fsdp", scatter_dimension=0, tiled=True
        ).astype(jnp.float32),
        lax.psum_scatter(
            grad_terms[8].astype(jnp.bfloat16), "fsdp", scatter_dimension=0, tiled=True
        ).astype(jnp.float32),
    )
    summed = (
        lax.psum(owned_grads[0].astype(jnp.bfloat16), "dp").astype(jnp.float32),
        lax.psum(owned_grads[1].astype(jnp.bfloat16), "dp").astype(jnp.float32),
        lax.psum(owned_grads[2].astype(jnp.bfloat16), "dp").astype(jnp.float32),
        lax.psum(owned_grads[3].astype(jnp.bfloat16), "dp").astype(jnp.float32),
        lax.psum(owned_grads[4].astype(jnp.bfloat16), "dp").astype(jnp.float32),
        lax.psum(owned_grads[5].astype(jnp.bfloat16), "dp").astype(jnp.float32),
        lax.psum(owned_grads[6].astype(jnp.bfloat16), "dp").astype(jnp.float32),
        lax.psum(owned_grads[7].astype(jnp.bfloat16), "dp").astype(jnp.float32),
        lax.psum(owned_grads[8].astype(jnp.bfloat16), "dp").astype(jnp.float32),
    )
    return (
        layer_out,
        tokens_grad,
        summed[4],
        summed[5],
        summed[0],
        summed[6],
        summed[1],
        summed[7],
        summed[8],
        summed[2],
        summed[3],
    )


def solution(mesh):
    in_specs = (
        P(("dp", "fsdp"), None),
        P("fsdp"),
        P("fsdp"),
        P("fsdp", None),
        P("fsdp"),
        P("fsdp", None),
        P("fsdp"),
        P("fsdp"),
        P("fsdp", None),
        P("fsdp", None),
        P(("dp", "fsdp"), None),
    )
    out_specs = (
        P(("dp", "fsdp"), None),
        P(("dp", "fsdp"), None),
        P("fsdp"),
        P("fsdp"),
        P("fsdp", None),
        P("fsdp"),
        P("fsdp", None),
        P("fsdp"),
        P("fsdp"),
        P("fsdp", None),
        P("fsdp", None),
    )
    return jax.shard_map(body, mesh=mesh, in_specs=in_specs, out_specs=out_specs, check_vma=False)
```

profile of v0, /device:TPU:0, one launch (start us, length us, event | category | flops | bytes accessed | tf_op | source)
XLA Modules:
  0.0 1132.2 jit_solution(1181279653588957996)
XLA Ops:
  9.3 5.1 all-gather.1
  14.3 5.3 all-gather
  20.4 5.1 all-gather.2
  28.1 47.2 %all-gather.12.cloned.1.call-done = bf16[1024,3072]{1,0:T(8,128)(2,1)} async-done(((bf16[256,3072]{1,0:T(8,128)(2,1)}), bf16[1024,3072]{1,0:T(8,128)(2,1)}) %all-gather.12.cloned.1.call-update) | async-done | bytes 6291472 | tf_op jit(solution)/shard_map/all_gather | solution.py:92
  75.3 4.9 convolution_add_fusion
  80.3 1.7 copy-done.13
  83.6 1.7 fusion.41
  89.5 5.1 all-gather.4
  94.5 5.2 all-gather.3
  100.8 13.0 %all-gather.14.cloned.1.call-done = bf16[1024,1024]{1,0:T(8,128)(2,1)} async-done(((bf16[256,1024]{1,0:T(8,128)(2,1)}), bf16[1024,1024]{1,0:T(8,128)(2,1)}) %all-gather.14.cloned.1.call-update) | async-done | bytes 2097168 | tf_op jit(solution)/shard_map/all_gather | solution.py:137
  113.8 2.9 copy.38
  116.6 28.6 %all-gather.16.cloned.1.call-done = bf16[1024,1024]{0,1:T(8,128)(2,1)} async-done(((bf16[256,1024]{0,1:T(8,128)(2,1)}), bf16[1024,1024]{0,1:T(8,128)(2,1)}) %all-gather.16.cloned.1.call-update) | async-done | bytes 2097168 | tf_op jit(solution)/shard_map/all_gather | solution.py:136
  145.3 4.7 fusion.42
  150.0 3.8 fusion
  153.8 1.8 copy-done
  156.1 5.0 fusion.13
  161.0 16.5 %all-gather.18.cloned.1.call-done = bf16[1024,1024]{1,0:T(8,128)(2,1)} async-done(((bf16[256,1024]{1,0:T(8,128)(2,1)}), bf16[1024,1024]{1,0:T(8,128)(2,1)}) %all-gather.18.cloned.1.call-update) | async-done | bytes 2097168 | tf_op jit(solution)/shard_map/all_gather | solution.py:93
  177.5 2.7 fusion.43
  181.1 105.0 %all-gather.20.cloned.1.call-done = bf16[1024,5632]{1,0:T(8,128)(2,1)} async-done(((bf16[256,5632]{1,0:T(8,128)(2,1)}), bf16[1024,5632]{1,0:T(8,128)(2,1)}) %all-gather.20.cloned.1.call-update) | async-done | bytes 11534352 | tf_op jit(solution)/shard_map/all_gather | solution.py:94
  286.1 9.4 fusion.40
  295.5 53.6 %all-gather.22.cloned.1.call-done = bf16[2816,1024]{1,0:T(8,128)(2,1)} async-done(((bf16[704,1024]{1,0:T(8,128)(2,1)}), bf16[2816,1024]{1,0:T(8,128)(2,1)}) %all-gather.22.cloned.1.call-update) | async-done | bytes 5767184 | tf_op jit(solution)/shard_map/all_gather | solution.py:95
  349.1 9.0 multiply_convert_fusion.3
  358.1 9.3 multiply_reduce_fusion.1
  371.2 15.2 %multiply_reduce_fusion = (f32[16,256]{1,0:T(8,128)}, f32[16,256,1024]{2,1,0:T(8,128)}) fusion(f32[16,256,1024]{2,1,0:T(8,128)} %copy-done, f32[16,256]{1,0:T(8,128)} %log_add_fusion, bf16[256,16,64]{0,2,1:T(8,128)(2,1)} %bitcast.56, bf16[1024,16,64]{0,2,1:T(8,128)(2,1)} %bitcast.52), kind=kOutput, calls=%fused_computation.1 | convolution fusion | flops 549449728 | bytes 36208640 | tf_op jit(solution)/shard_map/qhd,khd->hqk/dot_general | solution.py:202
  388.4 7.8 multiply_convert_fusion
  396.2 3.3 multiply_convert_fusion.1
  400.2 9.1 fusion.7
  409.4 3.2 convolution_convert_fusion.3
  412.8 5.3 convolution_convert_fusion.1
  418.4 6.8 fusion.11
  426.2 4.0 reduce-scatter.7.cloned.1.call-done
  434.4 28.3 %reduce-scatter.9.cloned.1.call-done = bf16[256,1024]{0,1:T(8,128)(2,1)} async-done(((bf16[1024,1024]{0,1:T(8,128)(2,1)}), bf16[256,1024]{0,1:T(8,128)(2,1)}) %reduce-scatter.9.cloned.1.call-update) | async-done | bytes 524304 | tf_op jit(solution)/shard_map/reduce_scatter | solution.py:226
  462.7 5.9 convolution_convert_fusion.2
  469.3 9.5 convolution_convert_fusion
  478.8 15.5 %reduce-scatter.13.cloned.1.call-done = bf16[256,1024]{1,0:T(8,128)(2,1)} async-done(((bf16[1024,1024]{1,0:T(8,128)(2,1)}), bf16[256,1024]{1,0:T(8,128)(2,1)}) %reduce-scatter.13.cloned.1.call-update) | async-done | bytes 524304 | tf_op jit(solution)/shard_map/reduce_scatter | solution.py:265
  494.4 62.2 %reduce-scatter.17.cloned.1.call-done = bf16[704,1024]{1,0:T(8,128)(2,1)} async-done(((bf16[2816,1024]{1,0:T(8,128)(2,1)}), bf16[704,1024]{1,0:T(8,128)(2,1)}) %reduce-scatter.17.cloned.1.call-update) | async-done | bytes 1441808 | tf_op jit(solution)/shard_map/reduce_scatter | solution.py:271
  556.6 66.1 %reduce-scatter.11.cloned.1.call-done = bf16[256,3072]{1,0:T(8,128)(2,1)} async-done(((bf16[1024,3072]{1,0:T(8,128)(2,1)}), bf16[256,3072]{1,0:T(8,128)(2,1)}) %reduce-scatter.11.cloned.1.call-update) | async-done | bytes 1572880 | tf_op jit(solution)/shard_map/reduce_scatter | solution.py:262
  622.7 108.1 %reduce-scatter.15.cloned.1.call-done = bf16[256,5632]{1,0:T(8,128)(2,1)} async-done(((bf16[1024,5632]{1,0:T(8,128)(2,1)}), bf16[256,5632]{1,0:T(8,128)(2,1)}) %reduce-scatter.15.cloned.1.call-update) | async-done | bytes 2883600 | tf_op jit(solution)/shard_map/reduce_scatter | solution.py:268
  733.4 5.6 fusion.12
  739.5 5.0 fusion.26
  744.5 11.4 %all-reduce.7 = (bf16[1024]{0:T(1024)(128)(2,1)S(1)}, bf16[1024]{0:T(1024)(128)(2,1)S(1)}, bf16[3072]{0:T(1024)(128)(2,1)S(1)}, bf16[1024]{0:T(1024)(128)(2,1)S(1)}, bf16[1024]{0:T(1024)(128)(2,1)S(1)}) all-reduce(bf16[1024]{0:T(1024)(128)(2,1)S(1)} %get-tuple-element.13, ...), channel_id=4, replica_groups=mesh['dp'=32,'fsdp'=4] {'fsdp'}, use_global_device_ids=true, to_apply=%region_14.15.clone | all-reduce | flops 7168 | bytes 28672
  756.2 95.9 %all-reduce.5 = (bf16[256]{0:T(256)(128)(2,1)S(1)}, bf16[256]{0:T(256)(128)(2,1)S(1)}, bf16[768]{0:T(1024)(128)(2,1)S(1)}, bf16[256]{0:T(256)(128)(2,1)S(1)}, bf16[256]{0:T(256)(128)(2,1)S(1)}) all-reduce(bf16[256]{0:T(256)(128)(2,1)S(1)} %dynamic-slice.1, ...), channel_id=1, replica_groups=mesh['dp'=32,'fsdp'=4] {'dp'}, use_global_device_ids=true, to_apply=%region_15.16 | all-reduce | flops 1792 | bytes 7168 | tf_op jit(solution)/shard_map/psum | solution.py:295
  855.0 1.3 fusion.25
  856.3 257.2 %all-reduce.10.cloned.1.call-done = (bf16[256,3072]{1,0:T(8,128)(2,1)}, bf16[256,1024]{1,0:T(8,128)(2,1)}, bf16[256,5632]{1,0:T(8,128)(2,1)}, bf16[704,1024]{1,0:T(8,128)(2,1)}) async-done(((bf16[256,3072]{1,0:T(8,128)(2,1)}, bf16[256,1024]{1,0:T(8,128)(2,1)}, bf16[256,5632]{1,0:T(8,128)(2,1)}, bf16[704,1024]{1,0:T(8,128)(2,1)}), (bf16[256,3072]{1,0:T(8,128)(2,1)}, bf16[256,1024]{1,0:T(8,128)(2,1)}, ...) | async-done | bytes 6422544 | tf_op jit(solution)/shard_map/psum | solution.py:291
  1113.5 2.2 convert_element_type.199
  1115.7 3.4 convert_element_type.196
  1119.2 1.9 convert_element_type.207
  1122.0 3.2 convert_element_type.205
  (175 shorter events, 31.9 us)
Async XLA Ops:
  7.2 68.1 %all-gather.12.cloned.1.call-start = ((), (), s32[]{:S(2)}) async-start(), calls=%async_computation.6 | async-start | bytes 7864320 | tf_op jit(solution)/shard_map/all_gather | solution.py:92
  7.9 105.8 %all-gather.14.cloned.1.call-start = ((), (), s32[]{:S(2)}) async-start(), calls=%async_computation.7 | async-start | bytes 2621440 | tf_op jit(solution)/shard_map/all_gather | solution.py:137
  14.3 65.9 %copy-start.38 = (f32[4,1,256]{2,1,0:T(1,128)}, f32[4,1,256]{2,1,0:T(1,128)S(1)}, u32[]{:S(2)}) copy-start(f32[4,1,256]{2,1,0:T(1,128)S(1)} %convert_element_type.209) | copy-start | bytes 12292
  19.7 60.5 %copy-start.31 = (f32[4,1,256]{2,1,0:T(1,128)}, f32[4,1,256]{2,1,0:T(1,128)S(1)}, u32[]{:S(2)}) copy-start(f32[4,1,256]{2,1,0:T(1,128)S(1)} %convert_element_type.208) | copy-start | bytes 12292
  26.8 53.5 %copy-start.34 = (f32[256]{0:T(256)}, f32[256]{0:T(256)S(1)}, u32[]{:S(2)}) copy-start(f32[256]{0:T(256)S(1)} %broadcast_multiply_fusion.5) | copy-start | bytes 3076
  28.1 52.1 %copy-start.36 = (f32[256]{0:T(256)}, f32[256]{0:T(256)S(1)}, u32[]{:S(2)}) copy-start(f32[256]{0:T(256)S(1)} %add_rsqrt_fusion.1) | copy-start | bytes 3076
  82.8 62.4 %all-gather.16.cloned.1.call-start = ((), (), s32[]{:S(2)}) async-start(), calls=%async_computation.8 | async-start | bytes 2621440 | tf_op jit(solution)/shard_map/all_gather | solution.py:136
  87.6 89.9 %all-gather.18.cloned.1.call-start = ((), (), s32[]{:S(2)}) async-start(), calls=%async_computation.9 | async-start | bytes 2621440 | tf_op jit(solution)/shard_map/all_gather | solution.py:93
  88.2 197.9 %all-gather.20.cloned.1.call-start = ((), (), s32[]{:S(2)}) async-start(), calls=%async_computation.10 | async-start | bytes 14417920 | tf_op jit(solution)/shard_map/all_gather | solution.py:94
  88.8 260.3 %all-gather.22.cloned.1.call-start = ((), (), s32[]{:S(2)}) async-start(), calls=%async_computation.11 | async-start | bytes 7208960 | tf_op jit(solution)/shard_map/all_gather | solution.py:95
  89.4 340.9 %reduce-scatter.7.cloned.1.call-start = ((), (), s32[]{:S(2)}) async-start(), calls=%async_computation.12 | async-start | bytes 2621440 | tf_op jit(solution)/shard_map/reduce_scatter | solution.py:223
  100.8 49.2 %copy-start.8 = (bf16[256,16,48]{0,2,1:T(8,128)(2,1)}, bf16[256,16,48]{0,2,1:T(8,128)(2,1)S(1)}, u32[]{:S(2)}) copy-start(bf16[256,16,48]{0,2,1:T(8,128)(2,1)S(1)} %slice.121) | copy-start | bytes 1179652
  100.8 44.5 %copy-start.19 = (pred[256,1024]{1,0:T(8,128)(4,1)S(1)}, pred[256,1024]{1,0:T(8,128)(4,1)}, u32[]{:S(2)}) copy-start(pred[256,1024]{1,0:T(8,128)(4,1)} %iota_compare_fusion) | copy-start | bytes 786436
  116.6 37.2 %copy-start.5 = (bf16[1024,1024]{0,1:T(8,128)(2,1)}, bf16[1024,1024]{0,1:T(8,128)(2,1)S(1)}, u32[]{:S(2)}) copy-start(bf16[1024,1024]{0,1:T(8,128)(2,1)S(1)} %copy.38) | copy-start | bytes 6291460
  149.9 5.7 copy-start
  150.0 6.1 copy-start.24
  161.0 19.4 %copy-start.25 = (f32[16,256]{1,0:T(8,128)S(1)}, f32[16,256]{1,0:T(8,128)}, u32[]{:S(2)}) copy-start(f32[16,256]{1,0:T(8,128)} %copy-done.24) | copy-start | bytes 49156
  180.5 187.0 %copy-start.28 = (f32[256]{0:T(256)}, f32[256]{0:T(256)S(1)}, u32[]{:S(2)}) copy-start(f32[256]{0:T(256)S(1)} %add_rsqrt_fusion) | copy-start | bytes 3076
  286.1 63.0 %copy-start.15 = (bf16[256,1024]{1,0:T(8,128)(2,1)S(1)}, bf16[256,1024]{1,0:T(8,128)(2,1)}, u32[]{:S(2)}) copy-start(bf16[256,1024]{1,0:T(8,128)(2,1)} %param.21) | copy-start | bytes 1572868
  358.1 9.4 copy-start.17
  358.1 9.3 copy-start.18
  371.2 15.2 %slice-start = ((s8[16777216]{0:T(1024)(128)(4,1)}), s8[4194304]{0:T(1024)(128)(4,1)S(1)}, s32[]{:S(2)}) async-start(s8[16777216]{0:T(1024)(128)(4,1)} %bitcast.48), calls=%async_computation.19 | async-start | bytes 8388608
  371.2 15.2 %slice-start.1 = ((s8[16777216]{0:T(1024)(128)(4,1)}), s8[4194304]{0:T(1024)(128)(4,1)S(1)}, s32[]{:S(2)}) async-start(s8[16777216]{0:T(1024)(128)(4,1)} %bitcast.48), calls=%async_computation.20 | async-start | bytes 8388608
  371.2 16.0 %slice-start.2 = ((s8[16777216]{0:T(1024)(128)(4,1)}), s8[4194304]{0:T(1024)(128)(4,1)S(1)}, s32[]{:S(2)}) async-start(s8[16777216]{0:T(1024)(128)(4,1)} %bitcast.48), calls=%async_computation.21 | async-start | bytes 8388608
  371.2 17.2 %slice-start.3 = ((s8[16777216]{0:T(1024)(128)(4,1)}), s8[4194304]{0:T(1024)(128)(4,1)S(1)}, s32[]{:S(2)}) async-start(s8[16777216]{0:T(1024)(128)(4,1)} %bitcast.48), calls=%async_computation.22 | async-start | bytes 8388608
  388.4 7.8 copy-start.9
  388.4 7.8 copy-start.20
  388.4 7.8 copy-start.21
  396.2 4.0 copy-start.7
  400.2 9.3 copy-start.3
  400.2 62.5 %reduce-scatter.9.cloned.1.call-start = ((), (), s32[]{:S(2)}) async-start(), calls=%async_computation.13 | async-start | bytes 2621440 | tf_op jit(solution)/shard_map/reduce_scatter | solution.py:226
  409.4 85.0 %reduce-scatter.13.cloned.1.call-start = ((), (), s32[]{:S(2)}) async-start(), calls=%async_computation.15 | async-start | bytes 2621440 | tf_op jit(solution)/shard_map/reduce_scatter | solution.py:265
  412.7 143.9 %reduce-scatter.17.cloned.1.call-start = ((), (), s32[]{:S(2)}) async-start(), calls=%async_computation.17 | async-start | bytes 7208960 | tf_op jit(solution)/shard_map/reduce_scatter | solution.py:271
  418.1 204.6 %reduce-scatter.11.cloned.1.call-start = ((), (), s32[]{:S(2)}) async-start(), calls=%async_computation.14 | async-start | bytes 7864320 | tf_op jit(solution)/shard_map/reduce_scatter | solution.py:262
  426.1 6.3 copy-start.27
  426.1 6.3 copy-start.30
  426.1 36.5 %copy-start.6 = (bf16[256,1024]{1,0:T(8,128)(2,1)S(1)}, bf16[256,1024]{1,0:T(8,128)(2,1)}, u32[]{:S(2)}) copy-start(bf16[256,1024]{1,0:T(8,128)(2,1)} %param.11) | copy-start | bytes 1572868
  426.2 36.5 %copy-start.32 = (f32[4,1,256]{2,1,0:T(1,128)S(1)}, f32[4,1,256]{2,1,0:T(1,128)}, u32[]{:S(2)}) copy-start(f32[4,1,256]{2,1,0:T(1,128)} %copy-done.31) | copy-start | bytes 12292
  468.6 262.1 %reduce-scatter.15.cloned.1.call-start = ((), (), s32[]{:S(2)}) async-start(), calls=%async_computation.16 | async-start | bytes 14417920 | tf_op jit(solution)/shard_map/reduce_scatter | solution.py:268
  478.8 634.7 %all-reduce.10.cloned.1.call-start = ((), (), s32[]{:S(2)}) async-start(), calls=%async_computation.18 | async-start | bytes 12845056 | tf_op jit(solution)/shard_map/psum | solution.py:291
  733.3 5.7 copy-start.14
  733.3 5.7 copy-start.22
  733.3 6.1 copy-start.33
  733.3 6.1 copy-start.35
  733.3 6.1 copy-start.37
  739.5 5.0 copy-start.39
  739.5 5.0 copy-start.40
  1113.5 5.7 copy-start.16
  (13 other events, 28.9 us)
Sparse Core Ops, SparseCore 0:
  9.7 65.5 all-gather.11
  82.9 30.7 all-gather.13
  116.0 29.2 all-gather.15
  146.8 30.6 all-gather.17
  179.0 107.0 all-gather.19
  287.6 61.4 all-gather.21
  400.3 29.9 reduce-scatter.6
  433.4 29.2 reduce-scatter.8
  465.1 29.2 reduce-scatter.12
  497.3 59.2 reduce-scatter.16
  559.1 63.4 reduce-scatter.10
  625.1 105.5 reduce-scatter.14
  733.8 379.6 all-reduce.9
where the time goes:
time: 1140 us; the launch traced here: 1130 us
  waiting for transfers between devices  808 us (71%)
  blocking collectives  133 us (12%)
  matrix products  115 us (10%)
  other arithmetic  37.3 us (3%)
  local copies, waits for them, and re-layouts  22.4 us (2%)
  between operations  16.3 us (1%)
    psum x1, waiting for transfers between devices, body(): lax.psum(owned_grads[0].astype(jnp.bfloat16), 'dp').astype(jnp.float32)  257 us
    reduce_scatter x1, waiting for transfers between devices, body(): lax.psum_scatter(grad_terms[2].astype(jnp.bfloat16), 'fsdp', scatter_dime...  108 us
    all_gather x1, waiting for transfers between devices, body(): lax.all_gather(gate_up_weight, 'fsdp', axis=0, tiled=True)  105 us
    psum x1, blocking collectives, body(): lax.psum(owned_grads[4].astype(jnp.bfloat16), 'dp').astype(jnp.float32)  95.9 us
    reduce_scatter x1, waiting for transfers between devices, body(): lax.psum_scatter(grad_terms[0].astype(jnp.bfloat16), 'fsdp', scatter_dime...  66.1 us
    reduce_scatter x1, waiting for transfers between devices, body(): lax.psum_scatter(grad_terms[3].astype(jnp.bfloat16), 'fsdp', scatter_dime...  62.2 us
    all_gather x1, waiting for transfers between devices, body(): lax.all_gather(down_weight, 'fsdp', axis=0, tiled=True)  53.6 us
    all_gather x1, waiting for transfers between devices, body(): lax.all_gather(qkv_weight, 'fsdp', axis=0, tiled=True)  47.2 us
  transfers between devices with their start and end apart: 13, of which 13 were waited for; matrix products, arithmetic and copies ran while one was open for 9% of the time, Pallas kernels for 0%

commit v1 on v0

v1 whole, which is shorter than its diff:
```python
import functools
import math

import jax
import jax.numpy as jnp
from jax import lax
from jax.experimental import pallas as pl
from jax.experimental.pallas import tpu as pltpu
from jax.sharding import PartitionSpec as P

D = 1024
HEADS = 16
HEAD = 64
ROTARY = 16
FF = 2816
GROUP = 4
ROWS = 256
FFS = FF // GROUP
FFP = 768
EPS = 1e-05
F32 = jnp.float32
BF16 = jnp.bfloat16
AXES = ("dp", "fsdp")
LOG2E = 1.0 / math.log(2.0)
SCALE2 = HEAD ** (-0.5) * LOG2E


def where_is(lin):
    return [(lin // 16) % 4, (lin // 4) % 4, (lin // 64) * 2 + (lin // 2) % 2, lin % 2]


def linear(x, y, z, core):
    return (((z // 2) * 4 + x) * 4 + y) * 4 + (z % 2) * 2 + core


def perm_of(move):
    return tuple((lin, linear(*move(*where_is(lin)))) for lin in range(128))


def flip(v, which):
    return v ^ 1 if which == 0 else 3 - v


SIBLING = perm_of(lambda x, y, z, c: (x, y, z, 1 - c))
ZNEAR = perm_of(lambda x, y, z, c: (x, y, z ^ 1, c))
ZFAR = perm_of(lambda x, y, z, c: (x, y, 3 - z, c))
ZFAR_SIBLING = perm_of(lambda x, y, z, c: (x, y, 3 - z, 1 - c))
ZNEAR_SIBLING = perm_of(lambda x, y, z, c: (x, y, z ^ 1, 1 - c))
ZREPLICA = perm_of(lambda x, y, z, c: (x, y, (z + 2) % 4, c))
SIBLING_T = perm_of(lambda x, y, z, c: (y, x, z, 1 - c))
ZNEAR_SIBLING_T = perm_of(lambda x, y, z, c: (y, x, z ^ 1, 1 - c))


def cube_move(bit):
    def move(x, y, z, c):
        on_x = (bit < 2) == (c == 0)
        return (flip(x, bit % 2), y, z, c) if on_x else (x, flip(y, bit % 2), z, c)

    return perm_of(move)


CUBE = tuple(cube_move(bit) for bit in range(4))


def gray(v):
    return (((v + 1) // 2) % 2, v // 2)


def piece_of(x, y, c):
    first, second = (x, y) if c == 0 else (y, x)
    a, b = gray(first)
    d, e = gray(second)
    return 8 * a + 4 * b + 2 * d + e


def plane_groups():
    groups = {}
    for lin in range(128):
        x, y, z, c = where_is(lin)
        groups.setdefault((z, c), []).append((4 * x + y, lin))
    return [[lin for _, lin in sorted(g)] for g in groups.values()]


PLANES = plane_groups()
PIECES = tuple(piece_of(n // 4, n % 4, 0) for n in range(16))
SPLITS = (
    ((0, 2, 128), (1, 2, 64), (2, 2, 32), (3, 2, 16)),
    ((1, 4, 64), (0, 2, 64), (3, 4, 16), (2, 2, 16)),
)
ME, SLOT, BIT = 0, 1, 5


def send(value, perm):
    return lax.ppermute(value, AXES, perm)


def dot(a, b):
    return lax.dot_general(a, b, (((1,), (0,)), ((), ())), preferred_element_type=F32)


def dot_nt(a, b):
    return lax.dot_general(a, b, (((1,), (1,)), ((), ())), preferred_element_type=F32)


def dot_tn(a, b):
    return lax.dot_general(a, b, (((0,), (0,)), ((), ())), preferred_element_type=F32)


def shaped(*shape, dtype=BF16):
    return jax.ShapeDtypeStruct(shape, dtype)


SMEM = pl.BlockSpec(memory_space=pltpu.SMEM)
ANY = pl.BlockSpec(memory_space=pl.ANY)
VMEM = pl.BlockSpec(memory_space=pltpu.VMEM)


def call(kernel, name, in_specs, out_shape, operands, *, us=1, limit=48, **kw):
    return pl.pallas_call(
        kernel,
        in_specs=in_specs,
        out_shape=out_shape,
        compiler_params=pltpu.CompilerParams(vmem_limit_bytes=limit << 20),
        cost_estimate=pl.CostEstimate(flops=us * 10**9, bytes_accessed=us << 20, transcendentals=0),
        name=name,
        **kw,
    )(*operands)


def row_of(slot, rows=ROWS):
    return pl.ds(pl.multiple_of(slot * rows, rows), rows)


def lanes_of(start, width=128):
    return pl.ds(pl.multiple_of(start, 128), width)


def stats_of(x):
    cen = x - jnp.mean(x, axis=1, keepdims=True)
    inv = lax.rsqrt(jnp.mean(cen * cen, axis=1, keepdims=True) + EPS)
    return cen * inv, inv


def partner_of(t, lane):
    return jnp.where(lane % HEAD < ROTARY // 2, pltpu.roll(t, 120, 1), pltpu.roll(t, 8, 1))


def pack_kernel(a_ref, b_ref, c_ref, d_ref, bias_ref, out_ref):
    out_ref[...] = jnp.zeros((16, D), BF16)
    for v, ref in enumerate((a_ref, b_ref, c_ref, d_ref)):
        out_ref[0:1, 256 * v : 256 * v + 256] = ref[...]
    out_ref[1:2, :768] = bias_ref[...]


def pack(*vectors):
    rows = [v.reshape(1, -1) for v in vectors]
    return call(pack_kernel, "pack", [VMEM] * 5, shaped(16, D), rows, limit=16, us=0)


def tables_kernel(info, cos_ref, sin_ref):
    at = lax.broadcasted_iota(jnp.int32, (ROWS, 128), 1) % HEAD
    rate = jnp.exp((at % (ROTARY // 2)).astype(F32) * (-math.log(10000.0) / (ROTARY // 2)))
    row = lax.broadcasted_iota(jnp.int32, (ROWS, 128), 0)
    for j in range(GROUP):
        place = row + (info[ME] ^ (0, 2, 1, 3)[j]) * ROWS
        angle = place.astype(F32) * rate
        sin = jnp.where(at < ROTARY // 2, -jnp.sin(angle), jnp.sin(angle))
        rows = slice(ROWS * j, ROWS * j + ROWS)
        cos_ref[rows, :] = jnp.where(at < ROTARY, jnp.cos(angle), 1.0)
        sin_ref[rows, :] = jnp.where(at < ROTARY, sin, 0.0)


def tables(info):
    return call(tables_kernel, "tables", [SMEM], [shaped(D, 128, dtype=F32)] * 2, (info,), limit=16, us=0)


def pick_qkv_kernel(info, w_ref, *outs):
    for j, out in enumerate(outs):
        d = info[ME] ^ j
        for c in range(3):
            out[:, 256 * c : 256 * c + 256] = w_ref[:, lanes_of(c * D + d * 256, 256)]


def pick_qkv(info, w):
    return call(
        pick_qkv_kernel, "pick_qkv", [SMEM, VMEM], [shaped(ROWS, 768)] * 4, (info, w), limit=32, us=0
    )


def pick_gate_up_kernel(info, w_ref, *refs):
    outs, all_ref = refs[:4], refs[4]
    all_ref[...] = jnp.zeros_like(all_ref)
    for d in range(GROUP):
        all_ref[d, :, :FFS] = w_ref[:, FFS * d : FFS * d + FFS]
        all_ref[d, :, FFP : FFP + FFS] = w_ref[:, FF + FFS * d : FF + FFS * d + FFS]
    for j, out in enumerate(outs):
        out[...] = all_ref[info[ME] ^ j]


def pick_gate_up(info, w):
    return call(
        pick_gate_up_kernel,
        "pick_gate_up",
        [SMEM, VMEM],
        [shaped(ROWS, 2 * FFP)] * 4,
        (info, w),
        limit=32,
        us=0,
        scratch_shapes=[pltpu.VMEM((GROUP, ROWS, 2 * FFP), BF16)],
    )


def project_kernel(
    info, x0, x1, x2, x3, v0, v1, v2, v3, w0, w1, w2, w3, cos_ref, sin_ref,
    hid_ref, qkv_ref, w_ref, norms_ref, bias_ref, sems,
):
    me = info[ME]
    copies = []
    for j, w in enumerate((w0, w1, w2, w3)):
        copy = pltpu.make_async_copy(w, w_ref.at[row_of(me ^ j)], sems.at[j])
        copy.start()
        copies.append(copy)
    for j, v in enumerate((v0, v1, v2, v3)):
        owner = me ^ (0, 2, 1, 3)[j]
        extra = v[0:2, :].astype(F32)
        for n in range(4):
            norms_ref[n : n + 1, lanes_of(owner * 256, 256)] = extra[0:1, 256 * n : 256 * n + 256]
        bias_ref[0:1, lanes_of(owner * 768, 768)] = extra[1:2, :768]
    gain, shift = norms_ref[0:1, :], norms_ref[1:2, :]
    bias = jnp.concatenate(
        [bias_ref[0:1, lanes_of(c * D + me * 256, 256)] for c in range(3)], axis=1
    )
    lane = lax.broadcasted_iota(jnp.int32, (ROWS, 128), 1)
    for j, x in enumerate((x0, x1, x2, x3)):
        rows = slice(ROWS * j, ROWS * j + ROWS)
        xhat, _ = stats_of(x[...].astype(F32))
        hid = (xhat * gain + shift).astype(BF16)
        hid_ref[rows, :] = hid
        if j == 0:
            for copy in copies:
                copy.wait()
        proj = dot(hid, w_ref[...]) + bias
        cos, sin = cos_ref[rows, :], sin_ref[rows, :]
        for c in range(4):
            t = proj[:, 128 * c : 128 * c + 128]
            qkv_ref[rows, 128 * c : 128 * c + 128] = (t * cos + partner_of(t, lane) * sin).astype(BF16)
        qkv_ref[rows, 512:] = proj[:, 512:].astype(BF16)


def project(info, xs, vs, ws, cos, sin):
    return call(
        project_kernel,
        "project",
        [SMEM] + [VMEM] * 8 + [ANY] * 4 + [VMEM] * 2,
        [shaped(D, D), shaped(D, 768), shaped(D, 768), shaped(8, D, dtype=F32)],
        (info, *xs, *vs, *ws, cos, sin),
        us=0,
        scratch_shapes=[pltpu.VMEM((8, 3 * D), F32), pltpu.SemaphoreType.DMA((4,))],
    )


def later_keys():
    return lax.broadcasted_iota(jnp.int32, (ROWS, ROWS), 0) > lax.broadcasted_iota(
        jnp.int32, (ROWS, ROWS), 1
    )


def attend_kernel(info, qkv_ref, w_ref, mixed_ref, lse_ref, low_ref, up_ref):
    pair = pl.program_id(0)
    side = lax.broadcasted_iota(jnp.int32, (ROWS, 128), 1) // HEAD
    lane0 = pair * 128
    later = later_keys()
    zero = jnp.zeros((), BF16)
    for i in range(GROUP):
        rows = row_of(info[SLOT + i])
        both = qkv_ref[rows, lanes_of(lane0)]
        outs = []
        for h in range(2):
            q = jnp.where(side == h, both, zero)
            tiles = []
            for n in range(i + 1):
                st = dot_nt(qkv_ref[row_of(info[SLOT + n]), lanes_of(lane0 + 256)], q)
                tiles.append(jnp.where(later, -1e30, st) if n == i else st)
            top = functools.reduce(jnp.maximum, [jnp.max(t, axis=0, keepdims=True) for t in tiles])
            top = top * SCALE2
            total = jnp.zeros((1, ROWS), F32)
            out = jnp.zeros((128, ROWS), F32)
            for n in range(i + 1):
                p = jnp.exp2(tiles[n] * SCALE2 - top)
                total = total + jnp.sum(p, axis=0, keepdims=True)
                v = qkv_ref[row_of(info[SLOT + n]), lanes_of(lane0 + 512)]
                out = out + dot_tn(v, p.astype(BF16))
            outs.append((out / total).T)
            lse_ref[0, h : h + 1, rows] = top + jnp.log2(total)
        mixed_ref[rows, lanes_of(lane0)] = jnp.where(side == 0, outs[0], outs[1]).astype(BF16)

    @pl.when(pair == 1)
    def _():
        up_ref[...] = dot(mixed_ref[512:, :], w_ref[...]).astype(BF16)
        low_ref[...] = dot(mixed_ref[:512, :], w_ref[...]).astype(BF16)


def attend(info, qkv, w):
    fixed = lambda h: (0, 0)
    return call(
        attend_kernel,
        "attend",
        [SMEM, pl.BlockSpec((D, 768), fixed), pl.BlockSpec((256, D), fixed)],
        [shaped(D, 256), shaped(2, 2, D, dtype=F32), shaped(512, D), shaped(512, D)],
        (info, qkv, w),
        us=0,
        grid=(2,),
        out_specs=[
            pl.BlockSpec((D, 256), fixed),
            pl.BlockSpec((1, 2, D), lambda h: (h, 0, 0)),
            pl.BlockSpec((512, D), fixed),
            pl.BlockSpec((512, D), fixed),
        ],
    )


def attend_back_kernel(
    pair, info, qkv_ref, b0, b1, b2, b3, w_ref, lse_ref, cos_ref, sin_ref,
    out_ref, do_ref, dq_ref, dk_ref, dv_ref,
):
    side = lax.broadcasted_iota(jnp.int32, (ROWS, 128), 1) // HEAD
    cols = [slice(256 * c + 128 * pair, 256 * c + 128 * pair + 128) for c in range(3)]
    later = later_keys()
    zero = jnp.zeros((), BF16)
    for j, b in enumerate((b0, b1, b2, b3)):
        do_ref[ROWS * j : ROWS * j + ROWS, :] = dot_nt(b[...], w_ref[...]).astype(BF16)
    dk_ref[...] = jnp.zeros_like(dk_ref)
    dv_ref[...] = jnp.zeros_like(dv_ref)
    for i in range(GROUP):
        rows = row_of(info[SLOT + i])
        q_both = qkv_ref[rows, cols[0]]
        do_both = do_ref[rows, :]
        dqt = jnp.zeros((128, ROWS), F32)
        for h in range(2):
            q = jnp.where(side == h, q_both, zero)
            do = jnp.where(side == h, do_both, zero)
            lse = lse_ref[pair, h : h + 1, rows]
            probs, grads = [], []
            delta = jnp.zeros((1, ROWS), F32)
            for n in range(i + 1):
                there = row_of(info[SLOT + n])
                p = jnp.exp2(dot_nt(qkv_ref[there, cols[1]], q) * SCALE2 - lse)
                if n == i:
                    p = jnp.where(later, 0.0, p)
                dp = dot_nt(qkv_ref[there, cols[2]], do)
                delta = delta + jnp.sum(p * dp, axis=0, keepdims=True)
                dv_ref[there, :] += dot(p.astype(BF16), do)
                probs.append(p)
                grads.append(dp)
            for n in range(i + 1):
                there = row_of(info[SLOT + n])
                k = jnp.where(side == h, qkv_ref[there, cols[1]], zero)
                ds = (probs[n] * (grads[n] - delta)).astype(BF16)
                dk_ref[there, :] += dot(ds, q)
                dqt = dqt + dot_tn(k, ds)
        dq_ref[rows, :] = dqt.T
    lane = lax.broadcasted_iota(jnp.int32, (D, 128), 1)
    scale = HEAD ** (-0.5)
    cos, sin = cos_ref[...], sin_ref[...]
    dq = dq_ref[...] * scale
    out_ref[:, :128] = (dq * cos - partner_of(dq, lane) * sin).astype(BF16)
    dk = dk_ref[...] * scale
    out_ref[:, 128:256] = (dk * cos - partner_of(dk, lane) * sin).astype(BF16)
    out_ref[:, 256:] = dv_ref[...].astype(BF16)


def attend_back(pair, info, qkv, branch, w, lse, cos, sin):
    fixed = lambda i: (0, 0)
    block = pl.BlockSpec((ROWS, D), fixed)
    return call(
        functools.partial(attend_back_kernel, pair),
        "attend_back",
        [
            SMEM,
            pl.BlockSpec((D, 768), fixed),
            block, block, block, block,
            pl.BlockSpec((128, D), lambda i: (pair, 0)),
            pl.BlockSpec((2, 2, D), lambda i: (0, 0, 0)),
            pl.BlockSpec((D, 128), fixed),
            pl.BlockSpec((D, 128), fixed),
        ],
        shaped(D, 384),
        (info, qkv, *branch, w, lse, cos, sin),
        us=7,
        grid=(1,),
        out_specs=pl.BlockSpec((D, 384), fixed),
        scratch_shapes=[pltpu.VMEM((D, 128), BF16)] + [pltpu.VMEM((D, 128), F32)] * 3,
    )


def whole(first, second):
    return jnp.concatenate(
        [v[:, 128 * c : 128 * c + 128] for c in range(3) for v in (first, second)], axis=1
    )


def hidden_back_kernel(d0, d1, w_ref, x0, x1, x2, x3, low_ref, up_ref, sums_ref):
    gains = jnp.zeros((1, D), F32)
    shifts = jnp.zeros((1, D), F32)
    for j in (2, 3, 0, 1):
        x = (x0, x1, x2, x3)[j]
        rows = slice(ROWS * j, ROWS * j + ROWS)
        e = dot_nt(whole(d0[rows, :], d1[rows, :]), w_ref[...])
        xhat, _ = stats_of(x[...].astype(F32))
        gains = gains + jnp.sum(e * xhat, axis=0, keepdims=True)
        shifts = shifts + jnp.sum(e, axis=0, keepdims=True)
        out = low_ref if j < 2 else up_ref
        out[ROWS * (j % 2) : ROWS * (j % 2) + ROWS, :] = e.astype(BF16)
    sums_ref[0:1, :] = gains
    sums_ref[1:2, :] = shifts


def hidden_back(dqkvs, w, xs):
    return call(
        hidden_back_kernel,
        "hidden_back",
        [VMEM] * 7,
        [shaped(512, D), shaped(512, D), shaped(2, D, dtype=F32)],
        (*dqkvs, w, *xs),
        us=5,
    )


def add_halves_kernel(low_ref, got_ref, own_ref, near_ref):
    total = low_ref[...].astype(F32) + got_ref[...].astype(F32)
    own_ref[...] = total[:ROWS, :]
    near_ref[...] = total[ROWS:, :].astype(BF16)


def scatter_group(low, up):
    own, near = call(
        add_halves_kernel,
        "add_halves",
        [VMEM] * 2,
        [shaped(ROWS, D, dtype=F32), shaped(ROWS, D)],
        (low, send(up, SIBLING)),
        limit=16,
    )
    return own, near


def gather_group(own, keep=None):
    near = send(own, ZNEAR)
    return (own, near, send(own, SIBLING), send(near, SIBLING))


def middle_kernel(x_ref, part_ref, other_ref, norms_ref, mid_ref, hid_ref):
    mid = x_ref[...].astype(F32) + part_ref[...] + other_ref[...].astype(F32)
    mid_ref[...] = mid
    xhat, _ = stats_of(mid)
    hid_ref[...] = (xhat * norms_ref[2:3, :] + norms_ref[3:4, :]).astype(BF16)


def middle_of(x, part, other, norms):
    return call(
        middle_kernel,
        "middle",
        [VMEM] * 4,
        [shaped(ROWS, D, dtype=F32), shaped(ROWS, D)],
        (x, part, other, norms),
        limit=16,
    )


def norm_back_kernel(which, part_ref, other_ref, base_ref, res_ref, norms_ref, out_ref, *rest):
    e = part_ref[...] + other_ref[...].astype(F32)
    xhat, inv = stats_of(base_ref[...].astype(F32))
    u = e * norms_ref[which : which + 1, :]
    back = u - jnp.mean(u, axis=1, keepdims=True) - xhat * jnp.mean(u * xhat, axis=1, keepdims=True)
    out = res_ref[...].astype(F32) + inv * back
    out_ref[...] = out
    if rest:
        low_ref, sums_ref = rest
        low_ref[...] = out.astype(BF16)
        sums_ref[0:1, :] = jnp.sum(e * xhat, axis=0, keepdims=True)
        sums_ref[1:2, :] = jnp.sum(e, axis=0, keepdims=True)


def norm_back(part, other, base, res, norms, which):
    outs = [shaped(ROWS, D, dtype=F32)]
    if which == 2:
        outs += [shaped(ROWS, D), shaped(2, D, dtype=F32)]
    return call(
        functools.partial(norm_back_kernel, which),
        "norm_back",
        [VMEM] * 5,
        outs,
        (part, other, base, res, norms),
        limit=16,
    )


def layer_out_kernel(mid_ref, part_ref, other_ref, out_ref):
    out_ref[...] = (mid_ref[...] + part_ref[...] + other_ref[...].astype(F32)).astype(BF16)


def layer_out_of(mid, part, other):
    return call(
        layer_out_kernel, "layer_out", [VMEM] * 3, shaped(ROWS, D), (mid, part, other), limit=16
    )


def feed_kernel(
    info, h0, h1, h2, h3, g0, g1, g2, g3, w0, w1, w2, w3, d_ref,
    act_ref, dgu_ref, gh_low, gh_up, out_low, out_up, h_ref, g_ref, w_ref, down_ref, sems,
):
    step = pl.program_id(0)

    def tokens_in(j):
        rows = slice(ROWS * j, ROWS * j + ROWS)
        return (
            pltpu.make_async_copy((h0, h1, h2, h3)[j], h_ref.at[rows], sems.at[j]),
            pltpu.make_async_copy((g0, g1, g2, g3)[j], g_ref.at[rows], sems.at[4 + j]),
        )

    def weights_in():
        for j, w in enumerate((w0, w1, w2, w3)):
            yield pltpu.make_async_copy(w, w_ref.at[row_of(info[ME] ^ j)], sems.at[8 + j])
        yield pltpu.make_async_copy(d_ref, down_ref.at[:FFS], sems.at[12])

    @pl.when(step == 0)
    def _():
        first = [*tokens_in(0), *tokens_in(1)]
        weights = list(weights_in())
        for copy in (*first, *weights, *tokens_in(2), *tokens_in(3)):
            copy.start()
        down_ref[FFS:, :] = jnp.zeros((FFP - FFS, D), BF16)
        for copy in (*first, *weights):
            copy.wait()

    @pl.when(step == 1)
    def _():
        for copy in (*tokens_in(2), *tokens_in(3)):
            copy.wait()

    rows = pl.ds(pl.multiple_of(step * 512, 512), 512)
    h, g = h_ref[rows, :], g_ref[rows, :]
    gate = dot(h, w_ref[:, :FFP])
    up = dot(h, w_ref[:, FFP:])
    sig = jax.nn.sigmoid(gate)
    silu = gate * sig
    act = (silu * up).astype(BF16)
    act_ref[...] = act
    grad_act = dot_nt(g, down_ref[...])
    dgate = (grad_act * up * (sig * (1.0 + gate * (1.0 - sig)))).astype(BF16)
    dup = (grad_act * silu).astype(BF16)
    dgu_ref[:, :FFP] = dgate
    dgu_ref[:, FFP:] = dup
    gh = (dot_nt(dgate, w_ref[:, :FFP]) + dot_nt(dup, w_ref[:, FFP:])).astype(BF16)
    out = dot(act, down_ref[...]).astype(BF16)

    @pl.when(step == 0)
    def _():
        gh_low[...] = gh
        out_low[...] = out

    @pl.when(step == 1)
    def _():
        gh_up[...] = gh
        out_up[...] = out


def feed(info, hs, gs, ws, down):
    row = lambda i: (i, 0)
    fixed = lambda i: (0, 0)
    half = pl.BlockSpec((512, D), fixed)
    return call(
        feed_kernel,
        "feed",
        [SMEM] + [ANY] * 13,
        [shaped(D, FFP), shaped(D, 2 * FFP)] + [shaped(512, D)] * 4,
        (info, *hs, *gs, *ws, down),
        us=18,
        limit=56,
        grid=(2,),
        out_specs=[pl.BlockSpec((512, FFP), row), pl.BlockSpec((512, 2 * FFP), row)] + [half] * 4,
        scratch_shapes=[
            pltpu.VMEM((D, D), BF16),
            pltpu.VMEM((D, D), BF16),
            pltpu.VMEM((D, 2 * FFP), BF16),
            pltpu.VMEM((FFP, D), BF16),
            pltpu.SemaphoreType.DMA((13,)),
        ],
    )


def halve(info, step, rows_of, outs):
    for part in range(2):
        bit, outer, run = SPLITS[part][step]
        mine = info[BIT + bit]
        keep, away = outs[2 * part], outs[2 * part + 1]
        for o in range(outer):
            at = slice(o * run, o * run + run)
            keep[at, :] = rows_of(part, pl.ds(pl.multiple_of((2 * o + mine) * run, run), run))
            away[at, :] = rows_of(part, pl.ds(pl.multiple_of((2 * o + 1 - mine) * run, run), run))


def split_result(info, res_ref, outs):
    halve(info, 0, lambda part, at: res_ref[part, at, :], outs)


def mlp_weights_kernel(
    info, h0, h1, h2, h3, g0, g1, g2, g3, dgu_ref, act_ref, k1, s1, k2, s2, h_ref, g_ref, res_ref, sems
):
    step = pl.program_id(0)

    def copies(refs, into, first):
        return [
            pltpu.make_async_copy(r, into.at[ROWS * j : ROWS * j + ROWS], sems.at[first + j])
            for j, r in enumerate(refs)
        ]

    @pl.when(step == 0)
    def _():
        hs = copies((h0, h1, h2, h3), h_ref, 0)
        for copy in hs + copies((g0, g1, g2, g3), g_ref, 4):
            copy.start()
        for copy in hs:
            copy.wait()

    @pl.when(step == 2)
    def _():
        for copy in copies((g0, g1, g2, g3), g_ref, 4):
            copy.wait()

    for half in range(2):
        cols = slice(512 * half, 512 * half + 512)

        @pl.when(step < 2)
        def _():
            res_ref[half] = dot_tn(h_ref[:, cols], dgu_ref[...]).astype(BF16)

        @pl.when(step == 2)
        def _():
            res_ref[half] = dot_tn(g_ref[:, cols], act_ref[...]).astype(BF16)

    split_result(info, res_ref, (k1, s1, k2, s2))


def mlp_weights(info, hs, gs, dgu, act):
    col = lambda i: (0, i)
    return call(
        mlp_weights_kernel,
        "mlp_weights",
        [SMEM]
        + [ANY] * 8
        + [pl.BlockSpec((D, FFP), lambda i: (0, jnp.minimum(i, 1))), pl.BlockSpec((D, FFP), lambda i: (0, 0))],
        [shaped(256, 3 * FFP)] * 4,
        (info, *hs, *gs, dgu, act),
        us=10,
        grid=(3,),
        out_specs=[pl.BlockSpec((256, FFP), col)] * 4,
        scratch_shapes=[
            pltpu.VMEM((D, D), BF16),
            pltpu.VMEM((D, D), BF16),
            pltpu.VMEM((2, 512, FFP), BF16),
            pltpu.SemaphoreType.DMA((8,)),
        ],
    )


EX = 128
ATT = 768 + EX + 256


def attn_weights_kernel(
    info, h_ref, d0, d1, m_ref, b0, b1, b2, b3, sa_ref, sm_ref,
    k1, s1, k2, s2, b_ref, d_ref, ex_ref, res_ref, sems,
):
    me = info[ME]
    copies = [
        pltpu.make_async_copy(r, b_ref.at[ROWS * j : ROWS * j + ROWS], sems.at[j])
        for j, r in enumerate((b0, b1, b2, b3))
    ]
    for copy in copies:
        copy.start()
    d_ref[...] = whole(d0[...], d1[...])
    ex_ref[...] = jnp.zeros_like(ex_ref)
    ex_ref[0:2, :] = sa_ref[...]
    ex_ref[2:4, :] = sm_ref[...]
    db = dot(jnp.ones((8, D), BF16), d_ref[...])[0:1, :]
    for c in range(3):
        one = db[:, 256 * c : 256 * c + 256]
        ex_ref[pl.ds(8 + 4 * c + me, 1), :] = jnp.concatenate([one] * GROUP, axis=1)
    ex = ex_ref[...].T.astype(BF16)
    for half in range(2):
        rows = slice(512 * half, 512 * half + 512)
        res_ref[half, :, :768] = dot_tn(h_ref[:, rows], d_ref[...]).astype(BF16)
        res_ref[half, :, 768 : 768 + EX] = ex[rows, :]
    for copy in copies:
        copy.wait()
    for half in range(2):
        res_ref[half, :, 768 + EX :] = dot_tn(b_ref[:, 512 * half : 512 * half + 512], m_ref[...]).astype(BF16)
    split_result(info, res_ref, (k1, s1, k2, s2))


def attn_weights(info, hidden, dqkvs, mixed, branch, sums_a, sums_m):
    return call(
        attn_weights_kernel,
        "attn_weights",
        [SMEM] + [VMEM] * 4 + [ANY] * 4 + [VMEM] * 2,
        [shaped(256, ATT)] * 4,
        (info, hidden, *dqkvs, mixed, *branch, sums_a, sums_m),
        us=5,
        scratch_shapes=[
            pltpu.VMEM((D, D), BF16),
            pltpu.VMEM((D, 768), BF16),
            pltpu.VMEM((EX, D), F32),
            pltpu.VMEM((2, 512, ATT), BF16),
            pltpu.SemaphoreType.DMA((4,)),
        ],
    )


def add(a, b):
    return (a.astype(F32) + b.astype(F32)).astype(BF16)


def halve_kernel(step, info, a1, g1, a2, g2, *outs):
    ins = ((a1, g1), (a2, g2))
    halve(info, step, lambda part, at: add(ins[part][0][at, :], ins[part][1][at, :]), outs)


def piece_kernel(a1, g1, a2, g2, out):
    out[:32, :] = add(a1[...], g1[...])
    out[32:, :] = add(a2[...], g2[...])


def share_kernel(cols, info, a_ref, g_ref, o0, o1, o2, o3, kept):
    width = a_ref.shape[1] - cols
    for j, out in enumerate((o0, o1, o2, o3)):
        rows = row_of(info[ME] ^ j, 16)
        out[...] = add(a_ref[rows, :cols], g_ref[rows, :cols])
    for t in range(GROUP):
        rows = slice(16 * t, 16 * t + 16)
        kept[:, width * t : width * t + width] = add(a_ref[rows, cols:], g_ref[rows, cols:])


def scatter_plane(info, first, name, gates):
    k1, s1, k2, s2 = first
    width = k1.shape[1]
    s1 = after(s1, *gates[0])
    s2 = after(s2, *gates[0])
    for step in range(4):
        got1 = send(s1, CUBE[SPLITS[0][step][0]])
        got2 = send(s2, CUBE[SPLITS[1][step][0]])
        operands = (after(k1, *gates[step + 1]), got1, k2, got2)
        if step == 3:
            return call(piece_kernel, "piece_" + name, [VMEM] * 4, shaped(64, width), operands, limit=24)
        rows = k1.shape[0] // 2
        k1, s1, k2, s2 = call(
            functools.partial(halve_kernel, step + 1),
            "halve_" + name,
            [SMEM] + [VMEM] * 4,
            [shaped(rows, width)] * 4,
            (info, *operands),
            limit=24,
        )


def share(info, piece, cols, name, gate=()):
    width = piece.shape[1]
    *blocks, kept = call(
        functools.partial(share_kernel, cols),
        "share_" + name,
        [SMEM] + [VMEM] * 2,
        [shaped(16, cols)] * 4 + [shaped(16, GROUP * (width - cols))],
        (info, after(piece, *gate), send(piece, ZREPLICA)),
        limit=16,
    )
    perms = (None, SIBLING_T, ZNEAR, ZNEAR_SIBLING_T)
    return [b if p is None else send(b, p) for b, p in zip(blocks, perms)], kept


def join_mlp_kernel(info, r0, r1, r2, r3, kept, out):
    for j, r in enumerate((r0, r1, r2, r3)):
        s = info[ME] ^ j
        out[:, lanes_of(s * FFP, FFP)] = r[:, :FFP]
        out[:, lanes_of((GROUP + s) * FFP, FFP)] = r[:, FFP:]
    out[:, 2 * GROUP * FFP :] = kept[...]


def join_attn_kernel(info, r0, r1, r2, r3, kept, one, two):
    refs = (r0, r1, r2, r3)
    for j, r in enumerate(refs):
        s = info[ME] ^ j
        one[:, lanes_of(s * 256, 256)] = r[:, :256]
        one[:, lanes_of(D + s * 256, 256)] = r[:, 256:512]
        two[:, lanes_of(s * 256, 256)] = r[:, 512:768]
    two[:, D : D + EX] = sum(r[:, 768:].astype(F32) for r in refs).astype(BF16)
    two[:, D + EX :] = kept[...]


def finish_mlp_kernel(info, all_ref, gu_ref, down_ref, turn_ref):
    for n, piece in enumerate(PIECES):
        turned = 4 * (n % 4) + n // 4
        at = row_of(jnp.where(info[ME] % 2 == 0, n, turned), 16)
        to = slice(16 * piece, 16 * piece + 16)
        for s in range(GROUP):
            for c in range(2):
                lo = (GROUP * c + s) * FFP
                gu_ref[to, FF * c + FFS * s : FF * c + FFS * s + FFS] = all_ref[at, lo : lo + FFS].astype(F32)
        turn_ref[to, :] = all_ref[at, 2 * GROUP * FFP :].astype(F32)
    for t in range(GROUP):
        down_ref[:, 256 * t : 256 * t + 256] = turn_ref[:, FFP * t : FFP * t + FFP].T[:FFS, :]


def finish_attn_kernel(info, a1, g1, a2, g2, qkv_ref, out_ref, vec_ref, turn_ref, ex_ref):
    q = info[BIT] * 8 + info[BIT + 1] * 4 + info[BIT + 2] * 2 + info[BIT + 3]
    for piece in range(16):
        d = q ^ piece
        e = ((d >> 2) & 1) * 8 + ((d >> 3) & 1) * 4 + (d & 1) * 2 + ((d >> 1) & 1)
        to = slice(16 * piece, 16 * piece + 16)
        for own, got, slot, one in ((a1, g1, d, True), (a2, g2, e, False)):
            at = row_of(slot & 7, 16)
            v = jnp.where(slot >= 8, got[at, :].astype(F32), own[at, :].astype(F32))
            if one:
                qkv_ref[to, : 2 * D] = v
            else:
                qkv_ref[to, 2 * D :] = v[:, :D]
                ex_ref[to, :] = v[:, D : D + EX]
                turn_ref[to, :] = v[:, D + EX :]
    for t in range(GROUP):
        out_ref[:, 256 * t : 256 * t + 256] = turn_ref[:, 256 * t : 256 * t + 256].T
    vec_ref[...] = ex_ref[...].T


def gather_plane(parts):
    for step in (3, 2, 1, 0):
        got = [send(p, CUBE[SPLITS[i][step][0]]) for i, p in enumerate(parts)]
        if step == 0:
            return parts[0], got[0], parts[1], got[1]
        parts = [jnp.concatenate([p, g], axis=0) for p, g in zip(parts, got)]


def after(value, *earlier):
    return lax.optimization_barrier((value, *earlier))[0]


def body(
    tokens,
    attn_norm_gain,
    attn_norm_shift,
    qkv_weight,
    qkv_bias,
    out_weight,
    mlp_norm_gain,
    mlp_norm_shift,
    gate_up_weight,
    down_weight,
    cotangent,
):
    me = lax.axis_index("fsdp")
    rank = lax.axis_index("dp")
    x, y = (rank // 4) % 4, rank % 4
    first = jnp.where(me % 2 == 0, x, y)
    second = jnp.where(me % 2 == 0, y, x)
    info = jnp.stack(
        [me]
        + [2 * ((n ^ me) % 2) + (n ^ me) // 2 for n in range(GROUP)]
        + [((first + 1) // 2) % 2, first // 2, ((second + 1) // 2) % 2, second // 2]
    ).astype(jnp.int32)
    near = send(tokens, ZNEAR)
    sibling = send(tokens, SIBLING)
    qkv_parts = pick_qkv(info, qkv_weight)
    far = (None, SIBLING, ZFAR, ZFAR_SIBLING)
    qkv_ws = [b if p is None else send(b, p) for b, p in zip(qkv_parts, far)]
    vs = gather_group(
        pack(attn_norm_gain, attn_norm_shift, mlp_norm_gain, mlp_norm_shift, after(qkv_bias, qkv_parts[0]))
    )
    cos, sin = tables(info)
    gate_up_parts = pick_gate_up(info, after(gate_up_weight, vs[0]))
    near = after(near, cos, gate_up_parts[0])
    xs = (tokens, near, sibling, send(near, SIBLING))
    gate_up_ws = [
        gate_up_parts[0],
        send(after(gate_up_parts[1], near), SIBLING),
        send(after(gate_up_parts[2], *qkv_ws[2:]), ZFAR),
        send(after(gate_up_parts[3], near), ZNEAR_SIBLING),
    ]

    hidden, qkv, qkv_w, norms = project(info, xs, vs, qkv_ws, cos, sin)
    mixed, lse, low, up = attend(info, qkv, out_weight)
    gs = gather_group(after(cotangent, gate_up_ws[3]))
    own, near = scatter_group(low, up)
    near = after(near, gate_up_ws[2], gs[1])
    mid, hid_own = middle_of(tokens, own, send(near, ZNEAR), norms)
    hs = gather_group(hid_own)
    act, dgu, gh_low, gh_up, out_low, out_up = feed(info, hs, gs, gate_up_ws, down_weight)

    gh_own, gh_near = scatter_group(gh_low, gh_up)
    mlp_halves = mlp_weights(info, hs, gs, after(dgu, gh_near), act)
    grad_mid, branch_own, sums_m = norm_back(gh_own, send(gh_near, ZNEAR), mid, cotangent, norms, 2)
    branch = gather_group(branch_own)

    dqkv0 = attend_back(0, info, qkv, branch, out_weight, lse, cos, sin)
    dqkv1 = attend_back(1, after(info, dqkv0), qkv, branch, out_weight, lse, cos, sin)
    dqkvs = (dqkv0, dqkv1)
    ga_low, ga_up, sums_a = hidden_back(dqkvs, qkv_w, xs)
    attn_halves = attn_weights(info, hidden, dqkvs, mixed, branch, after(sums_a, ga_low), sums_m)

    mlp_gates = ((branch_own,), (branch[1],), (dqkv0,), (dqkv1,), (ga_low,))
    mlp_piece = scatter_plane(info, mlp_halves, "mlp", mlp_gates)
    mlp_blocks, mlp_kept = share(info, mlp_piece, 2 * FFP, "mlp", (attn_halves[0],))
    mlp_piece = call(
        join_mlp_kernel,
        "join_mlp",
        [SMEM] + [VMEM] * 5,
        shaped(16, 3 * GROUP * FFP),
        (info, *mlp_blocks, mlp_kept),
        limit=16,
    )
    mlp_all = lax.all_gather(mlp_piece, AXES, axis=0, axis_index_groups=PLANES, tiled=True)

    o_own, o_near = scatter_group(out_low, after(out_up, gh_near))
    ga_own, ga_near = scatter_group(ga_low, ga_up)
    ga_other = send(after(ga_near, attn_halves[0]), ZNEAR)
    o_other = send(after(o_near, attn_halves[0]), ZNEAR)
    attn_gates = ((), (mlp_piece,), (), (ga_other,), (o_other,))
    attn_piece = scatter_plane(info, attn_halves, "attn", attn_gates)
    attn_blocks, attn_kept = share(info, attn_piece, 768 + EX, "attn")
    pieces = call(
        join_attn_kernel,
        "join_attn",
        [SMEM] + [VMEM] * 5,
        [shaped(16, 2 * D), shaped(16, 2 * D + EX)],
        (info, *attn_blocks, attn_kept),
        limit=16,
    )
    (tokens_grad,) = norm_back(ga_own, ga_other, tokens, grad_mid, norms, 0)
    layer_out = layer_out_of(mid, o_own, o_other)

    grad_gate_up, grad_down = call(
        finish_mlp_kernel,
        "finish_mlp",
        [SMEM, VMEM],
        [shaped(ROWS, 2 * FF, dtype=F32), shaped(FFS, D, dtype=F32)],
        (info, mlp_all),
        us=5,
        scratch_shapes=[pltpu.VMEM((ROWS, GROUP * FFP), F32)],
    )
    grad_qkv, grad_out, vec = call(
        finish_attn_kernel,
        "finish_attn",
        [SMEM] + [VMEM] * 4,
        [shaped(ROWS, 3 * D, dtype=F32), shaped(256, D, dtype=F32), shaped(EX, ROWS, dtype=F32)],
        (after(info, grad_down), *gather_plane(pieces)),
        us=4,
        scratch_shapes=[pltpu.VMEM((ROWS, D), F32), pltpu.VMEM((ROWS, EX), F32)],
    )
    grad_bias = lax.dynamic_slice_in_dim(vec[8:20].reshape(3 * D), 768 * me, 768, 0)
    return (
        layer_out,
        tokens_grad,
        vec[0],
        vec[1],
        grad_qkv,
        grad_bias,
        grad_out,
        vec[2],
        vec[3],
        grad_gate_up,
        grad_down,
    )


def solution(mesh):
    rows = P(("dp", "fsdp"), None)
    vector = P("fsdp")
    matrix = P("fsdp", None)
    in_specs = (rows, vector, vector, matrix, vector, matrix, vector, vector, matrix, matrix, rows)
    out_specs = (rows, rows, vector, vector, matrix, vector, matrix, vector, vector, matrix, matrix)
    return jax.shard_map(body, mesh=mesh, in_specs=in_specs, out_specs=out_specs, check_vma=False)
```

time: 1140 us -> 337 us (0.30)
  waiting for transfers between devices: 808 us -> 130 us
  blocking collectives: 133 us -> 0 us
  matrix products: 115 us -> 0 us
  Pallas kernels: 0 us -> 92.6 us
  starting transfers between devices: 0.78 us -> 68.3 us
  other arithmetic: 37.3 us -> 0.07 us
    reduce_scatter x6 -> x0, waiting for transfers between devices: 284 us -> none  [the longest x1 108 us: body(): lax.psum_scatter(grad_terms[2].astype(jnp.bfloat16), 'fsdp', scatter_dime...]
    all_gather x6 -> x1, waiting for transfers between devices: 264 us -> 0.01 us  [body(): lax.all_gather(mlp_piece, AXES, axis=0, axis_index_groups=PLANES, tiled=T...]
    psum x1 -> x0, waiting for transfers between devices: 257 us -> none  [body(): lax.psum(owned_grads[0].astype(jnp.bfloat16), 'dp').astype(jnp.float32)]
    ppermute x0 -> x61, waiting for transfers between devices: none -> 130 us  [send(): return lax.ppermute(value, AXES, perm)]
    dot_general x18 -> x0, matrix products: 115 us -> none  [the longest x4 24 us: contract_cols(): lax.dot_general(former, latter, (((1,), (1,)), ((), ())), preferred_eleme...]
    psum x1 -> x0, blocking collectives: 95.9 us -> none  [body(): lax.psum(owned_grads[4].astype(jnp.bfloat16), 'dp').astype(jnp.float32)]
    pallas_call x0 -> x34, Pallas kernels: none -> 92.6 us  [call(): pl.pallas_call(kernel, in_specs=in_specs, out_shape=out_shape, compiler_p...]
    ppermute x0 -> x61, starting transfers between devices: none -> 68.2 us  [send(): return lax.ppermute(value, AXES, perm)]
  transfers between devices with their start and end apart: 13 -> 62, of which waited for: 13 -> 33; matrix products, arithmetic and copies ran while one was open for 9% -> 2% of each run, Pallas kernels for 0% -> 20%
where the time goes in v1:
time: 337 us; the launch traced here: 332 us
  waiting for transfers between devices  130 us (39%)
  Pallas kernels  92.6 us (27%)
  starting transfers between devices  68.3 us (20%)
  local copies, waits for them, and re-layouts  25.6 us (8%)
  between operations  15.5 us (5%)
    ppermute x61, waiting for transfers between devices, send(): return lax.ppermute(value, AXES, perm)  130 us
    pallas_call x34, Pallas kernels, call(): pl.pallas_call(kernel, in_specs=in_specs, out_shape=out_shape, compiler_p...  92.6 us
    ppermute x61, starting transfers between devices, send(): return lax.ppermute(value, AXES, perm)  68.2 us
    unnamed x138, local copies, waits for them, and re-layouts  22.8 us
  transfers between devices with their start and end apart: 62, of which 33 were waited for; matrix products, arithmetic and copies ran while one was open for 2% of the time, Pallas kernels for 20%

profile of v1, /device:TPU:0, one launch (start us, length us, event | category | flops | bytes accessed | tf_op | source)
XLA Modules:
  0.0 332.0 jit_solution(8907007407057360199)
XLA Ops:
  7.2 2.1 collective-permute-start
  12.2 2.5 tables.1
  14.8 1.8 copy-done
  18.9 2.6 collective-permute-done.x1
  21.4 1.7 collective-permute-start.3
  23.4 1.9 collective-permute-done.3.v1
  25.4 3.9 %collective-permute-start.7 = (bf16[256,768]{1,0:T(8,128)(2,1)S(1)}, bf16[256,768]{1,0:T(8,128)(2,1)S(1)}, u32[]{:S(2)}, u32[]{:S(2)}) collective-permute-start(bf16[256,768]{1,0:T(8,128)(2,1)S(1)} %get-tuple-element.132), channel_id=1, source_target_pairs={{0,66},{1,67},{2,64},{3,65},{4,70},{5,71},{6,68},{7,69},{8,74},{9,... | collective-permute-start | bytes 1179656 | tf_op jit(solution)/shard_map/ppermute | solution.py:94
  30.4 8.8 %collective-permute-done.7.w2 = bf16[256,768]{1,0:T(8,128)(2,1)S(1)} collective-permute-done((bf16[256,768]{1,0:T(8,128)(2,1)S(1)}, bf16[256,768]{1,0:T(8,128)(2,1)S(1)}, u32[]{:S(2)}, u32[]{:S(2)}) %collective-permute-start.7) | collective-permute-done | bytes 393248 | tf_op jit(solution)/shard_map/ppermute | solution.py:94
  39.2 8.1 %collective-permute-done.8.w3 = bf16[256,768]{1,0:T(8,128)(2,1)S(1)} collective-permute-done((bf16[256,768]{1,0:T(8,128)(2,1)S(1)}, bf16[256,768]{1,0:T(8,128)(2,1)S(1)}, u32[]{:S(2)}, u32[]{:S(2)}) %collective-permute-start.8) | collective-permute-done | bytes 393248 | tf_op jit(solution)/shard_map/ppermute | solution.py:94
  47.3 5.9 %project.1 = (bf16[1024,1024]{1,0:T(8,128)(2,1)}, bf16[1024,768]{1,0:T(8,128)(2,1)}, bf16[1024,768]{1,0:T(8,128)(2,1)}, f32[8,1024]{1,0:T(8,128)S(1)}) custom-call(s32[9]{0:T(128)S(1)} %stack.39.info, bf16[256,1024]{1,0:T(8,128)(2,1)S(1)} %copy-done.1, bf16[256,1024]{1,0:T(8,128)(2,1)S(1)} %collective-permute-done.x1, ...), custom_call_target="tpu_custom_call" | custom-call | tf_op jit(solution)/shard_map/project/pallas_call | solution.py:119
  54.6 7.8 %attend.1 = (bf16[1024,256]{1,0:T(8,128)(2,1)S(1)}, f32[2,2,1024]{2,1,0:T(2,128)S(1)}, bf16[512,1024]{1,0:T(8,128)(2,1)S(1)}, bf16[512,1024]{1,0:T(8,128)(2,1)S(1)}) custom-call(s32[9]{0:T(128)S(1)} %stack.39.info, bf16[1024,768]{1,0:T(8,128)(2,1)S(1)} %copy-done.3, bf16[256,1024]{1,0:T(8,128)(2,1)S(1)} %copy-done.6), custom_call_target="tpu_custom_call" | custom-call | tf_op jit(solution)/shard_map/attend/pallas_call | solution.py:119
  63.2 2.8 collective-permute-start.10
  67.0 17.4 %collective-permute-done.10.w2 = bf16[256,1536]{1,0:T(8,128)(2,1)S(1)} collective-permute-done((bf16[256,1536]{1,0:T(8,128)(2,1)S(1)}, bf16[256,1536]{1,0:T(8,128)(2,1)S(1)}, u32[]{:S(2)}, u32[]{:S(2)}) %collective-permute-start.10) | collective-permute-done | bytes 786464 | tf_op jit(solution)/shard_map/ppermute | solution.py:94
  84.4 13.5 %collective-permute-done.13.other_ref = bf16[256,1024]{1,0:T(8,128)(2,1)S(1)} collective-permute-done((bf16[256,1024]{1,0:T(8,128)(2,1)S(1)}, bf16[256,1024]{1,0:T(8,128)(2,1)S(1)}, u32[]{:S(2)}, u32[]{:S(2)}) %collective-permute-start.13) | collective-permute-done | bytes 524320 | tf_op jit(solution)/shard_map/ppermute | solution.py:94
  100.6 11.3 %collective-permute-done.14.h1 = bf16[256,1024]{1,0:T(8,128)(2,1)S(1)} collective-permute-done((bf16[256,1024]{1,0:T(8,128)(2,1)S(1)}, bf16[256,1024]{1,0:T(8,128)(2,1)S(1)}, u32[]{:S(2)}, u32[]{:S(2)}) %collective-permute-start.14) | collective-permute-done | bytes 524320 | tf_op jit(solution)/shard_map/ppermute | solution.py:94
  114.3 18.3 %feed.1 = (bf16[1024,768]{1,0:T(8,128)(2,1)}, bf16[1024,1536]{1,0:T(8,128)(2,1)}, bf16[512,1024]{1,0:T(8,128)(2,1)}, bf16[512,1024]{1,0:T(8,128)(2,1)}, bf16[512...) custom-call(s32[9]{0:T(128)} %copy-done.7, bf16[256,1024]{1,0:T(8,128)(2,1)} %copy-done.30, bf16[256,1024]{1,0:T(8,128)(2,1)} %copy-done.32, ...), custom_call_target="tpu_custom_call" | custom-call | flops 17999998976 | bytes 18874368 | tf_op jit(solution)/shard_map/feed/pallas_call | solution.py:119
  132.8 2.7 collective-permute-done.20.got_ref
  138.8 11.2 %mlp_weights.1 = (bf16[256,2304]{1,0:T(8,128)(2,1)S(1)}, bf16[256,2304]{1,0:T(8,128)(2,1)}, bf16[256,2304]{1,0:T(8,128)(2,1)}, bf16[256,2304]{1,0:T(8,128)(2,1)}) custom-call(s32[9]{0:T(128)S(1)} %copy-done.8, bf16[256,1024]{1,0:T(8,128)(2,1)S(1)} %copy-done.31, bf16[256,1024]{1,0:T(8,128)(2,1)S(1)} %copy-done.33, bf16[256,1024]{1,0:T(8,128)(2,1)S(1)} %copy-done.39, ...), custom_call_target="tpu_custom_call" | custom-call | flops 10000000000 | bytes 10485760 | tf_op jit(solution)/shard_map/mlp_weights/pallas_call | solution.py:119
  153.9 2.1 collective-permute-start.30
  156.6 12.1 %collective-permute-done.23.b1 = bf16[256,1024]{1,0:T(8,128)(2,1)S(1)} collective-permute-done((bf16[256,1024]{1,0:T(8,128)(2,1)S(1)}, bf16[256,1024]{1,0:T(8,128)(2,1)S(1)}, u32[]{:S(2)}, u32[]{:S(2)}) %collective-permute-start.23) | collective-permute-done | bytes 524320 | tf_op jit(solution)/shard_map/ppermute | solution.py:94
  168.9 2.4 collective-permute-done.30.g2
  172.4 2.2 collective-permute-start.31
  176.5 7.2 %attend_back.2.d0 = bf16[1024,384]{1,0:T(8,128)(2,1)S(1)} custom-call(s32[9]{0:T(128)S(1)} %copy-done.8, bf16[1024,768]{1,0:T(8,128)(2,1)S(1)} %copy-done.4, bf16[256,1024]{1,0:T(8,128)(2,1)S(1)} %get-tuple-element.161.b0, bf16[256,1024]{1,0:T(8,128)(2,1)S(1)} %collective-permute-done.23.b1, bf16[256,1024]{1,0:T(8,128)(2,1)S(1)} %collective-permute-done.24.b2, ...), custom_call_target="tpu_custom_call" | custom-call | flops 7000000000 | bytes 7340032 | tf_op jit(solution)/shard_map/attend_back/pallas_call | solution.py:119
  185.3 1.7 collective-permute-start.33
  187.0 2.5 collective-permute-start.34
  189.5 7.2 %attend_back.3.d1 = bf16[1024,384]{1,0:T(8,128)(2,1)S(1)} custom-call(s32[9]{0:T(128)S(1)} %copy-done.8, bf16[1024,768]{1,0:T(8,128)(2,1)S(1)} %copy-done.4, bf16[256,1024]{1,0:T(8,128)(2,1)S(1)} %get-tuple-element.161.b0, bf16[256,1024]{1,0:T(8,128)(2,1)S(1)} %collective-permute-done.23.b1, bf16[256,1024]{1,0:T(8,128)(2,1)S(1)} %copy-done.22, ...), custom_call_target="tpu_custom_call" | custom-call | flops 7000000000 | bytes 7340032 | tf_op jit(solution)/shard_map/attend_back/pallas_call | solution.py:119
  198.9 3.9 %hidden_back.1 = (bf16[512,1024]{1,0:T(8,128)(2,1)S(1)}, bf16[512,1024]{1,0:T(8,128)(2,1)S(1)}, f32[2,1024]{1,0:T(2,128)S(1)}) custom-call(bf16[1024,384]{1,0:T(8,128)(2,1)S(1)} %attend_back.2.d0, bf16[1024,384]{1,0:T(8,128)(2,1)S(1)} %attend_back.3.d1, bf16[1024,768]{1,0:T(8,128)(2,1)} %get-tuple-element.165.w_ref, bf16[256,1024]{1,0:T(8,128)(2,1)S(1)} %copy-done.1, ...), custom_call_target="tpu_custom_call" | custom-call | flops 5000000000 | bytes 5242880 | tf_op jit(solution)/shard_map/hidden_back/pallas_call | solution.py:119
  203.9 2.8 collective-permute-start.37
  206.8 5.0 %attn_weights.1 = (bf16[256,1152]{1,0:T(8,128)(2,1)S(1)}, bf16[256,1152]{1,0:T(8,128)(2,1)S(1)}, bf16[256,1152]{1,0:T(8,128)(2,1)S(1)}, bf16[256,1152]{1,0:T(8,128)(2,1)S(1)}) custom-call(s32[9]{0:T(128)S(1)} %copy-done.8, bf16[1024,1024]{1,0:T(8,128)(2,1)} %get-tuple-element.159.h_ref, bf16[1024,384]{1,0:T(8,128)(2,1)S(1)} %copy-done.54, ...), custom_call_target="tpu_custom_call" | custom-call | flops 5000000000 | bytes 5242880 | tf_op jit(solution)/shard_map/attn_weights/pallas_call | solution.py:119
  215.1 2.8 collective-permute-done.39.r2
  219.9 3.4 %collective-permute-start.41 = (bf16[256,1152]{1,0:T(8,128)(2,1)}, bf16[256,1152]{1,0:T(8,128)(2,1)S(1)}, u32[]{:S(2)}, u32[]{:S(2)}) collective-permute-start(bf16[256,1152]{1,0:T(8,128)(2,1)} %copy-done.12), channel_id=1, source_target_pairs={{0,16},{1,5},{2,18},{3,7},{4,20},{5,1},{6,22},{7,3},{8,24},{9,13},... | collective-permute-start | bytes 1769480 | tf_op jit(solution)/shard_map/ppermute | solution.py:94
  223.3 6.8 %collective-permute-start.42 = (bf16[256,1152]{1,0:T(8,128)(2,1)}, bf16[256,1152]{1,0:T(8,128)(2,1)S(1)}, u32[]{:S(2)}, u32[]{:S(2)}) collective-permute-start(bf16[256,1152]{1,0:T(8,128)(2,1)} %copy-done.11), channel_id=1, source_target_pairs={{0,48},{1,13},{2,50},{3,15},{4,52},{5,9},{6,54},{7,11},{8,56},{9,5... | collective-permute-start | bytes 1769480 | tf_op jit(solution)/shard_map/ppermute | solution.py:94
  231.3 8.1 %collective-permute-done.42.g2 = bf16[256,1152]{1,0:T(8,128)(2,1)S(1)} collective-permute-done((bf16[256,1152]{1,0:T(8,128)(2,1)}, bf16[256,1152]{1,0:T(8,128)(2,1)S(1)}, u32[]{:S(2)}, u32[]{:S(2)}) %collective-permute-start.42) | collective-permute-done | bytes 589856 | tf_op jit(solution)/shard_map/ppermute | solution.py:94
  242.4 3.7 %collective-permute-start.43 = (bf16[128,1152]{1,0:T(8,128)(2,1)S(1)}, bf16[128,1152]{1,0:T(8,128)(2,1)S(1)}, u32[]{:S(2)}, u32[]{:S(2)}) collective-permute-start(bf16[128,1152]{1,0:T(8,128)(2,1)S(1)} %get-tuple-element.215), channel_id=1, source_target_pairs={{0,48},{1,13},{2,50},{3,15},{4,52},{5,9},{6,54},{7,11},{8,56},{9,5... | collective-permute-start | bytes 884744 | tf_op jit(solution)/shard_map/ppermute | solution.py:94
  253.6 7.6 %collective-permute-done.28.other_ref = bf16[256,1024]{1,0:T(8,128)(2,1)S(1)} collective-permute-done((bf16[256,1024]{1,0:T(8,128)(2,1)S(1)}, bf16[256,1024]{1,0:T(8,128)(2,1)S(1)}, u32[]{:S(2)}, u32[]{:S(2)}) %collective-permute-start.28) | collective-permute-done | bytes 524320 | tf_op jit(solution)/shard_map/ppermute | solution.py:94
  262.0 5.5 %collective-permute-done.26.other_ref = bf16[256,1024]{1,0:T(8,128)(2,1)S(1)} collective-permute-done((bf16[256,1024]{1,0:T(8,128)(2,1)S(1)}, bf16[256,1024]{1,0:T(8,128)(2,1)S(1)}, u32[]{:S(2)}, u32[]{:S(2)}) %collective-permute-start.26) | collective-permute-done | bytes 524320 | tf_op jit(solution)/shard_map/ppermute | solution.py:94
  269.1 3.4 %collective-permute-start.49 = (bf16[64,1152]{1,0:T(8,128)(2,1)S(1)}, bf16[64,1152]{1,0:T(8,128)(2,1)S(1)}, u32[]{:S(2)}, u32[]{:S(2)}) collective-permute-start(bf16[64,1152]{1,0:T(8,128)(2,1)S(1)} %piece_attn.1.a_ref), channel_id=1, source_target_pairs={{0,64},{1,65},{2,66},{3,67},{4,68},{5,69},{6,70},{7,71},{8,72},{9,... | collective-permute-start | bytes 442376 | tf_op jit(solution)/shard_map/ppermute | solution.py:94
  272.5 3.3 collective-permute-done.49.g_ref
  281.8 6.4 %collective-permute-start.53 = (bf16[16,2048]{1,0:T(8,128)(2,1)S(1)}, bf16[16,2048]{1,0:T(8,128)(2,1)S(1)}, u32[]{:S(2)}, u32[]{:S(2)}) collective-permute-start(bf16[16,2048]{1,0:T(8,128)(2,1)S(1)} %get-tuple-element.233), channel_id=1, source_target_pairs={{0,12},{1,49},{2,14},{3,51},{4,8},{5,53},{6,10},{7,55},{8,4},{9,57... | collective-permute-start | bytes 196616 | tf_op jit(solution)/shard_map/ppermute | solution.py:94
  295.5 2.0 collective-permute-start.55
  298.1 2.0 collective-permute-done.58
  300.2 2.6 collective-permute-start.59
  304.6 2.8 collective-permute-done.59
  308.4 1.8 norm_back.3
  310.1 2.3 copy-done.9
  312.5 5.0 %finish_mlp.1 = (f32[256,5632]{1,0:T(8,128)}, f32[704,1024]{1,0:T(8,128)}) custom-call(s32[9]{0:T(128)S(1)} %copy-done.8, bf16[256,9216]{1,0:T(8,128)(2,1)S(1)} %copy-done.9), custom_call_target="tpu_custom_call" | custom-call | flops 5000000000 | bytes 5242880 | tf_op jit(solution)/shard_map/finish_mlp/pallas_call | solution.py:119
  317.5 1.9 collective-permute-done.60.g2
  319.4 4.0 %finish_attn.1 = (f32[256,3072]{1,0:T(8,128)}, f32[256,1024]{1,0:T(8,128)}, f32[128,256]{1,0:T(8,128)S(1)}) custom-call(s32[9]{0:T(128)S(1)} %copy-done.8, bf16[128,2048]{1,0:T(8,128)(2,1)} %constant_dynamic-update-slice_fusion.a1, bf16[128,2048]{1,0:T(8,128)(2,1)} %collective-permute-done.56.g1, bf16[128,2176]{1,0:T(8,128)(2,1)} %constant_dynamic-update-slice_fusion.4.a2, ...), custom_call_target="tpu_custom_call" | custom-call | flops 4000000000 | bytes 4194304 | tf_op jit(solution)/shard_map/finish_attn/pallas_call | solution.py:119
  (265 shorter events, 68.1 us)
Async XLA Ops:
  7.2 302.9 %all-gather.2.cloned.1.call-start = ((), (), s32[]{:S(2)}) async-start(), calls=%async_computation | async-start | bytes 5013504 | tf_op jit(solution)/shard_map/all_gather | solution.py:918
  7.2 14.2 %collective-permute-start = (bf16[256,1024]{1,0:T(8,128)(2,1)}, bf16[256,1024]{1,0:T(8,128)(2,1)S(1)}, u32[]{:S(2)}, u32[]{:S(2)}) collective-permute-start(bf16[256,1024]{1,0:T(8,128)(2,1)} %base_ref.1), channel_id=1, source_target_pairs={{0,2},{1,3},{2,0},{3,1},{4,6},{5,7},{6,4},{7,5},{8,10},{9,11},{10,... | collective-permute-start | bytes 1572872 | tf_op jit(solution)/shard_map/ppermute | solution.py:94
  11.6 18.6 %collective-permute-start.6 = (bf16[256,768]{1,0:T(8,128)(2,1)S(1)}, bf16[256,768]{1,0:T(8,128)(2,1)S(1)}, u32[]{:S(2)}, u32[]{:S(2)}) collective-permute-start(bf16[256,768]{1,0:T(8,128)(2,1)S(1)} %get-tuple-element.131), channel_id=1, source_target_pairs={{0,1},{1,0},{2,3},{3,2},{4,5},{5,4},{6,7},{7,6},{8,9},{9,8},{10,11... | collective-permute-start | bytes 1179656 | tf_op jit(solution)/shard_map/ppermute | solution.py:94
  11.7 35.6 %collective-permute-start.1 = (bf16[256,1024]{1,0:T(8,128)(2,1)S(1)}, bf16[256,1024]{1,0:T(8,128)(2,1)S(1)}, u32[]{:S(2)}, u32[]{:S(2)}) collective-permute-start(bf16[256,1024]{1,0:T(8,128)(2,1)S(1)} %copy-done.1), channel_id=1, source_target_pairs={{0,1},{1,0},{2,3},{3,2},{4,5},{5,4},{6,7},{7,6},{8,9},{9,8},{10,11... | collective-permute-start | bytes 1572872 | tf_op jit(solution)/shard_map/ppermute | solution.py:94
  21.4 25.8 %collective-permute-start.2 = (bf16[256,1024]{1,0:T(8,128)(2,1)S(1)}, bf16[256,1024]{1,0:T(8,128)(2,1)S(1)}, u32[]{:S(2)}, u32[]{:S(2)}) collective-permute-start(bf16[256,1024]{1,0:T(8,128)(2,1)S(1)} %collective-permute-done.x1), channel_id=1, source_target_pairs={{0,1},{1,0},{2,3},{3,2},{4,5},{5,4},{6,7},{7,6},{8,9},{9,8},{10,11... | collective-permute-start | bytes 1572872 | tf_op jit(solution)/shard_map/ppermute | solution.py:94
  25.4 13.8 %collective-permute-start.7 = (bf16[256,768]{1,0:T(8,128)(2,1)S(1)}, bf16[256,768]{1,0:T(8,128)(2,1)S(1)}, u32[]{:S(2)}, u32[]{:S(2)}) collective-permute-start(bf16[256,768]{1,0:T(8,128)(2,1)S(1)} %get-tuple-element.132), channel_id=1, source_target_pairs={{0,66},{1,67},{2,64},{3,65},{4,70},{5,71},{6,68},{7,69},{8,74},{9,... | collective-permute-start | bytes 1179656 | tf_op jit(solution)/shard_map/ppermute | solution.py:94
  29.2 18.0 %collective-permute-start.8 = (bf16[256,768]{1,0:T(8,128)(2,1)S(1)}, bf16[256,768]{1,0:T(8,128)(2,1)S(1)}, u32[]{:S(2)}, u32[]{:S(2)}) collective-permute-start(bf16[256,768]{1,0:T(8,128)(2,1)S(1)} %get-tuple-element.133), channel_id=1, source_target_pairs={{0,67},{1,66},{2,65},{3,64},{4,71},{5,70},{6,69},{7,68},{8,75},{9,... | collective-permute-start | bytes 1179656 | tf_op jit(solution)/shard_map/ppermute | solution.py:94
  30.2 35.9 %collective-permute-start.11 = (bf16[256,1536]{1,0:T(8,128)(2,1)S(1)}, bf16[256,1536]{1,0:T(8,128)(2,1)S(1)}, u32[]{:S(2)}, u32[]{:S(2)}) collective-permute-start(bf16[256,1536]{1,0:T(8,128)(2,1)S(1)} %get-tuple-element.143), channel_id=1, source_target_pairs={{0,3},{1,2},{2,1},{3,0},{4,7},{5,6},{6,5},{7,4},{8,11},{9,10},{10,... | collective-permute-start | bytes 2359304 | tf_op jit(solution)/shard_map/ppermute | solution.py:94
  63.2 21.1 %collective-permute-start.10 = (bf16[256,1536]{1,0:T(8,128)(2,1)S(1)}, bf16[256,1536]{1,0:T(8,128)(2,1)S(1)}, u32[]{:S(2)}, u32[]{:S(2)}) collective-permute-start(bf16[256,1536]{1,0:T(8,128)(2,1)S(1)} %get-tuple-element.141), channel_id=1, source_target_pairs={{0,66},{1,67},{2,64},{3,65},{4,70},{5,71},{6,68},{7,69},{8,74},{9,... | collective-permute-start | bytes 2359304 | tf_op jit(solution)/shard_map/ppermute | solution.py:94
  66.1 18.2 %collective-permute-start.12 = (bf16[256,1024]{1,0:T(8,128)(2,1)S(1)}, bf16[256,1024]{1,0:T(8,128)(2,1)S(1)}, u32[]{:S(2)}, u32[]{:S(2)}) collective-permute-start(bf16[256,1024]{1,0:T(8,128)(2,1)S(1)} %copy-done.13), channel_id=1, source_target_pairs={{0,2},{1,3},{2,0},{3,1},{4,6},{5,7},{6,4},{7,5},{8,10},{9,11},{10,... | collective-permute-start | bytes 1572872 | tf_op jit(solution)/shard_map/ppermute | solution.py:94
  84.3 13.5 %collective-permute-start.13 = (bf16[256,1024]{1,0:T(8,128)(2,1)S(1)}, bf16[256,1024]{1,0:T(8,128)(2,1)S(1)}, u32[]{:S(2)}, u32[]{:S(2)}) collective-permute-start(bf16[256,1024]{1,0:T(8,128)(2,1)S(1)} %get-tuple-element.145), channel_id=1, source_target_pairs={{0,2},{1,3},{2,0},{3,1},{4,6},{5,7},{6,4},{7,5},{8,10},{9,11},{10,... | collective-permute-start | bytes 1572872 | tf_op jit(solution)/shard_map/ppermute | solution.py:94
  99.3 12.6 %collective-permute-start.14 = (bf16[256,1024]{1,0:T(8,128)(2,1)S(1)}, bf16[256,1024]{1,0:T(8,128)(2,1)S(1)}, u32[]{:S(2)}, u32[]{:S(2)}) collective-permute-start(bf16[256,1024]{1,0:T(8,128)(2,1)S(1)} %get-tuple-element.148.h0), channel_id=1, source_target_pairs={{0,2},{1,3},{2,0},{3,1},{4,6},{5,7},{6,4},{7,5},{8,10},{9,11},{10,... | collective-permute-start | bytes 1572872 | tf_op jit(solution)/shard_map/ppermute | solution.py:94
  99.6 12.7 %collective-permute-start.19 = (bf16[256,1536]{1,0:T(8,128)(2,1)S(1)}, bf16[256,1536]{1,0:T(8,128)(2,1)S(1)}, u32[]{:S(2)}, u32[]{:S(2)}) collective-permute-start(bf16[256,1536]{1,0:T(8,128)(2,1)S(1)} %get-tuple-element.150), channel_id=1, source_target_pairs={{0,1},{1,0},{2,3},{3,2},{4,5},{5,4},{6,7},{7,6},{8,9},{9,8},{10,11... | collective-permute-start | bytes 2359304 | tf_op jit(solution)/shard_map/ppermute | solution.py:94
  99.6 12.7 %collective-permute-start.17 = (bf16[256,1024]{1,0:T(8,128)(2,1)S(1)}, bf16[256,1024]{1,0:T(8,128)(2,1)S(1)}, u32[]{:S(2)}, u32[]{:S(2)}) collective-permute-start(bf16[256,1024]{1,0:T(8,128)(2,1)S(1)} %copy-done.13), channel_id=1, source_target_pairs={{0,1},{1,0},{2,3},{3,2},{4,5},{5,4},{6,7},{7,6},{8,9},{9,8},{10,11... | collective-permute-start | bytes 1572872 | tf_op jit(solution)/shard_map/ppermute | solution.py:94
  100.1 12.2 %collective-permute-start.18 = (bf16[256,1024]{1,0:T(8,128)(2,1)S(1)}, bf16[256,1024]{1,0:T(8,128)(2,1)S(1)}, u32[]{:S(2)}, u32[]{:S(2)}) collective-permute-start(bf16[256,1024]{1,0:T(8,128)(2,1)S(1)} %collective-permute-done.12.g1), channel_id=1, source_target_pairs={{0,1},{1,0},{2,3},{3,2},{4,5},{5,4},{6,7},{7,6},{8,9},{9,8},{10,11... | collective-permute-start | bytes 1572872 | tf_op jit(solution)/shard_map/ppermute | solution.py:94
  100.1 12.2 %collective-permute-start.15 = (bf16[256,1024]{1,0:T(8,128)(2,1)S(1)}, bf16[256,1024]{1,0:T(8,128)(2,1)S(1)}, u32[]{:S(2)}, u32[]{:S(2)}) collective-permute-start(bf16[256,1024]{1,0:T(8,128)(2,1)S(1)} %get-tuple-element.148.h0), channel_id=1, source_target_pairs={{0,1},{1,0},{2,3},{3,2},{4,5},{5,4},{6,7},{7,6},{8,9},{9,8},{10,11... | collective-permute-start | bytes 1572872 | tf_op jit(solution)/shard_map/ppermute | solution.py:94
  137.1 14.0 %collective-permute-start.22 = (bf16[256,1024]{1,0:T(8,128)(2,1)S(1)}, bf16[256,1024]{1,0:T(8,128)(2,1)S(1)}, u32[]{:S(2)}, u32[]{:S(2)}) collective-permute-start(bf16[256,1024]{1,0:T(8,128)(2,1)S(1)} %get-tuple-element.155), channel_id=1, source_target_pairs={{0,2},{1,3},{2,0},{3,1},{4,6},{5,7},{6,4},{7,5},{8,10},{9,11},{10,... | collective-permute-start | bytes 1572872 | tf_op jit(solution)/shard_map/ppermute | solution.py:94
  152.4 16.5 %collective-permute-start.29 = (bf16[256,2304]{1,0:T(8,128)(2,1)S(1)}, bf16[256,2304]{1,0:T(8,128)(2,1)S(1)}, u32[]{:S(2)}, u32[]{:S(2)}) collective-permute-start(bf16[256,2304]{1,0:T(8,128)(2,1)S(1)} %copy-done.58), channel_id=1, source_target_pairs={{0,16},{1,5},{2,18},{3,7},{4,20},{5,1},{6,22},{7,3},{8,24},{9,13},... | collective-permute-start | bytes 3538952 | tf_op jit(solution)/shard_map/ppermute | solution.py:94
  153.9 17.4 %collective-permute-start.30 = (bf16[256,2304]{1,0:T(8,128)(2,1)S(1)}, bf16[256,2304]{1,0:T(8,128)(2,1)S(1)}, u32[]{:S(2)}, u32[]{:S(2)}) collective-permute-start(bf16[256,2304]{1,0:T(8,128)(2,1)S(1)} %copy-done.57), channel_id=1, source_target_pairs={{0,48},{1,13},{2,50},{3,15},{4,52},{5,9},{6,54},{7,11},{8,56},{9,5... | collective-permute-start | bytes 3538952 | tf_op jit(solution)/shard_map/ppermute | solution.py:94
  156.0 12.7 %collective-permute-start.23 = (bf16[256,1024]{1,0:T(8,128)(2,1)S(1)}, bf16[256,1024]{1,0:T(8,128)(2,1)S(1)}, u32[]{:S(2)}, u32[]{:S(2)}) collective-permute-start(bf16[256,1024]{1,0:T(8,128)(2,1)S(1)} %get-tuple-element.161.b0), channel_id=1, source_target_pairs={{0,2},{1,3},{2,0},{3,1},{4,6},{5,7},{6,4},{7,5},{8,10},{9,11},{10,... | collective-permute-start | bytes 1572872 | tf_op jit(solution)/shard_map/ppermute | solution.py:94
  156.6 18.0 %collective-permute-start.24 = (bf16[256,1024]{1,0:T(8,128)(2,1)S(1)}, bf16[256,1024]{1,0:T(8,128)(2,1)S(1)}, u32[]{:S(2)}, u32[]{:S(2)}) collective-permute-start(bf16[256,1024]{1,0:T(8,128)(2,1)S(1)} %get-tuple-element.161.b0), channel_id=1, source_target_pairs={{0,1},{1,0},{2,3},{3,2},{4,5},{5,4},{6,7},{7,6},{8,9},{9,8},{10,11... | collective-permute-start | bytes 1572872 | tf_op jit(solution)/shard_map/ppermute | solution.py:94
  168.8 5.9 %collective-permute-start.25 = (bf16[256,1024]{1,0:T(8,128)(2,1)S(1)}, bf16[256,1024]{1,0:T(8,128)(2,1)S(1)}, u32[]{:S(2)}, u32[]{:S(2)}) collective-permute-start(bf16[256,1024]{1,0:T(8,128)(2,1)S(1)} %collective-permute-done.23.b1), channel_id=1, source_target_pairs={{0,1},{1,0},{2,3},{3,2},{4,5},{5,4},{6,7},{7,6},{8,9},{9,8},{10,11... | collective-permute-start | bytes 1572872 | tf_op jit(solution)/shard_map/ppermute | solution.py:94
  172.4 11.3 %collective-permute-start.31 = (bf16[128,2304]{1,0:T(8,128)(2,1)S(1)}, bf16[128,2304]{1,0:T(8,128)(2,1)S(1)}, u32[]{:S(2)}, u32[]{:S(2)}) collective-permute-start(bf16[128,2304]{1,0:T(8,128)(2,1)S(1)} %get-tuple-element.189), channel_id=1, source_target_pairs={{0,48},{1,13},{2,50},{3,15},{4,52},{5,9},{6,54},{7,11},{8,56},{9,5... | collective-permute-start | bytes 1769480 | tf_op jit(solution)/shard_map/ppermute | solution.py:94
  174.6 9.9 %collective-permute-start.32 = (bf16[128,2304]{1,0:T(8,128)(2,1)S(1)}, bf16[128,2304]{1,0:T(8,128)(2,1)S(1)}, u32[]{:S(2)}, u32[]{:S(2)}) collective-permute-start(bf16[128,2304]{1,0:T(8,128)(2,1)S(1)} %get-tuple-element.191), channel_id=1, source_target_pairs={{0,16},{1,5},{2,18},{3,7},{4,20},{5,1},{6,22},{7,3},{8,24},{9,13},... | collective-permute-start | bytes 1769480 | tf_op jit(solution)/shard_map/ppermute | solution.py:94
  185.3 11.4 %collective-permute-start.33 = (bf16[64,2304]{1,0:T(8,128)(2,1)S(1)}, bf16[64,2304]{1,0:T(8,128)(2,1)S(1)}, u32[]{:S(2)}, u32[]{:S(2)}) collective-permute-start(bf16[64,2304]{1,0:T(8,128)(2,1)S(1)} %get-tuple-element.194), channel_id=1, source_target_pairs={{0,4},{1,17},{2,6},{3,19},{4,0},{5,21},{6,2},{7,23},{8,12},{9,25},... | collective-permute-start | bytes 884744 | tf_op jit(solution)/shard_map/ppermute | solution.py:94
  187.0 9.7 %collective-permute-start.34 = (bf16[64,2304]{1,0:T(8,128)(2,1)S(1)}, bf16[64,2304]{1,0:T(8,128)(2,1)S(1)}, u32[]{:S(2)}, u32[]{:S(2)}) collective-permute-start(bf16[64,2304]{1,0:T(8,128)(2,1)S(1)} %get-tuple-element.196), channel_id=1, source_target_pairs={{0,12},{1,49},{2,14},{3,51},{4,8},{5,53},{6,10},{7,55},{8,4},{9,57... | collective-permute-start | bytes 884744 | tf_op jit(solution)/shard_map/ppermute | solution.py:94
  197.4 6.4 %collective-permute-start.35 = (bf16[32,2304]{1,0:T(8,128)(2,1)S(1)}, bf16[32,2304]{1,0:T(8,128)(2,1)S(1)}, u32[]{:S(2)}, u32[]{:S(2)}) collective-permute-start(bf16[32,2304]{1,0:T(8,128)(2,1)S(1)} %get-tuple-element.199), channel_id=1, source_target_pairs={{0,12},{1,49},{2,14},{3,51},{4,8},{5,53},{6,10},{7,55},{8,4},{9,57... | collective-permute-start | bytes 442376 | tf_op jit(solution)/shard_map/ppermute | solution.py:94
  198.4 5.4 %collective-permute-start.36 = (bf16[32,2304]{1,0:T(8,128)(2,1)S(1)}, bf16[32,2304]{1,0:T(8,128)(2,1)S(1)}, u32[]{:S(2)}, u32[]{:S(2)}) collective-permute-start(bf16[32,2304]{1,0:T(8,128)(2,1)S(1)} %get-tuple-element.201), channel_id=1, source_target_pairs={{0,4},{1,17},{2,6},{3,19},{4,0},{5,21},{6,2},{7,23},{8,12},{9,25},... | collective-permute-start | bytes 442376 | tf_op jit(solution)/shard_map/ppermute | solution.py:94
  203.9 8.6 %collective-permute-start.37 = (bf16[64,2304]{1,0:T(8,128)(2,1)S(1)}, bf16[64,2304]{1,0:T(8,128)(2,1)S(1)}, u32[]{:S(2)}, u32[]{:S(2)}) collective-permute-start(bf16[64,2304]{1,0:T(8,128)(2,1)S(1)} %piece_mlp.1.a_ref), channel_id=1, source_target_pairs={{0,64},{1,65},{2,66},{3,67},{4,68},{5,69},{6,70},{7,71},{8,72},{9,... | collective-permute-start | bytes 884744 | tf_op jit(solution)/shard_map/ppermute | solution.py:94
  219.3 26.7 %collective-permute-start.27 = (bf16[512,1024]{1,0:T(8,128)(2,1)S(1)}, bf16[512,1024]{1,0:T(8,128)(2,1)S(1)}, u32[]{:S(2)}, u32[]{:S(2)}) collective-permute-start(bf16[512,1024]{1,0:T(8,128)(2,1)S(1)} %get-tuple-element.172), channel_id=1, source_target_pairs={{0,1},{1,0},{2,3},{3,2},{4,5},{5,4},{6,7},{7,6},{8,9},{9,8},{10,11... | collective-permute-start | bytes 3145736 | tf_op jit(solution)/shard_map/ppermute | solution.py:94
  219.7 28.0 %collective-permute-start.21 = (bf16[512,1024]{1,0:T(8,128)(2,1)}, bf16[512,1024]{1,0:T(8,128)(2,1)S(1)}, u32[]{:S(2)}, u32[]{:S(2)}) collective-permute-start(bf16[512,1024]{1,0:T(8,128)(2,1)} %get-tuple-element.156), channel_id=1, source_target_pairs={{0,1},{1,0},{2,3},{3,2},{4,5},{5,4},{6,7},{7,6},{8,9},{9,8},{10,11... | collective-permute-start | bytes 3145736 | tf_op jit(solution)/shard_map/ppermute | solution.py:94
  219.9 11.5 %collective-permute-start.41 = (bf16[256,1152]{1,0:T(8,128)(2,1)}, bf16[256,1152]{1,0:T(8,128)(2,1)S(1)}, u32[]{:S(2)}, u32[]{:S(2)}) collective-permute-start(bf16[256,1152]{1,0:T(8,128)(2,1)} %copy-done.12), channel_id=1, source_target_pairs={{0,16},{1,5},{2,18},{3,7},{4,20},{5,1},{6,22},{7,3},{8,24},{9,13},... | collective-permute-start | bytes 1769480 | tf_op jit(solution)/shard_map/ppermute | solution.py:94
  223.3 16.1 %collective-permute-start.42 = (bf16[256,1152]{1,0:T(8,128)(2,1)}, bf16[256,1152]{1,0:T(8,128)(2,1)S(1)}, u32[]{:S(2)}, u32[]{:S(2)}) collective-permute-start(bf16[256,1152]{1,0:T(8,128)(2,1)} %copy-done.11), channel_id=1, source_target_pairs={{0,48},{1,13},{2,50},{3,15},{4,52},{5,9},{6,54},{7,11},{8,56},{9,5... | collective-permute-start | bytes 1769480 | tf_op jit(solution)/shard_map/ppermute | solution.py:94
  242.4 8.8 %collective-permute-start.43 = (bf16[128,1152]{1,0:T(8,128)(2,1)S(1)}, bf16[128,1152]{1,0:T(8,128)(2,1)S(1)}, u32[]{:S(2)}, u32[]{:S(2)}) collective-permute-start(bf16[128,1152]{1,0:T(8,128)(2,1)S(1)} %get-tuple-element.215), channel_id=1, source_target_pairs={{0,48},{1,13},{2,50},{3,15},{4,52},{5,9},{6,54},{7,11},{8,56},{9,5... | collective-permute-start | bytes 884744 | tf_op jit(solution)/shard_map/ppermute | solution.py:94
  246.0 6.7 %collective-permute-start.44 = (bf16[128,1152]{1,0:T(8,128)(2,1)S(1)}, bf16[128,1152]{1,0:T(8,128)(2,1)S(1)}, u32[]{:S(2)}, u32[]{:S(2)}) collective-permute-start(bf16[128,1152]{1,0:T(8,128)(2,1)S(1)} %get-tuple-element.217), channel_id=1, source_target_pairs={{0,16},{1,5},{2,18},{3,7},{4,20},{5,1},{6,22},{7,3},{8,24},{9,13},... | collective-permute-start | bytes 884744 | tf_op jit(solution)/shard_map/ppermute | solution.py:94
  246.3 14.9 %collective-permute-start.28 = (bf16[256,1024]{1,0:T(8,128)(2,1)S(1)}, bf16[256,1024]{1,0:T(8,128)(2,1)S(1)}, u32[]{:S(2)}, u32[]{:S(2)}) collective-permute-start(bf16[256,1024]{1,0:T(8,128)(2,1)S(1)} %get-tuple-element.175), channel_id=1, source_target_pairs={{0,2},{1,3},{2,0},{3,1},{4,6},{5,7},{6,4},{7,5},{8,10},{9,11},{10,... | collective-permute-start | bytes 1572872 | tf_op jit(solution)/shard_map/ppermute | solution.py:94
  248.9 18.7 %collective-permute-start.26 = (bf16[256,1024]{1,0:T(8,128)(2,1)S(1)}, bf16[256,1024]{1,0:T(8,128)(2,1)S(1)}, u32[]{:S(2)}, u32[]{:S(2)}) collective-permute-start(bf16[256,1024]{1,0:T(8,128)(2,1)S(1)} %get-tuple-element.171), channel_id=1, source_target_pairs={{0,2},{1,3},{2,0},{3,1},{4,6},{5,7},{6,4},{7,5},{8,10},{9,11},{10,... | collective-permute-start | bytes 1572872 | tf_op jit(solution)/shard_map/ppermute | solution.py:94
  253.4 7.8 %collective-permute-start.45 = (bf16[64,1152]{1,0:T(8,128)(2,1)S(1)}, bf16[64,1152]{1,0:T(8,128)(2,1)S(1)}, u32[]{:S(2)}, u32[]{:S(2)}) collective-permute-start(bf16[64,1152]{1,0:T(8,128)(2,1)S(1)} %get-tuple-element.220), channel_id=1, source_target_pairs={{0,4},{1,17},{2,6},{3,19},{4,0},{5,21},{6,2},{7,23},{8,12},{9,25},... | collective-permute-start | bytes 442376 | tf_op jit(solution)/shard_map/ppermute | solution.py:94
  253.5 7.7 %collective-permute-start.46 = (bf16[64,1152]{1,0:T(8,128)(2,1)S(1)}, bf16[64,1152]{1,0:T(8,128)(2,1)S(1)}, u32[]{:S(2)}, u32[]{:S(2)}) collective-permute-start(bf16[64,1152]{1,0:T(8,128)(2,1)S(1)} %get-tuple-element.222), channel_id=1, source_target_pairs={{0,12},{1,49},{2,14},{3,51},{4,8},{5,53},{6,10},{7,55},{8,4},{9,57... | collective-permute-start | bytes 442376 | tf_op jit(solution)/shard_map/ppermute | solution.py:94
  261.9 7.2 %collective-permute-start.47 = (bf16[32,1152]{1,0:T(8,128)(2,1)S(1)}, bf16[32,1152]{1,0:T(8,128)(2,1)S(1)}, u32[]{:S(2)}, u32[]{:S(2)}) collective-permute-start(bf16[32,1152]{1,0:T(8,128)(2,1)S(1)} %get-tuple-element.225), channel_id=1, source_target_pairs={{0,12},{1,49},{2,14},{3,51},{4,8},{5,53},{6,10},{7,55},{8,4},{9,57... | collective-permute-start | bytes 221192 | tf_op jit(solution)/shard_map/ppermute | solution.py:94
  262.0 7.1 %collective-permute-start.48 = (bf16[32,1152]{1,0:T(8,128)(2,1)S(1)}, bf16[32,1152]{1,0:T(8,128)(2,1)S(1)}, u32[]{:S(2)}, u32[]{:S(2)}) collective-permute-start(bf16[32,1152]{1,0:T(8,128)(2,1)S(1)} %get-tuple-element.227), channel_id=1, source_target_pairs={{0,4},{1,17},{2,6},{3,19},{4,0},{5,21},{6,2},{7,23},{8,12},{9,25},... | collective-permute-start | bytes 221192 | tf_op jit(solution)/shard_map/ppermute | solution.py:94
  269.1 6.7 %collective-permute-start.49 = (bf16[64,1152]{1,0:T(8,128)(2,1)S(1)}, bf16[64,1152]{1,0:T(8,128)(2,1)S(1)}, u32[]{:S(2)}, u32[]{:S(2)}) collective-permute-start(bf16[64,1152]{1,0:T(8,128)(2,1)S(1)} %piece_attn.1.a_ref), channel_id=1, source_target_pairs={{0,64},{1,65},{2,66},{3,67},{4,68},{5,69},{6,70},{7,71},{8,72},{9,... | collective-permute-start | bytes 442376 | tf_op jit(solution)/shard_map/ppermute | solution.py:94
  281.8 8.6 %collective-permute-start.53 = (bf16[16,2048]{1,0:T(8,128)(2,1)S(1)}, bf16[16,2048]{1,0:T(8,128)(2,1)S(1)}, u32[]{:S(2)}, u32[]{:S(2)}) collective-permute-start(bf16[16,2048]{1,0:T(8,128)(2,1)S(1)} %get-tuple-element.233), channel_id=1, source_target_pairs={{0,12},{1,49},{2,14},{3,51},{4,8},{5,53},{6,10},{7,55},{8,4},{9,57... | collective-permute-start | bytes 196616 | tf_op jit(solution)/shard_map/ppermute | solution.py:94
  293.7 6.4 %collective-permute-start.58 = (bf16[32,2176]{1,0:T(8,128)(2,1)S(1)}, bf16[32,2176]{1,0:T(8,128)(2,1)S(1)}, u32[]{:S(2)}, u32[]{:S(2)}) collective-permute-start(bf16[32,2176]{1,0:T(8,128)(2,1)S(1)} %pad_maximum_fusion.2), channel_id=1, source_target_pairs={{0,12},{1,49},{2,14},{3,51},{4,8},{5,53},{6,10},{7,55},{8,4},{9,57... | collective-permute-start | bytes 417800 | tf_op jit(solution)/shard_map/ppermute | solution.py:94
  295.5 8.0 %collective-permute-start.55 = (bf16[64,2048]{1,0:T(8,128)(2,1)S(1)}, bf16[64,2048]{1,0:T(8,128)(2,1)S(1)}, u32[]{:S(2)}, u32[]{:S(2)}) collective-permute-start(bf16[64,2048]{1,0:T(8,128)(2,1)S(1)} %pad_maximum_fusion.1), channel_id=1, source_target_pairs={{0,48},{1,13},{2,50},{3,15},{4,52},{5,9},{6,54},{7,11},{8,56},{9,5... | collective-permute-start | bytes 786440 | tf_op jit(solution)/shard_map/ppermute | solution.py:94
  300.2 7.2 %collective-permute-start.59 = (bf16[64,2176]{1,0:T(8,128)(2,1)S(1)}, bf16[64,2176]{1,0:T(8,128)(2,1)S(1)}, u32[]{:S(2)}, u32[]{:S(2)}) collective-permute-start(bf16[64,2176]{1,0:T(8,128)(2,1)S(1)} %pad_maximum_fusion), channel_id=1, source_target_pairs={{0,16},{1,5},{2,18},{3,7},{4,20},{5,1},{6,22},{7,3},{8,24},{9,13},... | collective-permute-start | bytes 835592 | tf_op jit(solution)/shard_map/ppermute | solution.py:94
  304.2 13.3 %collective-permute-start.56 = (bf16[128,2048]{1,0:T(8,128)(2,1)}, bf16[128,2048]{1,0:T(8,128)(2,1)}, u32[]{:S(2)}, u32[]{:S(2)}) collective-permute-start(bf16[128,2048]{1,0:T(8,128)(2,1)} %constant_dynamic-update-slice_fusion.a1), channel_id=1, source_target_pairs={{0,16},{1,5},{2,18},{3,7},{4,20},{5,1},{6,22},{7,3},{8,24},{9,13},... | collective-permute-start | bytes 1572872 | tf_op jit(solution)/shard_map/ppermute | solution.py:94
  308.1 11.3 %collective-permute-start.60 = (bf16[128,2176]{1,0:T(8,128)(2,1)}, bf16[128,2176]{1,0:T(8,128)(2,1)}, u32[]{:S(2)}, u32[]{:S(2)}) collective-permute-start(bf16[128,2176]{1,0:T(8,128)(2,1)} %constant_dynamic-update-slice_fusion.4.a2), channel_id=1, source_target_pairs={{0,48},{1,13},{2,50},{3,15},{4,52},{5,9},{6,54},{7,11},{8,56},{9,5... | collective-permute-start | bytes 1671176 | tf_op jit(solution)/shard_map/ppermute | solution.py:94
  (80 other events, 391.6 us)
Sparse Core Ops, SparseCore 0:
  219.4 61.7 all-gather.1

commit v2 on v1

--- a/solution.py
+++ b/solution.py
@@ -47,10 +47,6 @@
 ZFAR_SIBLING = perm_of(lambda x, y, z, c: (x, y, 3 - z, 1 - c))
 ZNEAR_SIBLING = perm_of(lambda x, y, z, c: (x, y, z ^ 1, 1 - c))
 ZREPLICA = perm_of(lambda x, y, z, c: (x, y, (z + 2) % 4, c))
-SIBLING_T = perm_of(lambda x, y, z, c: (y, x, z, 1 - c))
-ZNEAR_SIBLING_T = perm_of(lambda x, y, z, c: (y, x, z ^ 1, 1 - c))
-
-
 def cube_move(bit):
     def move(x, y, z, c):
         on_x = (bit < 2) == (c == 0)
@@ -62,27 +58,6 @@
 CUBE = tuple(cube_move(bit) for bit in range(4))
 
 
-def gray(v):
-    return (((v + 1) // 2) % 2, v // 2)
-
-
-def piece_of(x, y, c):
-    first, second = (x, y) if c == 0 else (y, x)
-    a, b = gray(first)
-    d, e = gray(second)
-    return 8 * a + 4 * b + 2 * d + e
-
-
-def plane_groups():
-    groups = {}
-    for lin in range(128):
-        x, y, z, c = where_is(lin)
-        groups.setdefault((z, c), []).append((4 * x + y, lin))
-    return [[lin for _, lin in sorted(g)] for g in groups.values()]
-
-
-PLANES = plane_groups()
-PIECES = tuple(piece_of(n // 4, n % 4, 0) for n in range(16))
 SPLITS = (
     ((0, 2, 128), (1, 2, 64), (2, 2, 32), (3, 2, 16)),
     ((1, 4, 64), (0, 2, 64), (3, 4, 16), (2, 2, 16)),
@@ -115,13 +90,13 @@
 VMEM = pl.BlockSpec(memory_space=pltpu.VMEM)
 
 
-def call(kernel, name, in_specs, out_shape, operands, *, us=1, limit=48, **kw):
+def call(kernel, name, in_specs, out_shape, operands, *, limit=48, **kw):
     return pl.pallas_call(
         kernel,
         in_specs=in_specs,
         out_shape=out_shape,
         compiler_params=pltpu.CompilerParams(vmem_limit_bytes=limit << 20),
-        cost_estimate=pl.CostEstimate(flops=us * 10**9, bytes_accessed=us << 20, transcendentals=0),
+        cost_estimate=pl.CostEstimate(flops=0, bytes_accessed=0, transcendentals=0),
         name=name,
         **kw,
     )(*operands)
@@ -148,13 +123,12 @@
 def pack_kernel(a_ref, b_ref, c_ref, d_ref, bias_ref, out_ref):
     out_ref[...] = jnp.zeros((16, D), BF16)
     for v, ref in enumerate((a_ref, b_ref, c_ref, d_ref)):
-        out_ref[0:1, 256 * v : 256 * v + 256] = ref[...]
-    out_ref[1:2, :768] = bias_ref[...]
+        out_ref[0:1, 256 * v : 256 * v + 256] = ref[...].reshape(1, 256)
+    out_ref[1:2, :768] = bias_ref[...].reshape(1, 768)
 
 
 def pack(*vectors):
-    rows = [v.reshape(1, -1) for v in vectors]
-    return call(pack_kernel, "pack", [VMEM] * 5, shaped(16, D), rows, limit=16, us=0)
+    return call(pack_kernel, "pack", [VMEM] * 5, shaped(16, D), vectors, limit=16)
 
 
 def tables_kernel(info, cos_ref, sin_ref):
@@ -171,19 +145,28 @@
 
 
 def tables(info):
-    return call(tables_kernel, "tables", [SMEM], [shaped(D, 128, dtype=F32)] * 2, (info,), limit=16, us=0)
-
-
-def pick_qkv_kernel(info, w_ref, *outs):
-    for j, out in enumerate(outs):
+    return call(tables_kernel, "tables", [SMEM], [shaped(D, 128, dtype=F32)] * 2, (info,), limit=16)
+
+
+def pick_qkv_kernel(info, w_ref, own, sibling, far):
+    for j in range(GROUP):
         d = info[ME] ^ j
         for c in range(3):
-            out[:, 256 * c : 256 * c + 256] = w_ref[:, lanes_of(c * D + d * 256, 256)]
+            cols = w_ref[:, lanes_of(c * D + d * 256, 256)]
+            if j < 2:
+                (own, sibling)[j][:, 256 * c : 256 * c + 256] = cols
+            else:
+                far[ROWS * (j - 2) : ROWS * (j - 1), 256 * c : 256 * c + 256] = cols
 
 
 def pick_qkv(info, w):
     return call(
-        pick_qkv_kernel, "pick_qkv", [SMEM, VMEM], [shaped(ROWS, 768)] * 4, (info, w), limit=32, us=0
+        pick_qkv_kernel,
+        "pick_qkv",
+        [SMEM, VMEM],
+        [shaped(ROWS, 768), shaped(ROWS, 768), shaped(2 * ROWS, 768)],
+        (info, w),
+        limit=32,
     )
 
 
@@ -205,7 +188,6 @@
         [shaped(ROWS, 2 * FFP)] * 4,
         (info, w),
         limit=32,
-        us=0,
         scratch_shapes=[pltpu.VMEM((GROUP, ROWS, 2 * FFP), BF16)],
     )
 
@@ -217,7 +199,7 @@
     me = info[ME]
     copies = []
     for j, w in enumerate((w0, w1, w2, w3)):
-        copy = pltpu.make_async_copy(w, w_ref.at[row_of(me ^ j)], sems.at[j])
+        copy = pltpu.make_async_copy(w.at[:ROWS], w_ref.at[row_of(me ^ j)], sems.at[j])
         copy.start()
         copies.append(copy)
     for j, v in enumerate((v0, v1, v2, v3)):
@@ -254,68 +236,81 @@
         [SMEM] + [VMEM] * 8 + [ANY] * 4 + [VMEM] * 2,
         [shaped(D, D), shaped(D, 768), shaped(D, 768), shaped(8, D, dtype=F32)],
         (info, *xs, *vs, *ws, cos, sin),
-        us=0,
+        limit=20,
         scratch_shapes=[pltpu.VMEM((8, 3 * D), F32), pltpu.SemaphoreType.DMA((4,))],
     )
 
 
 def later_keys():
-    return lax.broadcasted_iota(jnp.int32, (ROWS, ROWS), 0) > lax.broadcasted_iota(
-        jnp.int32, (ROWS, ROWS), 1
-    )
-
-
-def attend_kernel(info, qkv_ref, w_ref, mixed_ref, lse_ref, low_ref, up_ref):
-    pair = pl.program_id(0)
-    side = lax.broadcasted_iota(jnp.int32, (ROWS, 128), 1) // HEAD
-    lane0 = pair * 128
+    return lax.broadcasted_iota(jnp.int32, (ROWS, 2 * ROWS), 0) > (
+        lax.broadcasted_iota(jnp.int32, (ROWS, 2 * ROWS), 1) % ROWS
+    )
+
+
+def two_heads(v):
+    side = lax.broadcasted_iota(jnp.int32, v.shape, 1) // HEAD
+    zero = jnp.zeros((), v.dtype)
+    return jnp.concatenate([jnp.where(side == h, v, zero) for h in range(2)], axis=0)
+
+
+def one_pair(vt):
+    return jnp.concatenate([vt[:HEAD, :ROWS], vt[HEAD:, ROWS:]], axis=0).T
+
+
+def attend_pair(pair, info, qkv_ref, mixed_ref, lse_ref):
+    cols = [slice(256 * c + 128 * pair, 256 * c + 128 * pair + 128) for c in range(3)]
     later = later_keys()
-    zero = jnp.zeros((), BF16)
     for i in range(GROUP):
         rows = row_of(info[SLOT + i])
-        both = qkv_ref[rows, lanes_of(lane0)]
-        outs = []
-        for h in range(2):
-            q = jnp.where(side == h, both, zero)
-            tiles = []
-            for n in range(i + 1):
-                st = dot_nt(qkv_ref[row_of(info[SLOT + n]), lanes_of(lane0 + 256)], q)
-                tiles.append(jnp.where(later, -1e30, st) if n == i else st)
-            top = functools.reduce(jnp.maximum, [jnp.max(t, axis=0, keepdims=True) for t in tiles])
-            top = top * SCALE2
-            total = jnp.zeros((1, ROWS), F32)
-            out = jnp.zeros((128, ROWS), F32)
-            for n in range(i + 1):
-                p = jnp.exp2(tiles[n] * SCALE2 - top)
-                total = total + jnp.sum(p, axis=0, keepdims=True)
-                v = qkv_ref[row_of(info[SLOT + n]), lanes_of(lane0 + 512)]
-                out = out + dot_tn(v, p.astype(BF16))
-            outs.append((out / total).T)
-            lse_ref[0, h : h + 1, rows] = top + jnp.log2(total)
-        mixed_ref[rows, lanes_of(lane0)] = jnp.where(side == 0, outs[0], outs[1]).astype(BF16)
-
-    @pl.when(pair == 1)
-    def _():
-        up_ref[...] = dot(mixed_ref[512:, :], w_ref[...]).astype(BF16)
-        low_ref[...] = dot(mixed_ref[:512, :], w_ref[...]).astype(BF16)
-
-
-def attend(info, qkv, w):
-    fixed = lambda h: (0, 0)
-    return call(
-        attend_kernel,
-        "attend",
-        [SMEM, pl.BlockSpec((D, 768), fixed), pl.BlockSpec((256, D), fixed)],
-        [shaped(D, 256), shaped(2, 2, D, dtype=F32), shaped(512, D), shaped(512, D)],
-        (info, qkv, w),
-        us=0,
-        grid=(2,),
-        out_specs=[
-            pl.BlockSpec((D, 256), fixed),
-            pl.BlockSpec((1, 2, D), lambda h: (h, 0, 0)),
-            pl.BlockSpec((512, D), fixed),
-            pl.BlockSpec((512, D), fixed),
-        ],
+        q = two_heads(qkv_ref[rows, cols[0]])
+        tiles = []
+        for n in range(i + 1):
+            st = dot_nt(qkv_ref[row_of(info[SLOT + n]), cols[1]], q)
+            tiles.append(jnp.where(later, -1e30, st) if n == i else st)
+        top = functools.reduce(jnp.maximum, [jnp.max(t, axis=0, keepdims=True) for t in tiles])
+        top = top * SCALE2
+        total = jnp.zeros((1, 2 * ROWS), F32)
+        out = jnp.zeros((128, 2 * ROWS), F32)
+        for n in range(i + 1):
+            p = jnp.exp2(tiles[n] * SCALE2 - top)
+            total = total + jnp.sum(p, axis=0, keepdims=True)
+            out = out + dot_tn(qkv_ref[row_of(info[SLOT + n]), cols[2]], p.astype(BF16))
+        mixed_ref[rows, :] = one_pair(out / total).astype(BF16)
+        lse = top + jnp.log2(total)
+        lse_ref[0:1, rows] = lse[:, :ROWS]
+        lse_ref[1:2, rows] = lse[:, ROWS:]
+
+
+def attend_first_kernel(info, qkv_ref, mixed_ref, lse_ref):
+    attend_pair(0, info, qkv_ref, mixed_ref, lse_ref)
+
+
+def attend_second_kernel(info, qkv_ref, m0, w_ref, mixed_ref, lse_ref, low_ref, up_ref):
+    attend_pair(1, info, qkv_ref, mixed_ref, lse_ref)
+    for rows, out in ((slice(512, D), up_ref), (slice(0, 512), low_ref)):
+        m = jnp.concatenate([m0[rows, :], mixed_ref[rows, :]], axis=1)
+        out[...] = dot(m, w_ref[...]).astype(BF16)
+
+
+def attend_first(info, qkv):
+    return call(
+        attend_first_kernel,
+        "attend_first",
+        [SMEM, VMEM],
+        [shaped(D, 128), shaped(2, D, dtype=F32)],
+        (info, qkv),
+        limit=24,
+    )
+
+
+def attend_second(info, qkv, m0, w):
+    return call(
+        attend_second_kernel,
+        "attend_second",
+        [SMEM] + [VMEM] * 3,
+        [shaped(D, 128), shaped(2, D, dtype=F32), shaped(512, D), shaped(512, D)],
+        (info, qkv, m0, w),
+        limit=24,
     )
 
 
@@ -323,42 +318,37 @@
     pair, info, qkv_ref, b0, b1, b2, b3, w_ref, lse_ref, cos_ref, sin_ref,
     out_ref, do_ref, dq_ref, dk_ref, dv_ref,
 ):
-    side = lax.broadcasted_iota(jnp.int32, (ROWS, 128), 1) // HEAD
     cols = [slice(256 * c + 128 * pair, 256 * c + 128 * pair + 128) for c in range(3)]
     later = later_keys()
-    zero = jnp.zeros((), BF16)
+    w = w_ref[128 * pair : 128 * pair + 128, :]
     for j, b in enumerate((b0, b1, b2, b3)):
-        do_ref[ROWS * j : ROWS * j + ROWS, :] = dot_nt(b[...], w_ref[...]).astype(BF16)
+        do_ref[ROWS * j : ROWS * j + ROWS, :] = dot_nt(b[...], w).astype(BF16)
     dk_ref[...] = jnp.zeros_like(dk_ref)
     dv_ref[...] = jnp.zeros_like(dv_ref)
     for i in range(GROUP):
         rows = row_of(info[SLOT + i])
-        q_both = qkv_ref[rows, cols[0]]
-        do_both = do_ref[rows, :]
-        dqt = jnp.zeros((128, ROWS), F32)
-        for h in range(2):
-            q = jnp.where(side == h, q_both, zero)
-            do = jnp.where(side == h, do_both, zero)
-            lse = lse_ref[pair, h : h + 1, rows]
-            probs, grads = [], []
-            delta = jnp.zeros((1, ROWS), F32)
-            for n in range(i + 1):
-                there = row_of(info[SLOT + n])
-                p = jnp.exp2(dot_nt(qkv_ref[there, cols[1]], q) * SCALE2 - lse)
-                if n == i:
-                    p = jnp.where(later, 0.0, p)
-                dp = dot_nt(qkv_ref[there, cols[2]], do)
-                delta = delta + jnp.sum(p * dp, axis=0, keepdims=True)
-                dv_ref[there, :] += dot(p.astype(BF16), do)
-                probs.append(p)
-                grads.append(dp)
-            for n in range(i + 1):
-                there = row_of(info[SLOT + n])
-                k = jnp.where(side == h, qkv_ref[there, cols[1]], zero)
-                ds = (probs[n] * (grads[n] - delta)).astype(BF16)
-                dk_ref[there, :] += dot(ds, q)
-                dqt = dqt + dot_tn(k, ds)
-        dq_ref[rows, :] = dqt.T
+        q = two_heads(qkv_ref[rows, cols[0]])
+        do = two_heads(do_ref[rows, :])
+        lse = jnp.concatenate([lse_ref[0:1, rows], lse_ref[1:2, rows]], axis=1)
+        probs, grads = [], []
+        delta = jnp.zeros((1, 2 * ROWS), F32)
+        for n in range(i + 1):
+            there = row_of(info[SLOT + n])
+            p = jnp.exp2(dot_nt(qkv_ref[there, cols[1]], q) * SCALE2 - lse)
+            if n == i:
+                p = jnp.where(later, 0.0, p)
+            dp = dot_nt(qkv_ref[there, cols[2]], do)
+            delta = delta + jnp.sum(p * dp, axis=0, keepdims=True)
+            dv_ref[there, :] += dot(p.astype(BF16), do)
+            probs.append(p)
+            grads.append(dp)
+        dqt = jnp.zeros((128, 2 * ROWS), F32)
+        for n in range(i + 1):
+            there = row_of(info[SLOT + n])
+            ds = (probs[n] * (grads[n] - delta)).astype(BF16)
+            dk_ref[there, :] += dot(ds, q)
+            dqt = dqt + dot_tn(qkv_ref[there, cols[1]], ds)
+        dq_ref[rows, :] = one_pair(dqt)
     lane = lax.broadcasted_iota(jnp.int32, (D, 128), 1)
     scale = HEAD ** (-0.5)
     cos, sin = cos_ref[...], sin_ref[...]
@@ -370,25 +360,13 @@
 
 
 def attend_back(pair, info, qkv, branch, w, lse, cos, sin):
-    fixed = lambda i: (0, 0)
-    block = pl.BlockSpec((ROWS, D), fixed)
     return call(
         functools.partial(attend_back_kernel, pair),
         "attend_back",
-        [
-            SMEM,
-            pl.BlockSpec((D, 768), fixed),
-            block, block, block, block,
-            pl.BlockSpec((128, D), lambda i: (pair, 0)),
-            pl.BlockSpec((2, 2, D), lambda i: (0, 0, 0)),
-            pl.BlockSpec((D, 128), fixed),
-            pl.BlockSpec((D, 128), fixed),
-        ],
+        [SMEM] + [VMEM] * 9,
         shaped(D, 384),
         (info, qkv, *branch, w, lse, cos, sin),
-        us=7,
-        grid=(1,),
-        out_specs=pl.BlockSpec((D, 384), fixed),
+        limit=32,
         scratch_shapes=[pltpu.VMEM((D, 128), BF16)] + [pltpu.VMEM((D, 128), F32)] * 3,
     )
 
@@ -399,30 +377,20 @@
     )
 
 
-def hidden_back_kernel(d0, d1, w_ref, x0, x1, x2, x3, low_ref, up_ref, sums_ref):
-    gains = jnp.zeros((1, D), F32)
-    shifts = jnp.zeros((1, D), F32)
-    for j in (2, 3, 0, 1):
-        x = (x0, x1, x2, x3)[j]
-        rows = slice(ROWS * j, ROWS * j + ROWS)
-        e = dot_nt(whole(d0[rows, :], d1[rows, :]), w_ref[...])
-        xhat, _ = stats_of(x[...].astype(F32))
-        gains = gains + jnp.sum(e * xhat, axis=0, keepdims=True)
-        shifts = shifts + jnp.sum(e, axis=0, keepdims=True)
-        out = low_ref if j < 2 else up_ref
-        out[ROWS * (j % 2) : ROWS * (j % 2) + ROWS, :] = e.astype(BF16)
-    sums_ref[0:1, :] = gains
-    sums_ref[1:2, :] = shifts
-
-
-def hidden_back(dqkvs, w, xs):
+def hidden_back_kernel(d0, d1, w_ref, low_ref, up_ref):
+    for j in range(2):
+        rows = slice(512 * j, 512 * j + 512)
+        (low_ref, up_ref)[j][...] = dot_nt(whole(d0[rows, :], d1[rows, :]), w_ref[...]).astype(BF16)
+
+
+def hidden_back(dqkvs, w):
     return call(
         hidden_back_kernel,
         "hidden_back",
-        [VMEM] * 7,
-        [shaped(512, D), shaped(512, D), shaped(2, D, dtype=F32)],
-        (*dqkvs, w, *xs),
-        us=5,
+        [VMEM] * 3,
+        [shaped(512, D), shaped(512, D)],
+        (*dqkvs, w),
+        limit=24,
     )
 
 
@@ -430,6 +398,22 @@
     total = low_ref[...].astype(F32) + got_ref[...].astype(F32)
     own_ref[...] = total[:ROWS, :]
     near_ref[...] = total[ROWS:, :].astype(BF16)
+
+
+def add_base_kernel(base_ref, low_ref, got_ref, own_ref, near_ref):
+    add_halves_kernel(low_ref, got_ref, own_ref, near_ref)
+    own_ref[...] += base_ref[...]
+
+
+def scatter_group_onto(base, low, got):
+    return call(
+        add_base_kernel,
+        "add_base",
+        [VMEM] * 3,
+        [shaped(ROWS, D, dtype=F32), shaped(ROWS, D)],
+        (base, low, got),
+        limit=16,
+    )
 
 
 def scatter_group(low, up):
@@ -495,14 +479,12 @@
     )
 
 
-def layer_out_kernel(mid_ref, part_ref, other_ref, out_ref):
-    out_ref[...] = (mid_ref[...] + part_ref[...] + other_ref[...].astype(F32)).astype(BF16)
-
-
-def layer_out_of(mid, part, other):
-    return call(
-        layer_out_kernel, "layer_out", [VMEM] * 3, shaped(ROWS, D), (mid, part, other), limit=16
-    )
+def layer_out_kernel(part_ref, other_ref, out_ref):
+    out_ref[...] = (part_ref[...] + other_ref[...].astype(F32)).astype(BF16)
+
+
+def layer_out_of(part, other):
+    return call(layer_out_kernel, "layer_out", [VMEM] * 2, shaped(ROWS, D), (part, other), limit=16)
 
 
 def feed_kernel(
@@ -575,8 +557,7 @@
         [SMEM] + [ANY] * 13,
         [shaped(D, FFP), shaped(D, 2 * FFP)] + [shaped(512, D)] * 4,
         (info, *hs, *gs, *ws, down),
-        us=18,
-        limit=56,
+        limit=38,
         grid=(2,),
         out_specs=[pl.BlockSpec((512, FFP), row), pl.BlockSpec((512, 2 * FFP), row)] + [half] * 4,
         scratch_shapes=[
@@ -600,8 +581,20 @@
             away[at, :] = rows_of(part, pl.ds(pl.multiple_of((2 * o + 1 - mine) * run, run), run))
 
 
+def own_order(info, piece):
+    return jnp.where(info[ME] % 2 == 0, piece, ((piece & 3) << 2) | (piece >> 2))
+
+
 def split_result(info, res_ref, outs):
-    halve(info, 0, lambda part, at: res_ref[part, at, :], outs)
+    for part in range(2):
+        mine = info[BIT + part]
+        weight = 8 >> part
+        for t in range(2):
+            for n in range(8):
+                low = n if part == 0 else (n & 3) | ((n & 4) << 1)
+                to = slice(128 * t + 16 * n, 128 * t + 16 * n + 16)
+                for out, bit in ((outs[2 * part], mine), (outs[2 * part + 1], 1 - mine)):
+                    out[to, :] = res_ref[part, row_of(16 * t + own_order(info, low + weight * bit), 16), :]
 
 
 def mlp_weights_kernel(
@@ -652,7 +645,7 @@
         + [pl.BlockSpec((D, FFP), lambda i: (0, jnp.minimum(i, 1))), pl.BlockSpec((D, FFP), lambda i: (0, 0))],
         [shaped(256, 3 * FFP)] * 4,
         (info, *hs, *gs, dgu, act),
-        us=10,
+        limit=26,
         grid=(3,),
         out_specs=[pl.BlockSpec((256, FFP), col)] * 4,
         scratch_shapes=[
@@ -669,8 +662,8 @@
 
 
 def attn_weights_kernel(
-    info, h_ref, d0, d1, m_ref, b0, b1, b2, b3, sa_ref, sm_ref,
-    k1, s1, k2, s2, b_ref, d_ref, ex_ref, res_ref, sems,
+    info, h_ref, d0, d1, w_ref, m0, m1, b0, b1, b2, b3, norms_ref, sm_ref,
+    k1, s1, k2, s2, d_ref, b_ref, ex_ref, res_ref, sems,
 ):
     me = info[ME]
     copies = [
@@ -681,35 +674,43 @@
         copy.start()
     d_ref[...] = whole(d0[...], d1[...])
     ex_ref[...] = jnp.zeros_like(ex_ref)
-    ex_ref[0:2, :] = sa_ref[...]
+    ex_ref[0:2, :] = norms_ref[0:2, :]
     ex_ref[2:4, :] = sm_ref[...]
     db = dot(jnp.ones((8, D), BF16), d_ref[...])[0:1, :]
     for c in range(3):
         one = db[:, 256 * c : 256 * c + 256]
         ex_ref[pl.ds(8 + 4 * c + me, 1), :] = jnp.concatenate([one] * GROUP, axis=1)
-    ex = ex_ref[...].T.astype(BF16)
+    ex = ex_ref[...].T
+    lane = lax.broadcasted_iota(jnp.int32, (512, EX), 1)
     for half in range(2):
         rows = slice(512 * half, 512 * half + 512)
-        res_ref[half, :, :768] = dot_tn(h_ref[:, rows], d_ref[...]).astype(BF16)
-        res_ref[half, :, 768 : 768 + EX] = ex[rows, :]
+        dw = dot_tn(h_ref[:, rows], d_ref[...])
+        res_ref[half, :, :768] = dw.astype(BF16)
+        w = w_ref[rows, :].astype(F32)
+        gain, shift = ex[rows, 0:1], ex[rows, 1:2]
+        sum_e = jnp.sum(w * db, axis=1, keepdims=True)
+        sum_xe = (jnp.sum(w * dw, axis=1, keepdims=True) - shift * sum_e) / gain
+        cols = jnp.where(lane == 0, sum_xe, jnp.where(lane == 1, sum_e, ex[rows, :]))
+        res_ref[half, :, 768 : 768 + EX] = cols.astype(BF16)
     for copy in copies:
         copy.wait()
+    m = jnp.concatenate([m0[...], m1[...]], axis=1)
     for half in range(2):
-        res_ref[half, :, 768 + EX :] = dot_tn(b_ref[:, 512 * half : 512 * half + 512], m_ref[...]).astype(BF16)
+        res_ref[half, :, 768 + EX :] = dot_tn(b_ref[:, 512 * half : 512 * half + 512], m).astype(BF16)
     split_result(info, res_ref, (k1, s1, k2, s2))
 
 
-def attn_weights(info, hidden, dqkvs, mixed, branch, sums_a, sums_m):
+def attn_weights(info, hidden, dqkvs, w, mixed, branch, norms, sums_m):
     return call(
         attn_weights_kernel,
         "attn_weights",
-        [SMEM] + [VMEM] * 4 + [ANY] * 4 + [VMEM] * 2,
+        [SMEM] + [VMEM] * 6 + [ANY] * 4 + [VMEM] * 2,
         [shaped(256, ATT)] * 4,
-        (info, hidden, *dqkvs, mixed, *branch, sums_a, sums_m),
-        us=5,
+        (info, hidden, *dqkvs, w, *mixed, *branch, norms, sums_m),
+        limit=30,
         scratch_shapes=[
+            pltpu.VMEM((D, 768), BF16),
             pltpu.VMEM((D, D), BF16),
-            pltpu.VMEM((D, 768), BF16),
             pltpu.VMEM((EX, D), F32),
             pltpu.VMEM((2, 512, ATT), BF16),
             pltpu.SemaphoreType.DMA((4,)),
@@ -744,14 +745,15 @@
 def scatter_plane(info, first, name, gates):
     k1, s1, k2, s2 = first
     width = k1.shape[1]
-    s1 = after(s1, *gates[0])
-    s2 = after(s2, *gates[0])
+    s1 = after(s1, *gates[0]())
+    s2 = after(s2, *gates[0]())
     for step in range(4):
         got1 = send(s1, CUBE[SPLITS[0][step][0]])
         got2 = send(s2, CUBE[SPLITS[1][step][0]])
-        operands = (after(k1, *gates[step + 1]), got1, k2, got2)
+        operands = (after(k1, *gates[step + 1]()), got1, k2, got2)
         if step == 3:
-            return call(piece_kernel, "piece_" + name, [VMEM] * 4, shaped(64, width), operands, limit=24)
+            yield call(piece_kernel, "piece_" + name, [VMEM] * 4, shaped(64, width), operands, limit=24)
+            return
         rows = k1.shape[0] // 2
         k1, s1, k2, s2 = call(
             functools.partial(halve_kernel, step + 1),
@@ -761,6 +763,7 @@
             (info, *operands),
             limit=24,
         )
+        yield k1
 
 
 def share(info, piece, cols, name, gate=()):
@@ -773,16 +776,24 @@
         (info, after(piece, *gate), send(piece, ZREPLICA)),
         limit=16,
     )
-    perms = (None, SIBLING_T, ZNEAR, ZNEAR_SIBLING_T)
+    perms = (None, SIBLING, ZNEAR, ZNEAR_SIBLING)
     return [b if p is None else send(b, p) for b, p in zip(blocks, perms)], kept
 
 
-def join_mlp_kernel(info, r0, r1, r2, r3, kept, out):
+def join_mlp_kernel(info, r0, r1, r2, r3, kept, one, two):
     for j, r in enumerate((r0, r1, r2, r3)):
         s = info[ME] ^ j
-        out[:, lanes_of(s * FFP, FFP)] = r[:, :FFP]
-        out[:, lanes_of((GROUP + s) * FFP, FFP)] = r[:, FFP:]
-    out[:, 2 * GROUP * FFP :] = kept[...]
+        one[:, lanes_of(s * FFP, FFP)] = r[:, :FFP]
+
+        @pl.when(s < 2)
+        def _():
+            one[:, lanes_of((GROUP + s) * FFP, FFP)] = r[:, FFP:]
+
+        @pl.when(s >= 2)
+        def _():
+            two[:, lanes_of((s - 2) * FFP, FFP)] = r[:, FFP:]
+
+    two[:, 2 * FFP :] = kept[...]
 
 
 def join_attn_kernel(info, r0, r1, r2, r3, kept, one, two):
@@ -796,46 +807,65 @@
     two[:, D + EX :] = kept[...]
 
 
-def finish_mlp_kernel(info, all_ref, gu_ref, down_ref, turn_ref):
-    for n, piece in enumerate(PIECES):
-        turned = 4 * (n % 4) + n // 4
-        at = row_of(jnp.where(info[ME] % 2 == 0, n, turned), 16)
+def slots_of(info, piece):
+    d = own_order(info, piece) ^ (info[BIT] * 8 + info[BIT + 1] * 4 + info[BIT + 2] * 2 + info[BIT + 3])
+    return d, ((d >> 2) & 1) * 8 + ((d >> 3) & 1) * 4 + (d & 1) * 2 + ((d >> 1) & 1)
+
+
+def at_slot(own, got, slot):
+    rows = row_of(slot & 7, 16)
+    return jnp.where(slot >= 8, got[rows, :].astype(F32), own[rows, :].astype(F32))
+
+
+def finish_mlp_kernel(info, a1, g1, a2, g2, gu_ref, down_ref, turn_ref):
+    for piece in range(16):
         to = slice(16 * piece, 16 * piece + 16)
-        for s in range(GROUP):
-            for c in range(2):
-                lo = (GROUP * c + s) * FFP
-                gu_ref[to, FF * c + FFS * s : FF * c + FFS * s + FFS] = all_ref[at, lo : lo + FFS].astype(F32)
-        turn_ref[to, :] = all_ref[at, 2 * GROUP * FFP :].astype(F32)
+        one, two = slots_of(info, piece)
+        v, u = at_slot(a1, g1, one), at_slot(a2, g2, two)
+        for s in range(2 * GROUP):
+            src, lo = (v, s * FFP) if s < 6 else (u, (s - 6) * FFP)
+            gu_ref[to, FFS * s : FFS * s + FFS] = src[:, lo : lo + FFS]
+        turn_ref[to, :] = u[:, 2 * FFP :]
     for t in range(GROUP):
         down_ref[:, 256 * t : 256 * t + 256] = turn_ref[:, FFP * t : FFP * t + FFP].T[:FFS, :]
 
 
 def finish_attn_kernel(info, a1, g1, a2, g2, qkv_ref, out_ref, vec_ref, turn_ref, ex_ref):
-    q = info[BIT] * 8 + info[BIT + 1] * 4 + info[BIT + 2] * 2 + info[BIT + 3]
     for piece in range(16):
-        d = q ^ piece
-        e = ((d >> 2) & 1) * 8 + ((d >> 3) & 1) * 4 + (d & 1) * 2 + ((d >> 1) & 1)
         to = slice(16 * piece, 16 * piece + 16)
-        for own, got, slot, one in ((a1, g1, d, True), (a2, g2, e, False)):
-            at = row_of(slot & 7, 16)
-            v = jnp.where(slot >= 8, got[at, :].astype(F32), own[at, :].astype(F32))
-            if one:
-                qkv_ref[to, : 2 * D] = v
-            else:
-                qkv_ref[to, 2 * D :] = v[:, :D]
-                ex_ref[to, :] = v[:, D : D + EX]
-                turn_ref[to, :] = v[:, D + EX :]
+        one, two = slots_of(info, piece)
+        qkv_ref[to, : 2 * D] = at_slot(a1, g1, one)
+        v = at_slot(a2, g2, two)
+        qkv_ref[to, 2 * D :] = v[:, :D]
+        ex_ref[to, :] = v[:, D : D + EX]
+        turn_ref[to, :] = v[:, D + EX :]
     for t in range(GROUP):
         out_ref[:, 256 * t : 256 * t + 256] = turn_ref[:, 256 * t : 256 * t + 256].T
     vec_ref[...] = ex_ref[...].T
 
 
-def gather_plane(parts):
+def stack_kernel(a1, g1, a2, g2, one, two):
+    rows = a1.shape[0]
+    for own, got, out in ((a1, g1, one), (a2, g2, two)):
+        out[:rows, :] = own[...]
+        out[rows:, :] = got[...]
+
+
+def gather_plane(parts, name, gates=((), (), ())):
     for step in (3, 2, 1, 0):
         got = [send(p, CUBE[SPLITS[i][step][0]]) for i, p in enumerate(parts)]
+        four = (parts[0], got[0], parts[1], got[1])
+        yield four
         if step == 0:
-            return parts[0], got[0], parts[1], got[1]
-        parts = [jnp.concatenate([p, g], axis=0) for p, g in zip(parts, got)]
+            return
+        parts = call(
+            stack_kernel,
+            "stack_" + name,
+            [VMEM] * 4,
+            [shaped(2 * p.shape[0], p.shape[1]) for p in parts],
+            (after(four[0], *gates[3 - step]()), *four[1:]),
+            limit=16,
+        )
 
 
 def after(value, *earlier):
@@ -866,82 +896,122 @@
         + [((first + 1) // 2) % 2, first // 2, ((second + 1) // 2) % 2, second // 2]
     ).astype(jnp.int32)
     near = send(tokens, ZNEAR)
-    sibling = send(tokens, SIBLING)
-    qkv_parts = pick_qkv(info, qkv_weight)
-    far = (None, SIBLING, ZFAR, ZFAR_SIBLING)
-    qkv_ws = [b if p is None else send(b, p) for b, p in zip(qkv_parts, far)]
-    vs = gather_group(
-        pack(attn_norm_gain, attn_norm_shift, mlp_norm_gain, mlp_norm_shift, after(qkv_bias, qkv_parts[0]))
-    )
+    own_w, sibling_w, far_w = pick_qkv(info, qkv_weight)
+    far_w = send(far_w, ZFAR)
     cos, sin = tables(info)
-    gate_up_parts = pick_gate_up(info, after(gate_up_weight, vs[0]))
-    near = after(near, cos, gate_up_parts[0])
-    xs = (tokens, near, sibling, send(near, SIBLING))
+    gate_up_parts = pick_gate_up(info, after(gate_up_weight, own_w))
+    vec = pack(
+        attn_norm_gain, attn_norm_shift, mlp_norm_gain, mlp_norm_shift, after(qkv_bias, cos, gate_up_parts[0])
+    )
+    near_vec = send(vec, ZNEAR)
+    near = after(near, near_vec)
+    xs = (tokens, near, send(tokens, SIBLING), send(near, SIBLING))
+    vs = (vec, near_vec, send(vec, SIBLING), send(near_vec, SIBLING))
+    qkv_ws = (own_w, send(sibling_w, SIBLING), far_w, send(far_w[ROWS:], SIBLING))
+    gs = gather_group(after(cotangent, near))
     gate_up_ws = [
         gate_up_parts[0],
         send(after(gate_up_parts[1], near), SIBLING),
-        send(after(gate_up_parts[2], *qkv_ws[2:]), ZFAR),
-        send(after(gate_up_parts[3], near), ZNEAR_SIBLING),
+        send(after(gate_up_parts[2], far_w), ZFAR),
     ]
+    gate_up_ws.append(send(after(gate_up_parts[3], gate_up_ws[2]), ZFAR_SIBLING))
 
     hidden, qkv, qkv_w, norms = project(info, xs, vs, qkv_ws, cos, sin)
-    mixed, lse, low, up = attend(info, qkv, out_weight)
-    gs = gather_group(after(cotangent, gate_up_ws[3]))
+    m0, lse0 = attend_first(info, qkv)
+    m1, lse1, low, up = attend_second(info, qkv, m0, out_weight)
+    up = after(up, gate_up_ws[1], gate_up_ws[2], gs[1])
     own, near = scatter_group(low, up)
-    near = after(near, gate_up_ws[2], gs[1])
     mid, hid_own = middle_of(tokens, own, send(near, ZNEAR), norms)
-    hs = gather_group(hid_own)
+    hs = gather_group(after(hid_own, gate_up_ws[3]))
     act, dgu, gh_low, gh_up, out_low, out_up = feed(info, hs, gs, gate_up_ws, down_weight)
 
     gh_own, gh_near = scatter_group(gh_low, gh_up)
     mlp_halves = mlp_weights(info, hs, gs, after(dgu, gh_near), act)
+    out_got = send(after(out_up, gh_near), SIBLING)
+    o_own, o_near = scatter_group_onto(mid, out_low, out_got)
+    gh_own = after(gh_own, o_near)
     grad_mid, branch_own, sums_m = norm_back(gh_own, send(gh_near, ZNEAR), mid, cotangent, norms, 2)
-    branch = gather_group(branch_own)
-
-    dqkv0 = attend_back(0, info, qkv, branch, out_weight, lse, cos, sin)
-    dqkv1 = attend_back(1, after(info, dqkv0), qkv, branch, out_weight, lse, cos, sin)
+    branch = gather_group(after(branch_own, mlp_halves[0]))
+
+    ready = {}
+    mlp_sums = scatter_plane(
+        info,
+        mlp_halves,
+        "mlp",
+        (
+            lambda: (),
+            lambda: (branch[2], branch[3]),
+            lambda: (ready["dqkv0"],),
+            lambda: (ready["dqkv1"],),
+            lambda: (),
+        ),
+    )
+    dqkv0 = attend_back(0, after(info, next(mlp_sums)), qkv, branch, out_weight, lse0, cos, sin)
+    ready["dqkv0"] = dqkv0
+    dqkv1 = attend_back(1, after(info, next(mlp_sums)), qkv, branch, out_weight, lse1, cos, sin)
+    ready["dqkv1"] = dqkv1
     dqkvs = (dqkv0, dqkv1)
-    ga_low, ga_up, sums_a = hidden_back(dqkvs, qkv_w, xs)
-    attn_halves = attn_weights(info, hidden, dqkvs, mixed, branch, after(sums_a, ga_low), sums_m)
-
-    mlp_gates = ((branch_own,), (branch[1],), (dqkv0,), (dqkv1,), (ga_low,))
-    mlp_piece = scatter_plane(info, mlp_halves, "mlp", mlp_gates)
-    mlp_blocks, mlp_kept = share(info, mlp_piece, 2 * FFP, "mlp", (attn_halves[0],))
-    mlp_piece = call(
-        join_mlp_kernel,
-        "join_mlp",
-        [SMEM] + [VMEM] * 5,
-        shaped(16, 3 * GROUP * FFP),
-        (info, *mlp_blocks, mlp_kept),
-        limit=16,
-    )
-    mlp_all = lax.all_gather(mlp_piece, AXES, axis=0, axis_index_groups=PLANES, tiled=True)
-
-    o_own, o_near = scatter_group(out_low, after(out_up, gh_near))
-    ga_own, ga_near = scatter_group(ga_low, ga_up)
-    ga_other = send(after(ga_near, attn_halves[0]), ZNEAR)
-    o_other = send(after(o_near, attn_halves[0]), ZNEAR)
-    attn_gates = ((), (mlp_piece,), (), (ga_other,), (o_other,))
-    attn_piece = scatter_plane(info, attn_halves, "attn", attn_gates)
-    attn_blocks, attn_kept = share(info, attn_piece, 768 + EX, "attn")
+    ga_low, ga_up = hidden_back((dqkv0, after(dqkv1, next(mlp_sums))), qkv_w)
+    attn_halves = attn_weights(
+        after(info, ga_low), hidden, dqkvs, qkv_w, (m0, m1), branch, norms, sums_m
+    )
+    mlp_piece = next(mlp_sums)
+    ga_own, ga_near = scatter_group(after(ga_low, mlp_piece), ga_up)
+    mlp_blocks, mlp_kept = share(info, mlp_piece, 2 * FFP, "mlp", (ga_near,))
+    attn_sums = scatter_plane(
+        info,
+        attn_halves,
+        "attn",
+        (
+            lambda: (ga_near,),
+            lambda: mlp_blocks[1:],
+            lambda: ready["got0"],
+            lambda: (*ready["got1"], tokens_grad),
+            lambda: ready["got2"],
+        ),
+    )
+    sum0 = next(attn_sums)
+    ga_other = send(after(ga_near, sum0), ZNEAR)
+    (tokens_grad,) = norm_back(ga_own, ga_other, tokens, grad_mid, norms, 0)
+    mlp_all = gather_plane(
+        call(
+            join_mlp_kernel,
+            "join_mlp",
+            [SMEM] + [VMEM] * 5,
+            [shaped(16, 6 * FFP), shaped(16, 6 * FFP)],
+            (after(info, sum0), *mlp_blocks, mlp_kept),
+            limit=16,
+        ),
+        "mlp",
+        (lambda: (sum1,), lambda: (sum2,), lambda: (attn_piece,)),
+    )
+    ready["got0"] = next(mlp_all)[1::2]
+    sum1 = next(attn_sums)
+    ready["got1"] = next(mlp_all)[1::2]
+    sum2 = next(attn_sums)
+    ready["got2"] = next(mlp_all)[1::2]
+    attn_piece = next(attn_sums)
+    mlp_four = next(mlp_all)
+    attn_blocks, attn_kept = share(info, attn_piece, 768 + EX, "attn", (mlp_four[0],))
     pieces = call(
         join_attn_kernel,
         "join_attn",
         [SMEM] + [VMEM] * 5,
         [shaped(16, 2 * D), shaped(16, 2 * D + EX)],
-        (info, *attn_blocks, attn_kept),
+        (after(info, mlp_four[1], mlp_four[3]), *attn_blocks, attn_kept),
         limit=16,
     )
-    (tokens_grad,) = norm_back(ga_own, ga_other, tokens, grad_mid, norms, 0)
-    layer_out = layer_out_of(mid, o_own, o_other)
+    *_, attn_four = gather_plane(
+        pieces, "attn", (lambda: (), lambda: (), lambda: ())
+    )
 
     grad_gate_up, grad_down = call(
         finish_mlp_kernel,
         "finish_mlp",
-        [SMEM, VMEM],
+        [SMEM] + [VMEM] * 4,
         [shaped(ROWS, 2 * FF, dtype=F32), shaped(FFS, D, dtype=F32)],
-        (info, mlp_all),
-        us=5,
+        (info, *mlp_four),
+        limit=30,
         scratch_shapes=[pltpu.VMEM((ROWS, GROUP * FFP), F32)],
     )
     grad_qkv, grad_out, vec = call(
@@ -949,10 +1019,11 @@
         "finish_attn",
         [SMEM] + [VMEM] * 4,
         [shaped(ROWS, 3 * D, dtype=F32), shaped(256, D, dtype=F32), shaped(EX, ROWS, dtype=F32)],
-        (after(info, grad_down), *gather_plane(pieces)),
-        us=4,
+        (after(info, grad_down), *attn_four),
+        limit=24,
         scratch_shapes=[pltpu.VMEM((ROWS, D), F32), pltpu.VMEM((ROWS, EX), F32)],
     )
+    layer_out = layer_out_of(after(o_own, grad_qkv), send(after(o_near, pieces[0]), ZNEAR))
     grad_bias = lax.dynamic_slice_in_dim(vec[8:20].reshape(3 * D), 768 * me, 768, 0)
     return (
         layer_out,

time: 337 us -> 286 us (0.85)
  local copies, waits for them, and re-layouts: 25.6 us -> 9.77 us
  between operations: 15.5 us -> 1.86 us
  Pallas kernels: 92.6 us -> 81.7 us
  waiting for transfers between devices: 130 us -> 121 us
    unnamed x138 -> x32, local copies, waits for them, and re-layouts: 22.8 us -> 8.41 us
    pallas_call x34 -> x41, Pallas kernels: 92.6 us -> 81.7 us  [call(): pl.pallas_call(kernel, in_specs=in_specs, out_shape=out_shape, compiler_p...]
    ppermute x61 -> x69, waiting for transfers between devices: 130 us -> 121 us  [send(): return lax.ppermute(value, AXES, perm)]
    ppermute x61 -> x69, starting transfers between devices: 68.2 us -> 66.7 us  [send(): return lax.ppermute(value, AXES, perm)]
  transfers between devices with their start and end apart: 62 -> 69, of which waited for: 33 -> 36; matrix products, arithmetic and copies ran while one was open for 2% -> 0% of each run, Pallas kernels for 20% -> 20%
where the time goes in v2:
time: 286 us; the launch traced here: 281 us
  waiting for transfers between devices  121 us (42%)
  Pallas kernels  81.7 us (29%)
  starting transfers between devices  66.7 us (23%)
  local copies, waits for them, and re-layouts  9.77 us (3%)
    ppermute x69, waiting for transfers between devices, send(): return lax.ppermute(value, AXES, perm)  121 us
    pallas_call x41, Pallas kernels, call(): pl.pallas_call(kernel, in_specs=in_specs, out_shape=out_shape, compiler_p...  81.7 us
    ppermute x69, starting transfers between devices, send(): return lax.ppermute(value, AXES, perm)  66.7 us
    unnamed x32, local copies, waits for them, and re-layouts  8.41 us
  transfers between devices with their start and end apart: 69, of which 36 were waited for; matrix products, arithmetic and copies ran while one was open for 0% of the time, Pallas kernels for 20%

profile of v2, /device:TPU:0, one launch (start us, length us, event | category | flops | bytes accessed | tf_op | source)
XLA Modules:
  0.0 280.6 jit_solution(4818658737717049744)
XLA Ops:
  3.2 4.2 %collective-permute-start.7 = (bf16[512,768]{1,0:T(8,128)(2,1)S(1)}, bf16[512,768]{1,0:T(8,128)(2,1)S(1)}, u32[]{:S(2)}, u32[]{:S(2)}) collective-permute-start(bf16[512,768]{1,0:T(8,128)(2,1)S(1)} %get-tuple-element.159), channel_id=1, source_target_pairs={{0,66},{1,67},{2,64},{3,65},{4,70},{5,71},{6,68},{7,69},{8,74},{9,... | collective-permute-start | bytes 2359304 | tf_op jit(solution)/shard_map/ppermute | solution.py:69
  7.9 2.5 tables.1
  10.4 1.8 copy-done.4
  13.6 2.1 collective-permute-start.1
  15.7 5.8 %collective-permute-done.1.v1 = bf16[16,1024]{1,0:T(8,128)(2,1)S(1)} collective-permute-done((bf16[16,1024]{1,0:T(8,128)(2,1)S(1)}, bf16[16,1024]{1,0:T(8,128)(2,1)S(1)}, u32[]{:S(2)}, u32[]{:S(2)}) %collective-permute-start.1) | collective-permute-done | bytes 32800 | tf_op jit(solution)/shard_map/ppermute | solution.py:69
  21.5 3.4 %collective-permute-done.7.w2 = bf16[512,768]{1,0:T(8,128)(2,1)S(1)} collective-permute-done((bf16[512,768]{1,0:T(8,128)(2,1)S(1)}, bf16[512,768]{1,0:T(8,128)(2,1)S(1)}, u32[]{:S(2)}, u32[]{:S(2)}) %collective-permute-start.7) | collective-permute-done | bytes 786464 | tf_op jit(solution)/shard_map/ppermute | solution.py:69
  24.9 3.0 %collective-permute-start.10 = (bf16[256,1536]{1,0:T(8,128)(2,1)S(1)}, bf16[256,1536]{1,0:T(8,128)(2,1)S(1)}, u32[]{:S(2)}, u32[]{:S(2)}) collective-permute-start(bf16[256,1536]{1,0:T(8,128)(2,1)S(1)} %get-tuple-element.168), channel_id=1, source_target_pairs={{0,66},{1,67},{2,64},{3,65},{4,70},{5,71},{6,68},{7,69},{8,74},{9,... | collective-permute-start | bytes 2359304 | tf_op jit(solution)/shard_map/ppermute | solution.py:69
  32.8 4.3 %project.1 = (bf16[1024,1024]{1,0:T(8,128)(2,1)S(1)}, bf16[1024,768]{1,0:T(8,128)(2,1)S(1)}, bf16[1024,768]{1,0:T(8,128)(2,1)S(1)}, f32[8,1024]{1,0:T(8,128)S(1)}) custom-call(s32[9]{0:T(128)S(1)} %stack.39.info, bf16[256,1024]{1,0:T(8,128)(2,1)S(1)} %copy-done.2, bf16[256,1024]{1,0:T(8,128)(2,1)S(1)} %collective-permute-done.x1, ...), custom_call_target="tpu_custom_call" | custom-call | tf_op jit(solution)/shard_map/project/pallas_call | solution.py:94
  37.1 3.0 %attend_first.1 = (bf16[1024,128]{1,0:T(8,128)(2,1)S(1)}, f32[2,1024]{1,0:T(2,128)S(1)}) custom-call(s32[9]{0:T(128)S(1)} %stack.39.info, bf16[1024,768]{1,0:T(8,128)(2,1)S(1)} %get-tuple-element.161.qkv_ref), custom_call_target="tpu_custom_call" | custom-call | tf_op jit(solution)/shard_map/attend_first/pallas_call | solution.py:94
  40.2 3.7 %attend_second.1 = (bf16[1024,128]{1,0:T(8,128)(2,1)S(1)}, f32[2,1024]{1,0:T(2,128)S(1)}, bf16[512,1024]{1,0:T(8,128)(2,1)S(1)}, bf16[512,1024]{1,0:T(8,128)(2,1)S(1)}) custom-call(s32[9]{0:T(128)S(1)} %stack.39.info, bf16[1024,768]{1,0:T(8,128)(2,1)S(1)} %get-tuple-element.161.qkv_ref, bf16[1024,128]{1,0:T(8,128)(2,1)S(1)} %get-tuple-element.162.m0, ...), custom_call_target="tpu_custom_call" | custom-call | tf_op jit(solution)/shard_map/attend_second/pallas_call | solution.py:94
  44.9 2.7 collective-permute-start.14
  48.8 13.0 %collective-permute-done.13.other_ref = bf16[256,1024]{1,0:T(8,128)(2,1)S(1)} collective-permute-done((bf16[256,1024]{1,0:T(8,128)(2,1)S(1)}, bf16[256,1024]{1,0:T(8,128)(2,1)S(1)}, u32[]{:S(2)}, u32[]{:S(2)}) %collective-permute-start.13) | collective-permute-done | bytes 524320 | tf_op jit(solution)/shard_map/ppermute | solution.py:69
  62.3 2.9 %collective-permute-done.14.w3 = bf16[256,1536]{1,0:T(8,128)(2,1)S(1)} collective-permute-done((bf16[256,1536]{1,0:T(8,128)(2,1)S(1)}, bf16[256,1536]{1,0:T(8,128)(2,1)S(1)}, u32[]{:S(2)}, u32[]{:S(2)}) %collective-permute-start.14) | collective-permute-done | bytes 786464 | tf_op jit(solution)/shard_map/ppermute | solution.py:69
  66.3 13.3 %collective-permute-done.15.h1 = bf16[256,1024]{1,0:T(8,128)(2,1)S(1)} collective-permute-done((bf16[256,1024]{1,0:T(8,128)(2,1)S(1)}, bf16[256,1024]{1,0:T(8,128)(2,1)S(1)}, u32[]{:S(2)}, u32[]{:S(2)}) %collective-permute-start.15) | collective-permute-done | bytes 524320 | tf_op jit(solution)/shard_map/ppermute | solution.py:69
  80.0 1.9 collective-permute-done.17.h3
  81.9 14.3 %feed.1 = (bf16[1024,768]{1,0:T(8,128)(2,1)S(1)}, bf16[1024,1536]{1,0:T(8,128)(2,1)}, bf16[512,1024]{1,0:T(8,128)(2,1)S(1)}, bf16[512,1024]{1,0:T(8,128)(2,1)S(1...) custom-call(s32[9]{0:T(128)S(1)} %stack.39.info, bf16[256,1024]{1,0:T(8,128)(2,1)S(1)} %get-tuple-element.178.h0, ...), custom_call_target="tpu_custom_call" | custom-call | tf_op jit(solution)/shard_map/feed/pallas_call | solution.py:94
  96.4 2.5 collective-permute-done.20.got_ref
  99.7 1.9 copy-done.3
  101.6 8.4 %mlp_weights.1 = (bf16[256,2304]{1,0:T(8,128)(2,1)S(1)}, bf16[256,2304]{1,0:T(8,128)(2,1)S(1)}, bf16[256,2304]{1,0:T(8,128)(2,1)S(1)}, bf16[256,2304]{1,0:T(8,128)(2,1)S(1)}) custom-call(s32[9]{0:T(128)S(1)} %stack.39.info, bf16[256,1024]{1,0:T(8,128)(2,1)S(1)} %get-tuple-element.178.h0, bf16[256,1024]{1,0:T(8,128)(2,1)S(1)} %collective-permute-done.15.h1, ...), custom_call_target="tpu_custom_call" | custom-call | tf_op jit(solution)/shard_map/mlp_weights/pallas_call | solution.py:94
  111.6 2.2 collective-permute-start.27
  117.0 1.8 collective-permute-start.24
  118.8 11.8 %collective-permute-done.24.b1 = bf16[256,1024]{1,0:T(8,128)(2,1)S(1)} collective-permute-done((bf16[256,1024]{1,0:T(8,128)(2,1)S(1)}, bf16[256,1024]{1,0:T(8,128)(2,1)S(1)}, u32[]{:S(2)}, u32[]{:S(2)}) %collective-permute-start.24) | collective-permute-done | bytes 524320 | tf_op jit(solution)/shard_map/ppermute | solution.py:69
  130.6 1.9 collective-permute-done.25.b3
  133.6 2.2 collective-permute-start.28
  135.8 6.1 %attend_back.2.d0 = bf16[1024,384]{1,0:T(8,128)(2,1)S(1)} custom-call(s32[9]{0:T(128)S(1)} %stack.39.info, bf16[1024,768]{1,0:T(8,128)(2,1)S(1)} %get-tuple-element.161.qkv_ref, bf16[256,1024]{1,0:T(8,128)(2,1)S(1)} %get-tuple-element.194.b0, bf16[256,1024]{1,0:T(8,128)(2,1)S(1)} %collective-permute-done.24.b1, ...), custom_call_target="tpu_custom_call" | custom-call | tf_op jit(solution)/shard_map/attend_back/pallas_call | solution.py:94
  141.9 2.8 collective-permute-done.28.g1
  149.0 6.1 %attend_back.3.d1 = bf16[1024,384]{1,0:T(8,128)(2,1)S(1)} custom-call(s32[9]{0:T(128)S(1)} %stack.39.info, bf16[1024,768]{1,0:T(8,128)(2,1)S(1)} %get-tuple-element.161.qkv_ref, bf16[256,1024]{1,0:T(8,128)(2,1)S(1)} %get-tuple-element.194.b0, bf16[256,1024]{1,0:T(8,128)(2,1)S(1)} %collective-permute-done.24.b1, ...), custom_call_target="tpu_custom_call" | custom-call | tf_op jit(solution)/shard_map/attend_back/pallas_call | solution.py:94
  156.7 1.9 hidden_back.1
  160.2 4.3 %attn_weights.1 = (bf16[256,1152]{1,0:T(8,128)(2,1)S(1)}, bf16[256,1152]{1,0:T(8,128)(2,1)S(1)}, bf16[256,1152]{1,0:T(8,128)(2,1)S(1)}, bf16[256,1152]{1,0:T(8,128)(2,1)S(1)}) custom-call(s32[9]{0:T(128)S(1)} %stack.39.info, bf16[1024,1024]{1,0:T(8,128)(2,1)S(1)} %get-tuple-element.218.h_ref, bf16[1024,384]{1,0:T(8,128)(2,1)S(1)} %attend_back.2.d0, ...), custom_call_target="tpu_custom_call" | custom-call | tf_op jit(solution)/shard_map/attn_weights/pallas_call | solution.py:94
  166.9 3.8 %collective-permute-start.35 = (bf16[64,2304]{1,0:T(8,128)(2,1)S(1)}, bf16[64,2304]{1,0:T(8,128)(2,1)S(1)}, u32[]{:S(2)}, u32[]{:S(2)}) collective-permute-start(bf16[64,2304]{1,0:T(8,128)(2,1)S(1)} %piece_mlp.1.a_ref), channel_id=1, source_target_pairs={{0,64},{1,65},{2,66},{3,67},{4,68},{5,69},{6,70},{7,71},{8,72},{9,... | collective-permute-start | bytes 884744 | tf_op jit(solution)/shard_map/ppermute | solution.py:69
  170.8 6.4 %collective-permute-done.35.g_ref = bf16[64,2304]{1,0:T(8,128)(2,1)S(1)} collective-permute-done((bf16[64,2304]{1,0:T(8,128)(2,1)S(1)}, bf16[64,2304]{1,0:T(8,128)(2,1)S(1)}, u32[]{:S(2)}, u32[]{:S(2)}) %collective-permute-start.35) | collective-permute-done | bytes 294944 | tf_op jit(solution)/shard_map/ppermute | solution.py:69
  180.0 2.3 collective-permute-done.37.r2
  184.0 1.8 collective-permute-start.43
  188.7 1.9 collective-permute-start.41
  191.7 3.4 %collective-permute-done.41.g1 = bf16[16,4608]{1,0:T(8,128)(2,1)S(1)} collective-permute-done((bf16[16,4608]{1,0:T(8,128)(2,1)S(1)}, bf16[16,4608]{1,0:T(8,128)(2,1)S(1)}, u32[]{:S(2)}, u32[]{:S(2)}) %collective-permute-start.41) | collective-permute-done | bytes 147488 | tf_op jit(solution)/shard_map/ppermute | solution.py:69
  199.4 1.8 collective-permute-start.49
  203.3 2.3 collective-permute-done.46.g2
  211.2 7.8 %collective-permute-done.50.g1 = bf16[64,4608]{1,0:T(8,128)(2,1)S(1)} collective-permute-done((bf16[64,4608]{1,0:T(8,128)(2,1)S(1)}, bf16[64,4608]{1,0:T(8,128)(2,1)S(1)}, u32[]{:S(2)}, u32[]{:S(2)}) %collective-permute-start.50) | collective-permute-done | bytes 589856 | tf_op jit(solution)/shard_map/ppermute | solution.py:69
  221.7 3.0 %collective-permute-start.56 = (bf16[64,1152]{1,0:T(8,128)(2,1)S(1)}, bf16[64,1152]{1,0:T(8,128)(2,1)S(1)}, u32[]{:S(2)}, u32[]{:S(2)}) collective-permute-start(bf16[64,1152]{1,0:T(8,128)(2,1)S(1)} %piece_attn.1.a_ref), channel_id=1, source_target_pairs={{0,64},{1,65},{2,66},{3,67},{4,68},{5,69},{6,70},{7,71},{8,72},{9,... | collective-permute-start | bytes 442376 | tf_op jit(solution)/shard_map/ppermute | solution.py:69
  224.7 3.7 %collective-permute-done.56.g_ref = bf16[64,1152]{1,0:T(8,128)(2,1)S(1)} collective-permute-done((bf16[64,1152]{1,0:T(8,128)(2,1)S(1)}, bf16[64,1152]{1,0:T(8,128)(2,1)S(1)}, u32[]{:S(2)}, u32[]{:S(2)}) %collective-permute-start.56) | collective-permute-done | bytes 147488 | tf_op jit(solution)/shard_map/ppermute | solution.py:69
  230.9 4.7 %collective-permute-done.54.g1 = bf16[128,4608]{1,0:T(8,128)(2,1)S(1)} collective-permute-done((bf16[128,4608]{1,0:T(8,128)(2,1)S(1)}, bf16[128,4608]{1,0:T(8,128)(2,1)S(1)}, u32[]{:S(2)}, u32[]{:S(2)}) %collective-permute-start.54) | collective-permute-done | bytes 1179680 | tf_op jit(solution)/shard_map/ppermute | solution.py:69
  235.6 1.8 collective-permute-done.55.g2
  240.6 4.0 %collective-permute-done.60.g1 = bf16[16,2048]{1,0:T(8,128)(2,1)S(1)} collective-permute-done((bf16[16,2048]{1,0:T(8,128)(2,1)S(1)}, bf16[16,2048]{1,0:T(8,128)(2,1)S(1)}, u32[]{:S(2)}, u32[]{:S(2)}) %collective-permute-start.60) | collective-permute-done | bytes 65568 | tf_op jit(solution)/shard_map/ppermute | solution.py:69
  246.3 6.2 %collective-permute-done.62.g1 = bf16[32,2048]{1,0:T(8,128)(2,1)S(1)} collective-permute-done((bf16[32,2048]{1,0:T(8,128)(2,1)S(1)}, bf16[32,2048]{1,0:T(8,128)(2,1)S(1)}, u32[]{:S(2)}, u32[]{:S(2)}) %collective-permute-start.62) | collective-permute-done | bytes 131104 | tf_op jit(solution)/shard_map/ppermute | solution.py:69
  254.8 5.9 %collective-permute-done.64.g1 = bf16[64,2048]{1,0:T(8,128)(2,1)S(1)} collective-permute-done((bf16[64,2048]{1,0:T(8,128)(2,1)S(1)}, bf16[64,2048]{1,0:T(8,128)(2,1)S(1)}, u32[]{:S(2)}, u32[]{:S(2)}) %collective-permute-start.64) | collective-permute-done | bytes 262176 | tf_op jit(solution)/shard_map/ppermute | solution.py:69
  266.0 5.3 %finish_mlp.1 = (f32[256,5632]{1,0:T(8,128)}, f32[704,1024]{1,0:T(8,128)}) custom-call(s32[9]{0:T(128)S(1)} %stack.39.info, bf16[128,4608]{1,0:T(8,128)(2,1)S(1)} %get-tuple-element.268.a1, bf16[128,4608]{1,0:T(8,128)(2,1)S(1)} %collective-permute-done.54.g1, bf16[128,4608]{1,0:T(8,128)(2,1)S(1)} %get-tuple-element.269.a2, bf16[128,4608]{1,0:T(8,128)(2,1)S(1)} %copy-done.8), custom_call_target="tpu_custom_call" | custom-call | tf_op jit(solution)/shard_map/finish_mlp/pallas_call | solution.py:94
  273.0 4.0 %finish_attn.1 = (f32[256,3072]{1,0:T(8,128)}, f32[256,1024]{1,0:T(8,128)}, f32[128,256]{1,0:T(8,128)S(1)}) custom-call(s32[9]{0:T(128)S(1)} %stack.39.info, bf16[128,2048]{1,0:T(8,128)(2,1)} %get-tuple-element.285.a1, bf16[128,2048]{1,0:T(8,128)(2,1)} %collective-permute-done.66.g1, bf16[128,2176]{1,0:T(8,128)(2,1)} %get-tuple-element.286.a2, ...), custom_call_target="tpu_custom_call" | custom-call | tf_op jit(solution)/shard_map/finish_attn/pallas_call | solution.py:94
  278.3 1.9 layer_out.1
  (169 shorter events, 70.5 us)
Async XLA Ops:
  3.2 21.7 %collective-permute-start.7 = (bf16[512,768]{1,0:T(8,128)(2,1)S(1)}, bf16[512,768]{1,0:T(8,128)(2,1)S(1)}, u32[]{:S(2)}, u32[]{:S(2)}) collective-permute-start(bf16[512,768]{1,0:T(8,128)(2,1)S(1)} %get-tuple-element.159), channel_id=1, source_target_pairs={{0,66},{1,67},{2,64},{3,65},{4,70},{5,71},{6,68},{7,69},{8,74},{9,... | collective-permute-start | bytes 2359304 | tf_op jit(solution)/shard_map/ppermute | solution.py:69
  7.4 14.1 %collective-permute-start = (bf16[256,1024]{1,0:T(8,128)(2,1)S(1)}, bf16[256,1024]{1,0:T(8,128)(2,1)S(1)}, u32[]{:S(2)}, u32[]{:S(2)}) collective-permute-start(bf16[256,1024]{1,0:T(8,128)(2,1)S(1)} %copy-done.2), channel_id=1, source_target_pairs={{0,2},{1,3},{2,0},{3,1},{4,6},{5,7},{6,4},{7,5},{8,10},{9,11},{10,... | collective-permute-start | bytes 1572872 | tf_op jit(solution)/shard_map/ppermute | solution.py:69
  7.4 23.1 %collective-permute-start.2 = (bf16[256,1024]{1,0:T(8,128)(2,1)S(1)}, bf16[256,1024]{1,0:T(8,128)(2,1)S(1)}, u32[]{:S(2)}, u32[]{:S(2)}) collective-permute-start(bf16[256,1024]{1,0:T(8,128)(2,1)S(1)} %copy-done.2), channel_id=1, source_target_pairs={{0,1},{1,0},{2,3},{3,2},{4,5},{5,4},{6,7},{7,6},{8,9},{9,8},{10,11... | collective-permute-start | bytes 1572872 | tf_op jit(solution)/shard_map/ppermute | solution.py:69
  7.4 23.1 %collective-permute-start.6 = (bf16[256,768]{1,0:T(8,128)(2,1)S(1)}, bf16[256,768]{1,0:T(8,128)(2,1)S(1)}, u32[]{:S(2)}, u32[]{:S(2)}) collective-permute-start(bf16[256,768]{1,0:T(8,128)(2,1)S(1)} %get-tuple-element.158), channel_id=1, source_target_pairs={{0,1},{1,0},{2,3},{3,2},{4,5},{5,4},{6,7},{7,6},{8,9},{9,8},{10,11... | collective-permute-start | bytes 1179656 | tf_op jit(solution)/shard_map/ppermute | solution.py:69
  13.6 7.9 %collective-permute-start.1 = (bf16[16,1024]{1,0:T(8,128)(2,1)S(1)}, bf16[16,1024]{1,0:T(8,128)(2,1)S(1)}, u32[]{:S(2)}, u32[]{:S(2)}) collective-permute-start(bf16[16,1024]{1,0:T(8,128)(2,1)S(1)} %pack.1.v0), channel_id=1, source_target_pairs={{0,2},{1,3},{2,0},{3,1},{4,6},{5,7},{6,4},{7,5},{8,10},{9,11},{10,... | collective-permute-start | bytes 98312 | tf_op jit(solution)/shard_map/ppermute | solution.py:69
  21.5 23.2 %collective-permute-start.9 = (bf16[256,1536]{1,0:T(8,128)(2,1)S(1)}, bf16[256,1536]{1,0:T(8,128)(2,1)S(1)}, u32[]{:S(2)}, u32[]{:S(2)}) collective-permute-start(bf16[256,1536]{1,0:T(8,128)(2,1)S(1)} %get-tuple-element.166), channel_id=1, source_target_pairs={{0,1},{1,0},{2,3},{3,2},{4,5},{5,4},{6,7},{7,6},{8,9},{9,8},{10,11... | collective-permute-start | bytes 2359304 | tf_op jit(solution)/shard_map/ppermute | solution.py:69
  24.9 19.9 %collective-permute-start.10 = (bf16[256,1536]{1,0:T(8,128)(2,1)S(1)}, bf16[256,1536]{1,0:T(8,128)(2,1)S(1)}, u32[]{:S(2)}, u32[]{:S(2)}) collective-permute-start(bf16[256,1536]{1,0:T(8,128)(2,1)S(1)} %get-tuple-element.168), channel_id=1, source_target_pairs={{0,66},{1,67},{2,64},{3,65},{4,70},{5,71},{6,68},{7,69},{8,74},{9,... | collective-permute-start | bytes 2359304 | tf_op jit(solution)/shard_map/ppermute | solution.py:69
  30.5 14.2 %collective-permute-start.11 = (bf16[256,1024]{1,0:T(8,128)(2,1)S(1)}, bf16[256,1024]{1,0:T(8,128)(2,1)S(1)}, u32[]{:S(2)}, u32[]{:S(2)}) collective-permute-start(bf16[256,1024]{1,0:T(8,128)(2,1)S(1)} %copy-done), channel_id=1, source_target_pairs={{0,2},{1,3},{2,0},{3,1},{4,6},{5,7},{6,4},{7,5},{8,10},{9,11},{10,... | collective-permute-start | bytes 1572872 | tf_op jit(solution)/shard_map/ppermute | solution.py:69
  44.9 20.4 %collective-permute-start.14 = (bf16[256,1536]{1,0:T(8,128)(2,1)S(1)}, bf16[256,1536]{1,0:T(8,128)(2,1)S(1)}, u32[]{:S(2)}, u32[]{:S(2)}) collective-permute-start(bf16[256,1536]{1,0:T(8,128)(2,1)S(1)} %get-tuple-element.177), channel_id=1, source_target_pairs={{0,67},{1,66},{2,65},{3,64},{4,71},{5,70},{6,69},{7,68},{8,75},{9,... | collective-permute-start | bytes 2359304 | tf_op jit(solution)/shard_map/ppermute | solution.py:69
  47.9 14.0 %collective-permute-start.13 = (bf16[256,1024]{1,0:T(8,128)(2,1)S(1)}, bf16[256,1024]{1,0:T(8,128)(2,1)S(1)}, u32[]{:S(2)}, u32[]{:S(2)}) collective-permute-start(bf16[256,1024]{1,0:T(8,128)(2,1)S(1)} %get-tuple-element.172), channel_id=1, source_target_pairs={{0,2},{1,3},{2,0},{3,1},{4,6},{5,7},{6,4},{7,5},{8,10},{9,11},{10,... | collective-permute-start | bytes 1572872 | tf_op jit(solution)/shard_map/ppermute | solution.py:69
  65.3 14.3 %collective-permute-start.15 = (bf16[256,1024]{1,0:T(8,128)(2,1)S(1)}, bf16[256,1024]{1,0:T(8,128)(2,1)S(1)}, u32[]{:S(2)}, u32[]{:S(2)}) collective-permute-start(bf16[256,1024]{1,0:T(8,128)(2,1)S(1)} %get-tuple-element.178.h0), channel_id=1, source_target_pairs={{0,2},{1,3},{2,0},{3,1},{4,6},{5,7},{6,4},{7,5},{8,10},{9,11},{10,... | collective-permute-start | bytes 1572872 | tf_op jit(solution)/shard_map/ppermute | solution.py:69
  65.3 14.7 %collective-permute-start.18 = (bf16[256,1024]{1,0:T(8,128)(2,1)S(1)}, bf16[256,1024]{1,0:T(8,128)(2,1)S(1)}, u32[]{:S(2)}, u32[]{:S(2)}) collective-permute-start(bf16[256,1024]{1,0:T(8,128)(2,1)S(1)} %copy-done), channel_id=1, source_target_pairs={{0,1},{1,0},{2,3},{3,2},{4,5},{5,4},{6,7},{7,6},{8,9},{9,8},{10,11... | collective-permute-start | bytes 1572872 | tf_op jit(solution)/shard_map/ppermute | solution.py:69
  65.7 14.2 %collective-permute-start.19 = (bf16[256,1024]{1,0:T(8,128)(2,1)S(1)}, bf16[256,1024]{1,0:T(8,128)(2,1)S(1)}, u32[]{:S(2)}, u32[]{:S(2)}) collective-permute-start(bf16[256,1024]{1,0:T(8,128)(2,1)S(1)} %collective-permute-done.11.g1), channel_id=1, source_target_pairs={{0,1},{1,0},{2,3},{3,2},{4,5},{5,4},{6,7},{7,6},{8,9},{9,8},{10,11... | collective-permute-start | bytes 1572872 | tf_op jit(solution)/shard_map/ppermute | solution.py:69
  65.8 14.2 %collective-permute-start.16 = (bf16[256,1024]{1,0:T(8,128)(2,1)S(1)}, bf16[256,1024]{1,0:T(8,128)(2,1)S(1)}, u32[]{:S(2)}, u32[]{:S(2)}) collective-permute-start(bf16[256,1024]{1,0:T(8,128)(2,1)S(1)} %get-tuple-element.178.h0), channel_id=1, source_target_pairs={{0,1},{1,0},{2,3},{3,2},{4,5},{5,4},{6,7},{7,6},{8,9},{9,8},{10,11... | collective-permute-start | bytes 1572872 | tf_op jit(solution)/shard_map/ppermute | solution.py:69
  99.2 14.7 %collective-permute-start.21 = (bf16[512,1024]{1,0:T(8,128)(2,1)S(1)}, bf16[512,1024]{1,0:T(8,128)(2,1)S(1)}, u32[]{:S(2)}, u32[]{:S(2)}) collective-permute-start(bf16[512,1024]{1,0:T(8,128)(2,1)S(1)} %get-tuple-element.184), channel_id=1, source_target_pairs={{0,1},{1,0},{2,3},{3,2},{4,5},{5,4},{6,7},{7,6},{8,9},{9,8},{10,11... | collective-permute-start | bytes 3145736 | tf_op jit(solution)/shard_map/ppermute | solution.py:69
  99.4 16.7 %collective-permute-start.22 = (bf16[256,1024]{1,0:T(8,128)(2,1)S(1)}, bf16[256,1024]{1,0:T(8,128)(2,1)S(1)}, u32[]{:S(2)}, u32[]{:S(2)}) collective-permute-start(bf16[256,1024]{1,0:T(8,128)(2,1)S(1)} %get-tuple-element.183), channel_id=1, source_target_pairs={{0,2},{1,3},{2,0},{3,1},{4,6},{5,7},{6,4},{7,5},{8,10},{9,11},{10,... | collective-permute-start | bytes 1572872 | tf_op jit(solution)/shard_map/ppermute | solution.py:69
  110.0 22.5 %collective-permute-start.26 = (bf16[256,2304]{1,0:T(8,128)(2,1)S(1)}, bf16[256,2304]{1,0:T(8,128)(2,1)S(1)}, u32[]{:S(2)}, u32[]{:S(2)}) collective-permute-start(bf16[256,2304]{1,0:T(8,128)(2,1)S(1)} %get-tuple-element.196), channel_id=1, source_target_pairs={{0,16},{1,5},{2,18},{3,7},{4,20},{5,1},{6,22},{7,3},{8,24},{9,13},... | collective-permute-start | bytes 3538952 | tf_op jit(solution)/shard_map/ppermute | solution.py:69
  111.6 20.9 %collective-permute-start.27 = (bf16[256,2304]{1,0:T(8,128)(2,1)S(1)}, bf16[256,2304]{1,0:T(8,128)(2,1)S(1)}, u32[]{:S(2)}, u32[]{:S(2)}) collective-permute-start(bf16[256,2304]{1,0:T(8,128)(2,1)S(1)} %get-tuple-element.198), channel_id=1, source_target_pairs={{0,48},{1,13},{2,50},{3,15},{4,52},{5,9},{6,54},{7,11},{8,56},{9,5... | collective-permute-start | bytes 3538952 | tf_op jit(solution)/shard_map/ppermute | solution.py:69
  117.0 13.6 %collective-permute-start.24 = (bf16[256,1024]{1,0:T(8,128)(2,1)S(1)}, bf16[256,1024]{1,0:T(8,128)(2,1)S(1)}, u32[]{:S(2)}, u32[]{:S(2)}) collective-permute-start(bf16[256,1024]{1,0:T(8,128)(2,1)S(1)} %get-tuple-element.194.b0), channel_id=1, source_target_pairs={{0,2},{1,3},{2,0},{3,1},{4,6},{5,7},{6,4},{7,5},{8,10},{9,11},{10,... | collective-permute-start | bytes 1572872 | tf_op jit(solution)/shard_map/ppermute | solution.py:69
  118.8 11.8 %collective-permute-start.23 = (bf16[256,1024]{1,0:T(8,128)(2,1)S(1)}, bf16[256,1024]{1,0:T(8,128)(2,1)S(1)}, u32[]{:S(2)}, u32[]{:S(2)}) collective-permute-start(bf16[256,1024]{1,0:T(8,128)(2,1)S(1)} %get-tuple-element.194.b0), channel_id=1, source_target_pairs={{0,1},{1,0},{2,3},{3,2},{4,5},{5,4},{6,7},{7,6},{8,9},{9,8},{10,11... | collective-permute-start | bytes 1572872 | tf_op jit(solution)/shard_map/ppermute | solution.py:69
  133.6 11.2 %collective-permute-start.28 = (bf16[128,2304]{1,0:T(8,128)(2,1)S(1)}, bf16[128,2304]{1,0:T(8,128)(2,1)S(1)}, u32[]{:S(2)}, u32[]{:S(2)}) collective-permute-start(bf16[128,2304]{1,0:T(8,128)(2,1)S(1)} %get-tuple-element.203), channel_id=1, source_target_pairs={{0,48},{1,13},{2,50},{3,15},{4,52},{5,9},{6,54},{7,11},{8,56},{9,5... | collective-permute-start | bytes 1769480 | tf_op jit(solution)/shard_map/ppermute | solution.py:69
  135.8 9.9 %collective-permute-start.29 = (bf16[128,2304]{1,0:T(8,128)(2,1)S(1)}, bf16[128,2304]{1,0:T(8,128)(2,1)S(1)}, u32[]{:S(2)}, u32[]{:S(2)}) collective-permute-start(bf16[128,2304]{1,0:T(8,128)(2,1)S(1)} %get-tuple-element.205), channel_id=1, source_target_pairs={{0,16},{1,5},{2,18},{3,7},{4,20},{5,1},{6,22},{7,3},{8,24},{9,13},... | collective-permute-start | bytes 1769480 | tf_op jit(solution)/shard_map/ppermute | solution.py:69
  146.5 8.6 %collective-permute-start.30 = (bf16[64,2304]{1,0:T(8,128)(2,1)S(1)}, bf16[64,2304]{1,0:T(8,128)(2,1)S(1)}, u32[]{:S(2)}, u32[]{:S(2)}) collective-permute-start(bf16[64,2304]{1,0:T(8,128)(2,1)S(1)} %get-tuple-element.210), channel_id=1, source_target_pairs={{0,4},{1,17},{2,6},{3,19},{4,0},{5,21},{6,2},{7,23},{8,12},{9,25},... | collective-permute-start | bytes 884744 | tf_op jit(solution)/shard_map/ppermute | solution.py:69
  147.9 8.1 %collective-permute-start.31 = (bf16[64,2304]{1,0:T(8,128)(2,1)S(1)}, bf16[64,2304]{1,0:T(8,128)(2,1)S(1)}, u32[]{:S(2)}, u32[]{:S(2)}) collective-permute-start(bf16[64,2304]{1,0:T(8,128)(2,1)S(1)} %get-tuple-element.212), channel_id=1, source_target_pairs={{0,12},{1,49},{2,14},{3,51},{4,8},{5,53},{6,10},{7,55},{8,4},{9,57... | collective-permute-start | bytes 884744 | tf_op jit(solution)/shard_map/ppermute | solution.py:69
  158.6 6.9 %collective-permute-start.34 = (bf16[512,1024]{1,0:T(8,128)(2,1)S(1)}, bf16[512,1024]{1,0:T(8,128)(2,1)S(1)}, u32[]{:S(2)}, u32[]{:S(2)}) collective-permute-start(bf16[512,1024]{1,0:T(8,128)(2,1)S(1)} %get-tuple-element.226), channel_id=1, source_target_pairs={{0,1},{1,0},{2,3},{3,2},{4,5},{5,4},{6,7},{7,6},{8,9},{9,8},{10,11... | collective-permute-start | bytes 3145736 | tf_op jit(solution)/shard_map/ppermute | solution.py:69
  165.7 17.5 %collective-permute-start.40 = (bf16[256,1152]{1,0:T(8,128)(2,1)S(1)}, bf16[256,1152]{1,0:T(8,128)(2,1)S(1)}, u32[]{:S(2)}, u32[]{:S(2)}) collective-permute-start(bf16[256,1152]{1,0:T(8,128)(2,1)S(1)} %get-tuple-element.237), channel_id=1, source_target_pairs={{0,48},{1,13},{2,50},{3,15},{4,52},{5,9},{6,54},{7,11},{8,56},{9,5... | collective-permute-start | bytes 1769480 | tf_op jit(solution)/shard_map/ppermute | solution.py:69
  166.9 16.2 %collective-permute-start.39 = (bf16[256,1152]{1,0:T(8,128)(2,1)S(1)}, bf16[256,1152]{1,0:T(8,128)(2,1)S(1)}, u32[]{:S(2)}, u32[]{:S(2)}) collective-permute-start(bf16[256,1152]{1,0:T(8,128)(2,1)S(1)} %get-tuple-element.234), channel_id=1, source_target_pairs={{0,16},{1,5},{2,18},{3,7},{4,20},{5,1},{6,22},{7,3},{8,24},{9,13},... | collective-permute-start | bytes 1769480 | tf_op jit(solution)/shard_map/ppermute | solution.py:69
  166.9 10.3 %collective-permute-start.35 = (bf16[64,2304]{1,0:T(8,128)(2,1)S(1)}, bf16[64,2304]{1,0:T(8,128)(2,1)S(1)}, u32[]{:S(2)}, u32[]{:S(2)}) collective-permute-start(bf16[64,2304]{1,0:T(8,128)(2,1)S(1)} %piece_mlp.1.a_ref), channel_id=1, source_target_pairs={{0,64},{1,65},{2,66},{3,67},{4,68},{5,69},{6,70},{7,71},{8,72},{9,... | collective-permute-start | bytes 884744 | tf_op jit(solution)/shard_map/ppermute | solution.py:69
  184.0 11.7 %collective-permute-start.43 = (bf16[128,1152]{1,0:T(8,128)(2,1)S(1)}, bf16[128,1152]{1,0:T(8,128)(2,1)S(1)}, u32[]{:S(2)}, u32[]{:S(2)}) collective-permute-start(bf16[128,1152]{1,0:T(8,128)(2,1)S(1)} %get-tuple-element.245), channel_id=1, source_target_pairs={{0,48},{1,13},{2,50},{3,15},{4,52},{5,9},{6,54},{7,11},{8,56},{9,5... | collective-permute-start | bytes 884744 | tf_op jit(solution)/shard_map/ppermute | solution.py:69
  185.8 9.9 %collective-permute-start.44 = (bf16[128,1152]{1,0:T(8,128)(2,1)S(1)}, bf16[128,1152]{1,0:T(8,128)(2,1)S(1)}, u32[]{:S(2)}, u32[]{:S(2)}) collective-permute-start(bf16[128,1152]{1,0:T(8,128)(2,1)S(1)} %get-tuple-element.247), channel_id=1, source_target_pairs={{0,16},{1,5},{2,18},{3,7},{4,20},{5,1},{6,22},{7,3},{8,24},{9,13},... | collective-permute-start | bytes 884744 | tf_op jit(solution)/shard_map/ppermute | solution.py:69
  186.9 14.3 %collective-permute-start.47 = (bf16[256,1024]{1,0:T(8,128)(2,1)S(1)}, bf16[256,1024]{1,0:T(8,128)(2,1)S(1)}, u32[]{:S(2)}, u32[]{:S(2)}) collective-permute-start(bf16[256,1024]{1,0:T(8,128)(2,1)S(1)} %get-tuple-element.253), channel_id=1, source_target_pairs={{0,2},{1,3},{2,0},{3,1},{4,6},{5,7},{6,4},{7,5},{8,10},{9,11},{10,... | collective-permute-start | bytes 1572872 | tf_op jit(solution)/shard_map/ppermute | solution.py:69
  197.7 7.9 %collective-permute-start.46 = (bf16[32,4608]{1,0:T(8,128)(2,1)S(1)}, bf16[32,4608]{1,0:T(8,128)(2,1)S(1)}, u32[]{:S(2)}, u32[]{:S(2)}) collective-permute-start(bf16[32,4608]{1,0:T(8,128)(2,1)S(1)} %get-tuple-element.251.a2), channel_id=1, source_target_pairs={{0,12},{1,49},{2,14},{3,51},{4,8},{5,53},{6,10},{7,55},{8,4},{9,57... | collective-permute-start | bytes 884744 | tf_op jit(solution)/shard_map/ppermute | solution.py:69
  199.4 7.8 %collective-permute-start.49 = (bf16[64,1152]{1,0:T(8,128)(2,1)S(1)}, bf16[64,1152]{1,0:T(8,128)(2,1)S(1)}, u32[]{:S(2)}, u32[]{:S(2)}) collective-permute-start(bf16[64,1152]{1,0:T(8,128)(2,1)S(1)} %get-tuple-element.258), channel_id=1, source_target_pairs={{0,12},{1,49},{2,14},{3,51},{4,8},{5,53},{6,10},{7,55},{8,4},{9,57... | collective-permute-start | bytes 442376 | tf_op jit(solution)/shard_map/ppermute | solution.py:69
  207.9 11.2 %collective-permute-start.50 = (bf16[64,4608]{1,0:T(8,128)(2,1)S(1)}, bf16[64,4608]{1,0:T(8,128)(2,1)S(1)}, u32[]{:S(2)}, u32[]{:S(2)}) collective-permute-start(bf16[64,4608]{1,0:T(8,128)(2,1)S(1)} %get-tuple-element.267.a1), channel_id=1, source_target_pairs={{0,48},{1,13},{2,50},{3,15},{4,52},{5,9},{6,54},{7,11},{8,56},{9,5... | collective-permute-start | bytes 1769480 | tf_op jit(solution)/shard_map/ppermute | solution.py:69
  209.2 9.9 %collective-permute-start.51 = (bf16[64,4608]{1,0:T(8,128)(2,1)S(1)}, bf16[64,4608]{1,0:T(8,128)(2,1)S(1)}, u32[]{:S(2)}, u32[]{:S(2)}) collective-permute-start(bf16[64,4608]{1,0:T(8,128)(2,1)S(1)} %get-tuple-element.262.a2), channel_id=1, source_target_pairs={{0,16},{1,5},{2,18},{3,7},{4,20},{5,1},{6,22},{7,3},{8,24},{9,13},... | collective-permute-start | bytes 1769480 | tf_op jit(solution)/shard_map/ppermute | solution.py:69
  209.8 9.3 %collective-permute-start.52 = (bf16[32,1152]{1,0:T(8,128)(2,1)S(1)}, bf16[32,1152]{1,0:T(8,128)(2,1)S(1)}, u32[]{:S(2)}, u32[]{:S(2)}) collective-permute-start(bf16[32,1152]{1,0:T(8,128)(2,1)S(1)} %get-tuple-element.264), channel_id=1, source_target_pairs={{0,12},{1,49},{2,14},{3,51},{4,8},{5,53},{6,10},{7,55},{8,4},{9,57... | collective-permute-start | bytes 221192 | tf_op jit(solution)/shard_map/ppermute | solution.py:69
  211.2 7.9 %collective-permute-start.53 = (bf16[32,1152]{1,0:T(8,128)(2,1)S(1)}, bf16[32,1152]{1,0:T(8,128)(2,1)S(1)}, u32[]{:S(2)}, u32[]{:S(2)}) collective-permute-start(bf16[32,1152]{1,0:T(8,128)(2,1)S(1)} %get-tuple-element.266), channel_id=1, source_target_pairs={{0,4},{1,17},{2,6},{3,19},{4,0},{5,21},{6,2},{7,23},{8,12},{9,25},... | collective-permute-start | bytes 221192 | tf_op jit(solution)/shard_map/ppermute | solution.py:69
  219.3 16.3 %collective-permute-start.54 = (bf16[128,4608]{1,0:T(8,128)(2,1)S(1)}, bf16[128,4608]{1,0:T(8,128)(2,1)S(1)}, u32[]{:S(2)}, u32[]{:S(2)}) collective-permute-start(bf16[128,4608]{1,0:T(8,128)(2,1)S(1)} %get-tuple-element.268.a1), channel_id=1, source_target_pairs={{0,16},{1,5},{2,18},{3,7},{4,20},{5,1},{6,22},{7,3},{8,24},{9,13},... | collective-permute-start | bytes 3538952 | tf_op jit(solution)/shard_map/ppermute | solution.py:69
  220.0 17.4 %collective-permute-start.55 = (bf16[128,4608]{1,0:T(8,128)(2,1)S(1)}, bf16[128,4608]{1,0:T(8,128)(2,1)S(1)}, u32[]{:S(2)}, u32[]{:S(2)}) collective-permute-start(bf16[128,4608]{1,0:T(8,128)(2,1)S(1)} %get-tuple-element.269.a2), channel_id=1, source_target_pairs={{0,48},{1,13},{2,50},{3,15},{4,52},{5,9},{6,54},{7,11},{8,56},{9,5... | collective-permute-start | bytes 3538952 | tf_op jit(solution)/shard_map/ppermute | solution.py:69
  228.9 9.5 %collective-permute-start.57 = (bf16[16,896]{1,0:T(8,128)(2,1)S(1)}, bf16[16,896]{1,0:T(8,128)(2,1)S(1)}, u32[]{:S(2)}, u32[]{:S(2)}) collective-permute-start(bf16[16,896]{1,0:T(8,128)(2,1)S(1)} %get-tuple-element.275), channel_id=1, source_target_pairs={{0,1},{1,0},{2,3},{3,2},{4,5},{5,4},{6,7},{7,6},{8,9},{9,8},{10,11... | collective-permute-start | bytes 86024 | tf_op jit(solution)/shard_map/ppermute | solution.py:69
  229.0 9.4 %collective-permute-start.58 = (bf16[16,896]{1,0:T(8,128)(2,1)S(1)}, bf16[16,896]{1,0:T(8,128)(2,1)S(1)}, u32[]{:S(2)}, u32[]{:S(2)}) collective-permute-start(bf16[16,896]{1,0:T(8,128)(2,1)S(1)} %get-tuple-element.276), channel_id=1, source_target_pairs={{0,2},{1,3},{2,0},{3,1},{4,6},{5,7},{6,4},{7,5},{8,10},{9,11},{10,... | collective-permute-start | bytes 86024 | tf_op jit(solution)/shard_map/ppermute | solution.py:69
  229.9 8.5 %collective-permute-start.59 = (bf16[16,896]{1,0:T(8,128)(2,1)S(1)}, bf16[16,896]{1,0:T(8,128)(2,1)S(1)}, u32[]{:S(2)}, u32[]{:S(2)}) collective-permute-start(bf16[16,896]{1,0:T(8,128)(2,1)S(1)} %get-tuple-element.277), channel_id=1, source_target_pairs={{0,3},{1,2},{2,1},{3,0},{4,7},{5,6},{6,5},{7,4},{8,11},{9,10},{10,... | collective-permute-start | bytes 86024 | tf_op jit(solution)/shard_map/ppermute | solution.py:69
  244.6 7.8 %collective-permute-start.63 = (bf16[32,2176]{1,0:T(8,128)(2,1)S(1)}, bf16[32,2176]{1,0:T(8,128)(2,1)S(1)}, u32[]{:S(2)}, u32[]{:S(2)}) collective-permute-start(bf16[32,2176]{1,0:T(8,128)(2,1)S(1)} %get-tuple-element.282.a2), channel_id=1, source_target_pairs={{0,12},{1,49},{2,14},{3,51},{4,8},{5,53},{6,10},{7,55},{8,4},{9,57... | collective-permute-start | bytes 417800 | tf_op jit(solution)/shard_map/ppermute | solution.py:69
  252.5 8.2 %collective-permute-start.65 = (bf16[64,2176]{1,0:T(8,128)(2,1)S(1)}, bf16[64,2176]{1,0:T(8,128)(2,1)S(1)}, u32[]{:S(2)}, u32[]{:S(2)}) collective-permute-start(bf16[64,2176]{1,0:T(8,128)(2,1)S(1)} %get-tuple-element.284.a2), channel_id=1, source_target_pairs={{0,16},{1,5},{2,18},{3,7},{4,20},{5,1},{6,22},{7,3},{8,24},{9,13},... | collective-permute-start | bytes 835592 | tf_op jit(solution)/shard_map/ppermute | solution.py:69
  253.1 7.6 %collective-permute-start.64 = (bf16[64,2048]{1,0:T(8,128)(2,1)S(1)}, bf16[64,2048]{1,0:T(8,128)(2,1)S(1)}, u32[]{:S(2)}, u32[]{:S(2)}) collective-permute-start(bf16[64,2048]{1,0:T(8,128)(2,1)S(1)} %get-tuple-element.283.a1), channel_id=1, source_target_pairs={{0,48},{1,13},{2,50},{3,15},{4,52},{5,9},{6,54},{7,11},{8,56},{9,5... | collective-permute-start | bytes 786440 | tf_op jit(solution)/shard_map/ppermute | solution.py:69
  261.8 11.2 %collective-permute-start.67 = (bf16[128,2176]{1,0:T(8,128)(2,1)}, bf16[128,2176]{1,0:T(8,128)(2,1)}, u32[]{:S(2)}, u32[]{:S(2)}) collective-permute-start(bf16[128,2176]{1,0:T(8,128)(2,1)} %get-tuple-element.286.a2), channel_id=1, source_target_pairs={{0,48},{1,13},{2,50},{3,15},{4,52},{5,9},{6,54},{7,11},{8,56},{9,5... | collective-permute-start | bytes 1671176 | tf_op jit(solution)/shard_map/ppermute | solution.py:69
  263.5 9.5 %collective-permute-start.66 = (bf16[128,2048]{1,0:T(8,128)(2,1)}, bf16[128,2048]{1,0:T(8,128)(2,1)}, u32[]{:S(2)}, u32[]{:S(2)}) collective-permute-start(bf16[128,2048]{1,0:T(8,128)(2,1)} %get-tuple-element.285.a1), channel_id=1, source_target_pairs={{0,16},{1,5},{2,18},{3,7},{4,20},{5,1},{6,22},{7,3},{8,24},{9,13},... | collective-permute-start | bytes 1572872 | tf_op jit(solution)/shard_map/ppermute | solution.py:69
  263.5 14.8 %collective-permute-start.68 = (bf16[256,1024]{1,0:T(8,128)(2,1)}, bf16[256,1024]{1,0:T(8,128)(2,1)}, u32[]{:S(2)}, u32[]{:S(2)}) collective-permute-start(bf16[256,1024]{1,0:T(8,128)(2,1)} %get-tuple-element.289), channel_id=1, source_target_pairs={{0,2},{1,3},{2,0},{3,1},{4,6},{5,7},{6,4},{7,5},{8,10},{9,11},{10,... | collective-permute-start | bytes 1572872 | tf_op jit(solution)/shard_map/ppermute | solution.py:69
  (37 other events, 171.1 us)
